TPU v7x, 128 devices: a whole 4x4x4 slice. The times are simulated.
128 devices in a mesh: tok: 8 (over z, core), lat: 16 (over y, x).
Axes of the slice: x: 4, y: 4, z: 4, core: 2. Of those that a mesh axis runs over, the one named last changes fastest.
Arguments:
- activations: bfloat16 [2048, 2, 8192], P('lat', None, 'tok'), may hold values from -6 to 6
- enc_weight: bfloat16 [64, 2, 8192, 256], P('lat', None, 'tok'), may hold values from -0.046875 to 0.046875
- enc_bias: float32 [64, 256], P('lat'), may hold values from -3 to 3
- dec_weight: bfloat16 [64, 256, 2, 8192], P('lat', None, None, 'tok'), may hold values from -0.09375 to 0.09375
- dec_bias: float32 [2, 8192], P(None, 'tok'), may hold values from -3 to 3
- active: int32 [16, 16], replicated, may hold values from 0 to 63, all different within a row; in each aligned block of 16 rows (0 to 15, 16 to 31, ...) at most 8 rows name the same one
Outputs:
- grad_enc: bfloat16 [64, 2, 8192, 256], P('lat', None, 'tok')
- grad_enc_bias: float32 [64, 256], P('lat')
- grad_dec: bfloat16 [64, 256, 2, 8192], P('lat', None, None, 'tok')
- grad_dec_bias: float32 [2, 8192], P(None, 'tok')
Inputs may be any that keep to these rules, and one draw needn't show every extreme that they name: `active`: each row lists 16 different block ids; every block id appears in some row; no block id appears in more than 8 rows, and some block id appears in exactly 8 rows.
All inputs are finite; a program needn't handle non-finite values.
Results may differ from a plain program's by a relative error of at most 0.02.
Values may be sent and summed in bfloat16 or wider, within the bound.
A program may use at most 192 MiB of HBM per device.

v0:
```python
import math

import jax
import jax.numpy as jnp
from jax import lax
from jax.sharding import PartitionSpec as P

MOST = 8
TILE = 128


SPARSITY = 0.25
NORM_EPSILON = 1e-06


def slot_lists(active, first_block, block_count):
    tile_count = active.shape[0]
    block_ids = first_block + jnp.arange(block_count, dtype=jnp.int32)
    is_active = jnp.any(active[:, :, None] == block_ids[None, None, :], axis=1).astype(jnp.int32)
    rank_count = jnp.cumsum(is_active, axis=0)
    wanted = jnp.arange(MOST, dtype=jnp.int32) + 1
    picked = (is_active[:, :, None] == 1) & (rank_count[:, :, None] == wanted[None, None, :])
    tile_ids = jnp.arange(tile_count, dtype=jnp.int32)
    slot_tile = jnp.sum(jnp.where(picked, tile_ids[:, None, None], 0), axis=0)
    live_slot = jnp.any(picked, axis=0)
    return (slot_tile, live_slot)


def on_device(activations, enc_weight, enc_bias, dec_weight, dec_bias, active):
    slab_count = enc_weight.shape[0]
    tile_count = active.shape[0]
    tile_rows = activations.shape[0]
    models = activations.shape[1]
    feat_width = activations.shape[2]
    loss_scale = 1.0 / math.sqrt(MOST * TILE)
    first_block = lax.axis_index("lat") * slab_count
    slot_tile, live_slot = slot_lists(active, first_block, slab_count)
    live_mask = live_slot[:, :, None, None]
    gathered = lax.all_gather(activations, "lat", axis=0, tiled=True)
    tile_acts = gathered.reshape(tile_count, tile_rows, models, feat_width)
    chosen = tile_acts[slot_tile]
    pre_part = jnp.einsum(
        "smrad,sadj->smrj", chosen, enc_weight, preferred_element_type=jnp.float32
    )
    pre_act = lax.psum(pre_part, "tok") + enc_bias[:, None, None, :]
    features = jnp.where(live_mask, jnp.maximum(pre_act, 0.0), 0.0).astype(jnp.bfloat16)
    product = jnp.einsum(
        "smrj,sjad->smrad", features, dec_weight, preferred_element_type=jnp.float32
    )
    partial_value = (
        jnp.zeros((tile_count, tile_rows, models, feat_width), jnp.float32)
        .at[slot_tile]
        .add(product)
    )
    rounded = lax.optimization_barrier(partial_value.astype(jnp.bfloat16)).astype(jnp.float32)
    rounded = rounded.reshape(tile_count * tile_rows, models, feat_width)
    recon_mine = (
        lax.psum_scatter(
            rounded.astype(jnp.bfloat16), "lat", scatter_dimension=0, tiled=True
        ).astype(jnp.float32)
        + dec_bias[None, :, :]
    )
    error_mine = (recon_mine - activations.astype(jnp.float32)).astype(jnp.bfloat16)
    error_all = lax.all_gather(error_mine, "lat", axis=0, tiled=True)
    tile_err = error_all.reshape(tile_count, tile_rows, models, feat_width)
    err_chosen = tile_err[slot_tile]
    grad_part = jnp.einsum(
        "smrad,sjad->smrj", err_chosen, dec_weight, preferred_element_type=jnp.float32
    )
    dec_wide = dec_weight.astype(jnp.float32)
    squares = jnp.sum(jnp.square(dec_wide), axis=3)
    grad_sum, square_sum = (
        lax.psum(grad_part.astype(jnp.bfloat16), "tok").astype(jnp.float32),
        lax.psum(squares.astype(jnp.bfloat16), "tok").astype(jnp.float32),
    )
    dec_norms = jnp.sqrt(square_sum + NORM_EPSILON)
    feat_grad = loss_scale * (grad_sum + SPARSITY * jnp.sum(dec_norms, axis=2)[:, None, None, :])
    pre_grad = jnp.where(features > 0, feat_grad, 0.0).astype(jnp.bfloat16)
    grad_enc = jnp.einsum(
        "smrad,smrj->sadj", chosen, pre_grad, preferred_element_type=jnp.float32
    ).astype(jnp.bfloat16)
    grad_enc_bias = jnp.sum(pre_grad.astype(jnp.float32), axis=(1, 2))
    feat_total = jnp.sum(features.astype(jnp.float32), axis=(1, 2))
    recon_term = jnp.einsum(
        "smrj,smrad->sjad", features, err_chosen, preferred_element_type=jnp.float32
    )
    norm_term = SPARSITY * feat_total[:, :, None, None] * dec_wide / dec_norms[:, :, :, None]
    grad_dec = (loss_scale * (recon_term + norm_term)).astype(jnp.bfloat16)
    grad_dec_bias = loss_scale * jnp.sum(error_all.astype(jnp.float32), axis=0)
    return (grad_enc, grad_enc_bias, grad_dec, grad_dec_bias)


def solution(mesh):
    placed = (
        P("lat", None, "tok"),
        P("lat", None, "tok", None),
        P("lat", None),
        P("lat", None, None, "tok"),
        P(None, "tok"),
        P(),
    )
    return jax.shard_map(
        on_device,
        mesh=mesh,
        in_specs=placed,
        out_specs=(
            P("lat", None, "tok", None),
            P("lat", None),
            P("lat", None, None, "tok"),
            P(None, "tok"),
        ),
        check_vma=False,
    )
```

profile of v0, /device:TPU:1, one launch (start us, length us, event | category | flops | bytes accessed | tf_op | source)
XLA Modules:
  0.0 584.5 jit_solution(5982257089558291725)
XLA Ops:
  7.2 0.0 all-gather.3.cloned.1.call-start
  7.2 2.0 copy.46
  9.2 0.0 all-gather.3.cloned.1.call-update
  9.2 0.0 all-reduce.3.cloned.1.call-start
  9.3 0.9 compare_reduce_fusion
  10.2 0.1 copy.47
  10.3 0.1 copy.48
  10.4 0.2 select_reduce_fusion
  10.6 0.1 reshape.64
  10.7 73.9 %all-gather.3.cloned.1.call-done = bf16[2048,2,1024]{2,0,1:T(8,128)(2,1)} async-done(((bf16[128,2,1024]{2,0,1:T(8,128)(2,1)}), bf16[2048,2,1024]{2,0,1:T(8,128)(2,1)}) %all-gather.3.cloned.1.call-update) | async-done | bytes 8388624 | tf_op jit(solution)/shard_map/all_gather | solution.py:39
  84.6 8.2 %copy.49 = bf16[16,128,2,1024]{3,1,2,0:T(8,128)(2,1)} copy(bf16[16,128,2,1024]{3,1,0,2:T(8,128)(2,1)} %bitcast.69) | data formatting | bytes 16777216 | tf_op jit(solution)/shard_map/reshape | solution.py:40
  92.8 10.5 %gather_fusion = bf16[32,128,2,1024]{3,1,2,0:T(8,128)(2,1)} fusion(bf16[16,128,2,1024]{3,1,2,0:T(8,128)(2,1)} %copy.49, s32[1024]{0:T(1024)S(1)} %pad_clamp_fusion), kind=kCustom, calls=%fused_computation | custom fusion | bytes 33554560 | tf_op jit(solution)/shard_map/gather | solution.py:41
  103.3 13.5 %fusion.11 = f32[4,8,128,256]{3,2,1,0:T(8,128)} fusion(bf16[4,8,128,2,1024]{4,2,3,1,0:T(8,128)(2,1)} %bitcast.65, bf16[4,2,1024,256]{3,2,1,0:T(8,128)(2,1)} %param.7), kind=kOutput, calls=%fused_computation.23 | convolution fusion | flops 4294967296 | bytes 25165824 | tf_op jit(solution)/shard_map/smrad,sadj->smrj/dot_general | solution.py:42
  116.7 0.0 all-reduce.3.cloned.1.call-update
  116.8 0.2 reduce-scatter.2.cloned.1.call-start
  117.0 0.2 fusion.19
  117.2 70.5 %all-reduce.3.cloned.1.call-done = f32[4,8,128,256]{3,2,1,0:T(8,128)} async-done(((f32[4,8,128,256]{3,2,1,0:T(8,128)}), f32[4,8,128,256]{3,2,1,0:T(8,128)}) %all-reduce.3.cloned.1.call-update) | async-done | bytes 4194320 | tf_op jit(solution)/shard_map/psum | solution.py:45
  187.7 0.0 copy-done.4
  187.7 3.1 select_convert_fusion.1
  190.8 0.4 copy-done
  191.2 13.1 %fusion.9 = f32[4,8,128,2,1024]{4,2,3,1,0:T(8,128)} fusion(bf16[4,256,2,1024,1]{3,2,1,0,4:T(2,128)(2,1)S(1)} %bitcast.64, bf16[4,8,128,256]{3,2,1,0:T(8,128)(2,1)S(1)} %select_convert_fusion.1), kind=kOutput, calls=%fused_computation.21 | convolution fusion | flops 4294967296 | bytes 39845888 | tf_op jit(solution)/shard_map/smrj,sjad->smrad/dot_general | solution.py:47
  204.3 7.8 %broadcast_in_dim.28 = f32[16,128,2,1024]{3,1,2,0:T(8,128)} broadcast(f32[]{:T(128)} %constant.17.clone.1), dimensions={} | broadcast | bytes 16777220 | tf_op jit(solution)/shard_map/broadcast_in_dim | solution.py:51
  212.1 65.6 %scatter_fusion = f32[16,128,2,1024]{3,1,2,0:T(8,128)} fusion(f32[16,128,2,1024]{3,1,2,0:T(8,128)} %broadcast_in_dim.28, s32[32]{0:T(128)S(1)} %reshape.64, f32[32,128,2,1024]{3,1,2,0:T(8,128)} %bitcast.60), kind=kCustom, calls=%fused_computation.2 | custom fusion | flops 8388608 | bytes 100663424 | tf_op jit(solution)/shard_map/scatter-add | solution.py:53
  277.7 9.1 %convert_element_type.66 = bf16[16,128,2,1024]{3,1,2,0:T(8,128)(2,1)} convert(f32[16,128,2,1024]{3,1,2,0:T(8,128)} %scatter_fusion) | non-fusion elementwise | flops 4194304 | bytes 25165824 | tf_op jit(solution)/shard_map/convert_element_type | solution.py:55
  286.8 8.2 %copy.51 = bf16[16,128,2,1024]{3,1,0,2:T(8,128)(2,1)} copy(bf16[16,128,2,1024]{3,1,2,0:T(8,128)(2,1)} %convert_element_type.66) | data formatting | bytes 16777216 | tf_op jit(solution)/shard_map/optimization_barrier | solution.py:55
  295.0 0.0 reduce-scatter.2.cloned.1.call-update
  295.0 0.0 all-gather.5.cloned.1.call-start
  295.1 85.5 %reduce-scatter.2.cloned.1.call-done = bf16[128,2,1024]{2,0,1:T(8,128)(2,1)} async-done(((bf16[2048,2,1024]{2,0,1:T(8,128)(2,1)}), bf16[128,2,1024]{2,0,1:T(8,128)(2,1)}) %reduce-scatter.2.cloned.1.call-update) | async-done | bytes 524304 | tf_op jit(solution)/shard_map/reduce_scatter | solution.py:58
  380.6 0.0 copy-done.3
  380.6 0.0 copy-done.5
  380.6 2.1 subtract_convert_fusion
  382.6 0.0 all-gather.5.cloned.1.call-update
  382.6 0.0 all-reduce.5.cloned.1.call-start
  382.7 3.4 fusion
  386.1 14.3 %psum.23 = bf16[4,256,2]{1,2,0:T(2,128)(2,1)S(1)} all-reduce(bf16[4,256,2]{1,2,0:T(2,128)(2,1)S(1)} %fusion), channel_id=1, replica_groups=mesh['tok'=8,'lat'=16] {'tok'}, use_global_device_ids=true, to_apply=%region_9.10 | all-reduce | flops 2048 | bytes 8192 | tf_op jit(solution)/shard_map/psum | solution.py:74
  400.4 54.3 %all-gather.5.cloned.1.call-done = bf16[2048,2,1024]{2,0,1:T(8,128)(2,1)} async-done(((bf16[128,2,1024]{2,0,1:T(8,128)(2,1)}), bf16[2048,2,1024]{2,0,1:T(8,128)(2,1)}) %all-gather.5.cloned.1.call-update) | async-done | bytes 8388624 | tf_op jit(solution)/shard_map/all_gather | solution.py:64
  454.7 10.5 %gather_fusion.1 = bf16[32,128,2,1024]{3,1,2,0:T(8,128)(2,1)} fusion(bf16[16,128,2,1024]{3,1,0,2:T(8,128)(2,1)} %bitcast.61, s32[1024]{0:T(1024)S(1)} %pad_clamp_fusion), kind=kCustom, calls=%fused_computation.1 | custom fusion | bytes 33554560 | tf_op jit(solution)/shard_map/gather | solution.py:66
  465.2 12.8 %bitcast_convert_fusion.1 = bf16[4,8,128,256]{3,2,1,0:T(8,128)(2,1)} fusion(bf16[4,8,128,2,1024]{4,2,3,1,0:T(8,128)(2,1)} %bitcast.67, bf16[4,256,2,1024,1]{3,2,1,0,4:T(2,128)(2,1)} %bitcast.63), kind=kOutput, calls=%fused_computation.14 | convolution fusion | flops 4296015872 | bytes 23068672 | tf_op jit(solution)/shard_map/smrad,sjad->smrj/dot_general | solution.py:67
  478.0 0.0 all-reduce.5.cloned.1.call-update
  478.1 5.0 convert_reduce_fusion
  483.1 0.6 broadcast_multiply_fusion
  483.7 58.1 %all-reduce.5.cloned.1.call-done = bf16[4,8,128,256]{3,2,1,0:T(8,128)(2,1)} async-done(((bf16[4,8,128,256]{3,2,1,0:T(8,128)(2,1)}), bf16[4,8,128,256]{3,2,1,0:T(8,128)(2,1)}) %all-reduce.5.cloned.1.call-update) | async-done | bytes 2097168 | tf_op jit(solution)/shard_map/psum | solution.py:73
  541.8 5.1 convert_reduce_fusion.1
  546.9 0.0 copy-done.1
  546.9 10.7 %fusion.4 = bf16[4,256,2,1024]{3,1,2,0:T(8,128)(2,1)} fusion(f32[4,256,2]{1,2,0:T(2,128)S(1)} %get-tuple-element.26, f32[4,256]{1,0:T(4,128)S(1)} %broadcast_multiply_fusion.1, bf16[4,256,2,1024]{3,2,1,0:T(2,128)(2,1)S(1)} %copy-done.1, bf16[4,8,128,2,1024]{4,2,3,1,0:T(8,128)(2,1)} %bitcast.68, bf16[4,8,128,256]{3,2,1,0:T(8,128)(2,1)S(1)} %select_convert_fusion.1), kind=kOutput, calls=%fused_computation.11 | convolution fusion | flops 4307550208 | bytes 27275264 | tf_op jit(solution)/shard_map/smrj,smrad->sjad/dot_general | solution.py:84
  557.6 8.7 %copy.58 = bf16[4,256,2,1024]{3,2,1,0:T(2,128)(2,1)} copy(bf16[4,256,2,1024]{3,1,2,0:T(8,128)(2,1)} %fusion.4) | data formatting | bytes 8388608
  566.2 0.0 copy-done.2
  566.2 11.8 %bitcast_convert_fusion = bf16[4,2,1024,256]{3,2,1,0:T(8,128)(2,1)} fusion(bf16[4,8,128,2,1024]{4,2,3,1,0:T(8,128)(2,1)} %bitcast.66, bf16[4,8,128,256]{3,2,1,0:T(8,128)(2,1)S(1)} %copy-done.2, bf16[4,8,128,256]{3,2,1,0:T(8,128)(2,1)S(1)} %select_convert_fusion.1, f32[4,256]{1,0:T(4,128)S(1)} %broadcast_multiply_fusion.2), kind=kOutput, calls=%fused_computation.10 | convolution fusion | flops 4303355904 | bytes 25169920 | tf_op jit(solution)/shard_map/smrad,smrj->sadj/dot_general | solution.py:79
  (15 shorter events, 0.1 us)
Async XLA Ops:
  7.2 77.4 %all-gather.3.cloned.1.call-start = ((), (), s32[]{:S(2)}) async-start(), calls=%async_computation.1 | async-start | bytes 8912896 | tf_op jit(solution)/shard_map/all_gather | solution.py:39
  9.2 178.5 %all-reduce.3.cloned.1.call-start = ((), (), s32[]{:S(2)}) async-start(), calls=%async_computation.2 | async-start | bytes 8388608 | tf_op jit(solution)/shard_map/psum | solution.py:45
  116.7 71.0 %copy-start.4 = (f32[4,256]{1,0:T(4,128)S(1)}, f32[4,256]{1,0:T(4,128)}, u32[]{:S(2)}) copy-start(f32[4,256]{1,0:T(4,128)} %param.8) | copy-start | bytes 12292
  116.8 263.8 %reduce-scatter.2.cloned.1.call-start = ((), (), s32[]{:S(2)}) async-start(), calls=%async_computation.3 | async-start | bytes 8912896 | tf_op jit(solution)/shard_map/reduce_scatter | solution.py:58
  187.7 3.4 copy-start
  295.0 85.6 %copy-start.3 = (bf16[128,2,1024]{2,1,0:T(2,128)(2,1)S(1)}, bf16[128,2,1024]{2,1,0:T(2,128)(2,1)}, u32[]{:S(2)}) copy-start(bf16[128,2,1024]{2,1,0:T(2,128)(2,1)} %param.6) | copy-start | bytes 1572868
  295.0 85.6 %copy-start.5 = (f32[2,1024]{1,0:T(2,128)S(1)}, f32[2,1024]{1,0:T(2,128)}, u32[]{:S(2)}) copy-start(f32[2,1024]{1,0:T(2,128)} %param.10) | copy-start | bytes 24580
  295.0 159.6 %all-gather.5.cloned.1.call-start = ((), (), s32[]{:S(2)}) async-start(), calls=%async_computation.4 | async-start | bytes 8912896 | tf_op jit(solution)/shard_map/all_gather | solution.py:64
  382.6 159.2 %all-reduce.5.cloned.1.call-start = ((), (), s32[]{:S(2)}) async-start(), calls=%async_computation.5 | async-start | bytes 4194304 | tf_op jit(solution)/shard_map/psum | solution.py:73
  541.8 5.1 copy-start.1
  557.6 8.7 %copy-start.2 = (bf16[4,8,128,256]{3,2,1,0:T(8,128)(2,1)S(1)}, bf16[4,8,128,256]{3,2,1,0:T(8,128)(2,1)}, u32[]{:S(2)}) copy-start(bf16[4,8,128,256]{3,2,1,0:T(8,128)(2,1)} %all-reduce.5.cloned.1.call-done) | copy-start | bytes 6291460
Sparse Core Ops, SparseCore 0:
  10.7 73.8 all-gather.2
  116.9 70.7 all-reduce.2
  295.1 85.3 reduce-scatter.1
  383.1 71.4 all-gather.4
  478.1 63.6 all-reduce.4
where the time goes:
time: 586 us; the launch traced here: 585 us
  waiting for transfers between devices  342 us (58%)
  other arithmetic  95.3 us (16%)
  matrix products  61.8 us (11%)
  local copies, waits for them, and re-layouts  56.5 us (10%)
  blocking collectives  14.3 us (2%)
  between operations  13.8 us (2%)
    reduce_scatter x1, waiting for transfers between devices, on_device(): lax.psum_scatter(rounded.astype(jnp.bfloat16), 'lat', scatter_dimension=0...  85.5 us
    all_gather x1, waiting for transfers between devices, on_device(): gathered = lax.all_gather(activations, 'lat', axis=0, tiled=True)  73.9 us
    psum x1, waiting for transfers between devices, on_device(): pre_act = lax.psum(pre_part, 'tok') + enc_bias[:, None, None, :]  70.5 us
    scatter-add x1, other arithmetic, on_device(): partial_value = jnp.zeros((tile_count, tile_rows, models, feat_width), jn...  65.6 us
    psum x1, waiting for transfers between devices, on_device(): lax.psum(grad_part.astype(jnp.bfloat16), 'tok').astype(jnp.float32)  58.1 us
    all_gather x1, waiting for transfers between devices, on_device(): error_all = lax.all_gather(error_mine, 'lat', axis=0, tiled=True)  54.3 us
    psum x1, blocking collectives, on_device(): lax.psum(squares.astype(jnp.bfloat16), 'tok').astype(jnp.float32)  14.3 us
    dot_general x1, matrix products, on_device(): jnp.einsum('smrad,sadj->smrj', chosen, enc_weight, preferred_element_type...  13.5 us
  transfers between devices with their start and end apart: 5, of which 5 were waited for; matrix products, arithmetic and copies ran while one was open for 2% of the time, Pallas kernels for 0%

commit v1 on v0

v1 whole, which is shorter than its diff:
```python
import functools
import math

import jax
import jax.numpy as jnp
from jax import lax
from jax.experimental import pallas as pl
from jax.experimental.pallas import tpu as pltpu
from jax.sharding import PartitionSpec as P

MOST = 8
TILE = 128
SPARSITY = 0.25
NORM_EPSILON = 1e-06
DEAD = -1e30
MESH = pl.DeviceIdType.MESH
SIDE = 4
BIG = 56 * 1024 * 1024
DIRS = (1, -1)


def params(**kw):
    return pltpu.CompilerParams(vmem_limit_bytes=BIG, **kw)


def ring(i, step):
    return lax.rem(i + step + SIDE, SIDE)


def lat_peer(y, x):
    return {"lat": y * SIDE + x}


def plane():
    lat = lax.axis_index("lat")
    return lax.rem(lat, SIDE), lax.div(lat, SIDE)


def greet(peers):
    barrier = pltpu.get_barrier_semaphore()
    for peer in peers:
        pl.semaphore_signal(barrier, inc=1, device_id=peer, device_id_type=MESH)
    pl.semaphore_wait(barrier, len(peers))


def greet_plane():
    x, y = plane()
    greet(
        [lat_peer(y, ring(x, d)) for d in DIRS] + [lat_peer(ring(y, d), x) for d in DIRS]
    )


def remote(src, dst, send, recv, peer):
    return pltpu.make_async_remote_copy(
        src_ref=src, dst_ref=dst, send_sem=send, recv_sem=recv, device_id=peer, device_id_type=MESH
    )


def half_rows(d, rows):
    return pl.ds(0 if d == 1 else rows // 2, rows // 2)


class Plane:
    def __init__(self, h):
        x, y = plane()
        self.h = h
        self.p, self.q = (x, y) if h == 0 else (y, x)

    def tile(self, p, q):
        return q * SIDE + p if self.h == 0 else p * SIDE + q

    def near(self, dp, dq):
        p, q = ring(self.p, dp), ring(self.q, dq)
        return lat_peer(q, p) if self.h == 0 else lat_peer(p, q)


def gather_plane(own, out, send, recv):
    rows = out.shape[2]
    flows = [Plane(h) for h in (0, 1)]
    started = []

    def go(copy):
        copy.start()
        started.append(copy)

    def sems(h, phase, k, d):
        n = ((h * 2 + phase) * SIDE + k) * 2 + (0 if d == 1 else 1)
        return n

    def first_full(f, d):
        n = sems(f.h, 0, 0, d)
        return remote(
            own(f.h), out.at[f.tile(f.p, f.q), f.h], send.at[n], recv.at[n], f.near(d, 0)
        )

    def first_half(f, d):
        n = sems(f.h, 0, 1, d)
        at = out.at[f.tile(ring(f.p, -d), f.q), f.h, half_rows(d, rows)]
        return remote(at, at, send.at[n], recv.at[n], f.near(d, 0))

    def second_full(f, k, d):
        n = sems(f.h, 1, k, d)
        at = out.at[f.tile(ring(f.p, -k), f.q), f.h]
        return remote(own(f.h) if k == 0 else at, at, send.at[n], recv.at[n], f.near(0, d))

    def second_half(f, k, d):
        n = 32 + ((f.h * SIDE) + k) * 2 + (0 if d == 1 else 1)
        at = out.at[f.tile(ring(f.p, -k), ring(f.q, -d)), f.h, half_rows(d, rows)]
        return remote(at, at, send.at[n], recv.at[n], f.near(0, d))

    for f in flows:
        for d in DIRS:
            go(first_full(f, d))
    for f in flows:
        for d in DIRS:
            go(second_full(f, 0, d))
    for f in flows:
        for d, k in ((1, 1), (-1, 3)):
            first_full(f, d).wait_recv()
            go(first_half(f, d))
            for e in DIRS:
                go(second_full(f, k, e))
    for f in flows:
        for d in DIRS:
            second_full(f, 0, d).wait_recv()
            go(second_half(f, 0, d))
    for f in flows:
        for d in DIRS:
            first_half(f, d).wait_recv()
        for e in DIRS:
            go(second_full(f, 2, e))
    for k in (1, 3, 2):
        for f in flows:
            for d in DIRS:
                second_full(f, k, d).wait_recv()
                go(second_half(f, k, d))
    for k in range(SIDE):
        for f in flows:
            for d in DIRS:
                second_half(f, k, d).wait_recv()
    for copy in started:
        copy.wait_send()


def gather_kernel(x_ref, out_ref, local, send, recv):
    greet_plane()
    x, y = plane()
    keep = pltpu.make_async_copy(x_ref, out_ref.at[y * SIDE + x], local)
    keep.start()
    gather_plane(lambda h: x_ref.at[h], out_ref, send, recv)
    keep.wait()


def gather_acts(mine):
    any_space = pl.BlockSpec(memory_space=pl.ANY)
    return pl.pallas_call(
        gather_kernel,
        out_shape=jax.ShapeDtypeStruct((SIDE * SIDE,) + mine.shape, mine.dtype),
        in_specs=[any_space],
        out_specs=any_space,
        scratch_shapes=[
            pltpu.SemaphoreType.DMA,
            pltpu.SemaphoreType.DMA((48,)),
            pltpu.SemaphoreType.DMA((48,)),
        ],
        compiler_params=params(collective_id=0, has_side_effects=True),
        name="gather_acts",
    )(mine)


CHUNK = 32


def by_rows(rows, body):
    def step(i, carry):
        body(pl.multiple_of(i * CHUNK, CHUNK))
        return carry

    lax.fori_loop(0, rows // CHUNK, step, 0)


def f32(v):
    return v.astype(jnp.float32)


def recon_kernel(
    part, act, bias, out, r1, r2, s2, c, r4, r5, s5, err, local, send, recv, gsend, grecv
):
    greet_plane()
    rows = part.shape[2]
    half = rows // 2
    flows = [Plane(h) for h in (0, 1)]
    started = []

    def go(copy):
        copy.start()
        started.append(copy)

    def s(d):
        return 0 if d == 1 else 1

    def num(kind, h, j, d):
        return ((kind * 2 + h) * SIDE + j) * 2 + s(d)

    def far(f, j, d):
        n = num(0, f.h, j, d)
        t = f.tile(ring(f.p, 2), ring(f.q, j))
        return remote(
            part.at[t, f.h, half_rows(d, rows)], r1.at[f.h, j, s(d)], send.at[n], recv.at[n], f.near(d, 0)
        )

    def plain(f, j, d):
        n = num(1, f.h, j, d)
        t = f.tile(ring(f.p, d), ring(f.q, j))
        return remote(
            part.at[t, f.h, half_rows(-d, rows)],
            r2.at[f.h, j, s(d), half_rows(-d, rows)],
            send.at[n],
            recv.at[n],
            f.near(d, 0),
        )

    def summed(f, j, d):
        n = num(2, f.h, j, d)
        return remote(
            s2.at[f.h, j, s(d)],
            r2.at[f.h, j, s(d), half_rows(d, rows)],
            send.at[n],
            recv.at[n],
            f.near(d, 0),
        )

    def far2(f, d):
        n = num(3, f.h, 0, d)
        return remote(
            c.at[f.h, 2, half_rows(d, rows)], r4.at[f.h, s(d)], send.at[n], recv.at[n], f.near(0, d)
        )

    def plain2(f, d):
        n = num(3, f.h, 1, d)
        return remote(
            c.at[f.h, 1 if d == 1 else 3, half_rows(-d, rows)],
            r5.at[f.h, s(d), half_rows(-d, rows)],
            send.at[n],
            recv.at[n],
            f.near(0, d),
        )

    def summed2(f, d):
        n = num(3, f.h, 2, d)
        return remote(
            s5.at[f.h, s(d)], r5.at[f.h, s(d), half_rows(d, rows)], send.at[n], recv.at[n], f.near(0, d)
        )

    order = (2, 1, 3, 0)
    for j in order:
        for f in flows:
            for d in DIRS:
                go(far(f, j, d))
        for f in flows:
            for d in DIRS:
                go(plain(f, j, d))

    def add_far(f, j):
        for d in DIRS:
            far(f, j, d).wait_recv()
            t = f.tile(ring(f.p, d), ring(f.q, j))
            base = 0 if d == 1 else half

            def add(i, t=t, base=base, d=d):
                s2[f.h, j, s(d), pl.ds(i, CHUNK)] = (
                    f32(part[t, f.h, pl.ds(base + i, CHUNK)]) + f32(r1[f.h, j, s(d), pl.ds(i, CHUNK)])
                ).astype(jnp.bfloat16)

            by_rows(half, add)
            go(summed(f, j, d))

    def reduce(f, j):
        for d in DIRS:
            plain(f, j, d).wait_recv()
            summed(f, j, d).wait_recv()
        t = f.tile(f.p, ring(f.q, j))

        def add(i):
            at = pl.ds(i, CHUNK)
            c[f.h, j, at] = (
                f32(part[t, f.h, at]) + f32(r2[f.h, j, 0, at]) + f32(r2[f.h, j, 1, at])
            ).astype(jnp.bfloat16)

        by_rows(rows, add)

    for j in order:
        for f in flows:
            add_far(f, j)
    for f in flows:
        reduce(f, 2)
        for d in DIRS:
            go(far2(f, d))
    for f in flows:
        for d, j in ((1, 1), (-1, 3)):
            reduce(f, j)
            go(plain2(f, d))
    for f in flows:
        for d, j in ((1, 1), (-1, 3)):
            far2(f, d).wait_recv()
            base = 0 if d == 1 else half

            def add(i, j=j, base=base, d=d):
                s5[f.h, s(d), pl.ds(i, CHUNK)] = (
                    f32(c[f.h, j, pl.ds(base + i, CHUNK)]) + f32(r4[f.h, s(d), pl.ds(i, CHUNK)])
                ).astype(jnp.bfloat16)

            by_rows(half, add)
            go(summed2(f, d))
    for f in flows:
        reduce(f, 0)
    for f in flows:
        for d in DIRS:
            plain2(f, d).wait_recv()
            summed2(f, d).wait_recv()

        def add(i):
            at = pl.ds(i, CHUNK)
            recon = f32(c[f.h, 0, at]) + f32(r5[f.h, 0, at]) + f32(r5[f.h, 1, at]) + bias[f.h][None, :]
            err[f.h, at] = (recon - f32(act[f.h, at])).astype(jnp.bfloat16)

        by_rows(rows, add)
    for copy in started:
        copy.wait_send()
    x, y = plane()
    keep = pltpu.make_async_copy(err, out.at[y * SIDE + x], local)
    keep.start()
    gather_plane(lambda h: err.at[h], out, gsend, grecv)
    keep.wait()


def recon_error(part, act, bias):
    tiles, models, rows, width = part.shape
    half = rows // 2
    vmem = pl.BlockSpec(memory_space=pltpu.VMEM)
    b = jnp.bfloat16
    return pl.pallas_call(
        recon_kernel,
        out_shape=jax.ShapeDtypeStruct(part.shape, part.dtype),
        in_specs=[vmem] * 3,
        out_specs=pl.BlockSpec(memory_space=pl.ANY),
        scratch_shapes=[
            pltpu.VMEM((2, SIDE, 2, half, width), b),
            pltpu.VMEM((2, SIDE, 2, rows, width), b),
            pltpu.VMEM((2, SIDE, 2, half, width), b),
            pltpu.VMEM((2, SIDE, rows, width), b),
            pltpu.VMEM((2, 2, half, width), b),
            pltpu.VMEM((2, 2, rows, width), b),
            pltpu.VMEM((2, 2, half, width), b),
            pltpu.VMEM((2, rows, width), b),
            pltpu.SemaphoreType.DMA,
            pltpu.SemaphoreType.DMA((64,)),
            pltpu.SemaphoreType.DMA((64,)),
            pltpu.SemaphoreType.DMA((48,)),
            pltpu.SemaphoreType.DMA((48,)),
        ],
        compiler_params=params(collective_id=1, has_side_effects=True),
        name="recon_error",
    )(part, act, bias)


def tok_peer(z, core):
    return {"tok": z * 2 + core}


def tok_sum_kernel(epilogue, n_extra, part, *refs):
    extra, (out, r1, s1, r2, r3, s3, own, local, send, recv) = refs[:n_extra], refs[n_extra:]
    tok = lax.axis_index("tok")
    z, core = lax.div(tok, 2), lax.rem(tok, 2)
    other = tok_peer(z, 1 - core)
    greet([other] + [tok_peer(ring(z, d), core) for d in DIRS])
    group = part.shape[1] // 2
    half = group // 2
    mine, theirs = pl.ds(core * group, group), pl.ds((1 - core) * group, group)
    started = []

    def go(copy):
        copy.start()
        started.append(copy)

    def s(d):
        return 0 if d == 1 else 1

    def hs(d):
        return pl.ds(0 if d == 1 else half, half)

    def swap(j):
        at = ring(z, j)
        return remote(part.at[at, theirs], r1.at[j], send.at[j], recv.at[j], other)

    def far(d):
        n = 4 + s(d)
        return remote(s1.at[2, hs(d)], r2.at[s(d)], send.at[n], recv.at[n], tok_peer(ring(z, d), core))

    def plain(d):
        n = 6 + s(d)
        return remote(
            s1.at[1 if d == 1 else 3, hs(-d)],
            r3.at[s(d), hs(-d)],
            send.at[n],
            recv.at[n],
            tok_peer(ring(z, d), core),
        )

    def summed(d):
        n = 8 + s(d)
        return remote(
            s3.at[s(d)], r3.at[s(d), hs(d)], send.at[n], recv.at[n], tok_peer(ring(z, d), core)
        )

    def spread(d):
        n = 10 + s(d)
        return remote(own, out.at[z, mine], send.at[n], recv.at[n], tok_peer(ring(z, d), core))

    def forward(d):
        n = 12 + s(d)
        at = out.at[ring(z, -d), pl.ds(core * group + (0 if d == 1 else half), half)]
        return remote(at, at, send.at[n], recv.at[n], tok_peer(ring(z, d), core))

    def hand(j):
        n = 14 + j
        at = out.at[ring(z, j), mine]
        return remote(own if j == 0 else at, at, send.at[n], recv.at[n], other)

    order = (2, 1, 3, 0)
    for j in order:
        go(swap(j))

    def first(j):
        swap(j).wait_recv()
        at = ring(z, j)

        def add(i, carry):
            s1[j, i] = (f32(part[at, core * group + i]) + f32(r1[j, i])).astype(s1.dtype)
            return carry

        lax.fori_loop(0, group, add, 0)

    first(2)
    for d in DIRS:
        go(far(d))
    for d in DIRS:
        first(1 if d == 1 else 3)
        go(plain(d))
    first(0)
    for d in DIRS:
        far(d).wait_recv()
        j, base = (1, 0) if d == 1 else (3, half)

        def add(i, carry, j=j, base=base, d=d):
            s3[s(d), i] = (f32(s1[j, base + i]) + f32(r2[s(d), i])).astype(s3.dtype)
            return carry

        lax.fori_loop(0, half, add, 0)
        go(summed(d))
    for d in DIRS:
        plain(d).wait_recv()
        summed(d).wait_recv()

    def last(i, carry):
        total = f32(s1[0, i]) + f32(r3[0, i]) + f32(r3[1, i])
        own[i] = epilogue(total, z, core * group + i, *extra).astype(own.dtype)
        return carry

    lax.fori_loop(0, group, last, 0)
    keep = pltpu.make_async_copy(own, out.at[z, mine], local)
    keep.start()
    for d in DIRS:
        go(spread(d))
    go(hand(0))
    for d in DIRS:
        spread(d).wait_recv()
        go(forward(d))
        go(hand(3 if d == 1 else 1))
    for d in DIRS:
        forward(d).wait_recv()
    go(hand(2))
    for j in range(SIDE):
        hand(j).wait_recv()
    for copy in started:
        copy.wait_send()
    keep.wait()


def tok_sum(name, collective_id, epilogue, part, *extra):
    slabs, slots, rows, width = part.shape
    group = slots // 2
    vmem = pl.BlockSpec(memory_space=pltpu.VMEM)
    t, b = part.dtype, jnp.bfloat16
    return pl.pallas_call(
        functools.partial(tok_sum_kernel, epilogue, len(extra)),
        out_shape=jax.ShapeDtypeStruct(part.shape, b),
        in_specs=[vmem] * (1 + len(extra)),
        out_specs=pl.BlockSpec(memory_space=pl.ANY),
        scratch_shapes=[
            pltpu.VMEM((SIDE, group, rows, width), t),
            pltpu.VMEM((SIDE, group, rows, width), t),
            pltpu.VMEM((2, group // 2, rows, width), t),
            pltpu.VMEM((2, group, rows, width), t),
            pltpu.VMEM((2, group // 2, rows, width), t),
            pltpu.VMEM((group, rows, width), b),
            pltpu.SemaphoreType.DMA,
            pltpu.SemaphoreType.DMA((18,)),
            pltpu.SemaphoreType.DMA((18,)),
        ],
        compiler_params=params(collective_id=collective_id, has_side_effects=True),
        name=name,
    )(part, *extra)


def encode_kernel(tile_of, live, acts, enc, out):
    slab = pl.program_id(0)
    for r in range(0, MOST, 2):
        at = slab * MOST + r

        @pl.when(live[at] == 1)
        def _():
            total = None
            for m in range(acts.shape[1]):
                x = jnp.concatenate([acts[tile_of[at], m], acts[tile_of[at + 1], m]], axis=0)
                term = jnp.dot(x, enc[0, m], preferred_element_type=jnp.float32)
                total = term if total is None else total + term
            out[0, r] = total[:TILE]
            out[0, r + 1] = jnp.where(live[at + 1] == 1, total[TILE:], DEAD)

        @pl.when(live[at] == 0)
        def _():
            out[0, r] = jnp.full(out.shape[2:], DEAD, out.dtype)
            out[0, r + 1] = jnp.full(out.shape[2:], DEAD, out.dtype)


def whole(shape):
    return pl.BlockSpec(shape, lambda *_: (0,) * len(shape))


def slabwise(shape):
    return pl.BlockSpec((1,) + shape[1:], lambda s, *_: (s,) + (0,) * (len(shape) - 1))


def slab_call(kernel, name, lists, ins, outs, scratch=()):
    return pl.pallas_call(
        kernel,
        out_shape=[jax.ShapeDtypeStruct(s, t) for s, t in outs],
        grid_spec=pltpu.PrefetchScalarGridSpec(
            num_scalar_prefetch=len(lists),
            grid=(SIDE,),
            in_specs=[spec(a.shape) for a, spec in ins],
            out_specs=[slabwise(s) for s, _ in outs],
            scratch_shapes=list(scratch),
        ),
        compiler_params=params(),
        name=name,
    )(*lists, *[a for a, _ in ins])


def decode_kernel(rank, feat, dec, out, acc):
    tile = pl.program_id(0)
    acc[...] = jnp.zeros_like(acc)
    for s in range(dec.shape[0]):
        r = rank[tile * dec.shape[0] + s]

        @pl.when(r >= 0)
        def _():
            f = feat[s, r]
            for m in range(dec.shape[1]):
                acc[m] += jnp.dot(f, dec[s, m], preferred_element_type=jnp.float32)

    out[0] = acc[...].astype(out.dtype)


def decode(rank, feat, dec):
    tiles = SIDE * SIDE
    models, width = dec.shape[1], dec.shape[3]
    shape = (tiles, models, TILE, width)
    return pl.pallas_call(
        decode_kernel,
        out_shape=jax.ShapeDtypeStruct(shape, jnp.bfloat16),
        grid_spec=pltpu.PrefetchScalarGridSpec(
            num_scalar_prefetch=1,
            grid=(tiles,),
            in_specs=[whole(feat.shape), whole(dec.shape)],
            out_specs=slabwise(shape),
            scratch_shapes=[pltpu.VMEM(shape[1:], jnp.float32)],
        ),
        compiler_params=params(),
        name="decode",
    )(rank, feat, dec)


NT = (((1,), (1,)), ((), ()))
TN = (((0,), (0,)), ((), ()))


def dec_grad_kernel(scale, tile_of, live, err, dec, feat, inv_norm, part, grad_dec, acc, tot):
    slab = pl.program_id(0)
    acc[...] = jnp.zeros_like(acc)
    tot[...] = jnp.zeros_like(tot)
    for r in range(0, MOST, 2):
        at = slab * MOST + r

        @pl.when(live[at] == 1)
        def _():
            f = jnp.concatenate([feat[0, r], feat[0, r + 1]], axis=0)
            total = None
            for m in range(err.shape[1]):
                e = jnp.concatenate([err[tile_of[at], m], err[tile_of[at + 1], m]], axis=0)
                term = lax.dot_general(e, dec[0, m], NT, preferred_element_type=jnp.float32)
                total = term if total is None else total + term
                acc[m] += lax.dot_general(f, e, TN, preferred_element_type=jnp.float32)
            part[0, r] = total[:TILE].astype(part.dtype)
            part[0, r + 1] = total[TILE:].astype(part.dtype)
            ones = jnp.ones((2 * TILE, 128), jnp.bfloat16)
            tot[...] += lax.dot_general(f, ones, TN, preferred_element_type=jnp.float32)

        @pl.when(live[at] == 0)
        def _():
            part[0, r] = jnp.zeros(part.shape[2:], part.dtype)
            part[0, r + 1] = jnp.zeros(part.shape[2:], part.dtype)

    for m in range(err.shape[1]):
        col = SPARSITY * tot[:, :1] * inv_norm[0, m]
        grad_dec[0, m] = (scale * (acc[m] + col * f32(dec[0, m]))).astype(grad_dec.dtype)


def enc_grad_kernel(tile_of, live, acts, pre_grad, grad_enc, grad_bias, acc):
    slab = pl.program_id(0)
    acc[...] = jnp.zeros_like(acc)
    grad_bias[...] = jnp.sum(f32(pre_grad[0]), axis=(0, 1))[None, None, :]
    for r in range(0, MOST, 2):
        at = slab * MOST + r

        @pl.when(live[at] == 1)
        def _():
            g = jnp.concatenate([pre_grad[0, r], pre_grad[0, r + 1]], axis=0)
            for m in range(acts.shape[1]):
                x = jnp.concatenate([acts[tile_of[at], m], acts[tile_of[at + 1], m]], axis=0)
                acc[m] += lax.dot_general(x, g, TN, preferred_element_type=jnp.float32)

    grad_enc[0] = acc[...].astype(grad_enc.dtype)


def slot_lists(active, first_block, block_count):
    tile_count = active.shape[0]
    block_ids = first_block + jnp.arange(block_count, dtype=jnp.int32)
    is_active = jnp.any(active[:, :, None] == block_ids[None, None, :], axis=1).astype(jnp.int32)
    upto = (jnp.arange(tile_count)[:, None] >= jnp.arange(tile_count)[None, :]).astype(jnp.int32)
    rank_count = jnp.sum(upto[:, :, None] * is_active[None, :, :], axis=1)
    wanted = jnp.arange(MOST, dtype=jnp.int32) + 1
    picked = (is_active[:, :, None] == 1) & (rank_count[:, :, None] == wanted[None, None, :])
    tile_ids = jnp.arange(tile_count, dtype=jnp.int32)
    slot_tile = jnp.sum(jnp.where(picked, tile_ids[:, None, None], 0), axis=0)
    live_slot = jnp.any(picked, axis=0).astype(jnp.int32)
    rank = jnp.where(is_active == 1, rank_count - 1, -1)
    return slot_tile.reshape(-1), live_slot.reshape(-1), rank.reshape(-1)


def feature_of(total, z, slot, bias):
    return jnp.maximum(total + bias[z], 0.0)


def pre_grad_of(scale, total, z, slot, feat, norm):
    grad = scale * (total + SPARSITY * norm[z])
    return jnp.where(f32(feat[z, slot]) > 0.0, grad, 0.0)


def on_device(activations, enc_weight, enc_bias, dec_weight, dec_bias, active):
    slabs = enc_weight.shape[0]
    scale = 1.0 / math.sqrt(MOST * TILE)
    width = activations.shape[2]
    block = enc_weight.shape[3]
    slot_tile, live, rank = slot_lists(active, lax.axis_index("lat") * slabs, slabs)
    mine = activations.transpose(1, 0, 2)
    dec = dec_weight.transpose(0, 2, 1, 3)
    squares = lax.psum(jnp.sum(jnp.square(dec.astype(jnp.float32)), axis=3), "tok")
    norms = jnp.sqrt(squares + NORM_EPSILON)
    acts = gather_acts(mine)
    pre_shape = (slabs, MOST, TILE, block)
    (pre,) = slab_call(
        encode_kernel,
        "encode",
        (slot_tile, live),
        [(acts, whole), (enc_weight, slabwise)],
        [(pre_shape, jnp.float32)],
    )
    feat = tok_sum("features", 2, feature_of, pre, enc_bias.reshape(slabs, 1, block))
    part = decode(rank, feat, dec)
    err = recon_error(part, mine, dec_bias)
    grad_part, grad_dec = slab_call(
        functools.partial(dec_grad_kernel, scale),
        "dec_grad",
        (slot_tile, live),
        [(err, whole), (dec, slabwise), (feat, slabwise), ((1.0 / norms)[..., None], slabwise)],
        [(pre_shape, jnp.bfloat16), (dec.shape, jnp.bfloat16)],
        [pltpu.VMEM(dec.shape[1:], jnp.float32), pltpu.VMEM((block, 128), jnp.float32)],
    )
    pre_grad = tok_sum(
        "pre_grad",
        3,
        functools.partial(pre_grad_of, scale),
        grad_part,
        feat,
        jnp.sum(norms, axis=1).reshape(slabs, 1, block),
    )
    grad_enc, grad_enc_bias = slab_call(
        enc_grad_kernel,
        "enc_grad",
        (slot_tile, live),
        [(acts, whole), (pre_grad, slabwise)],
        [(enc_weight.shape, jnp.bfloat16), ((slabs, 1, block), jnp.float32)],
        [pltpu.VMEM(enc_weight.shape[1:], jnp.float32)],
    )
    grad_dec_bias = scale * jnp.sum(err.astype(jnp.float32), axis=(0, 2))
    return (
        grad_enc,
        grad_enc_bias.reshape(slabs, block),
        grad_dec.transpose(0, 2, 1, 3),
        grad_dec_bias,
    )


def solution(mesh):
    placed = (
        P("lat", None, "tok"),
        P("lat", None, "tok", None),
        P("lat", None),
        P("lat", None, None, "tok"),
        P(None, "tok"),
        P(),
    )
    return jax.shard_map(
        on_device,
        mesh=mesh,
        in_specs=placed,
        out_specs=(
            P("lat", None, "tok", None),
            P("lat", None),
            P("lat", None, None, "tok"),
            P(None, "tok"),
        ),
        check_vma=False,
    )
```

time: 586 us -> 315 us (0.54)
  waiting for transfers between devices: 342 us -> 0 us
  Pallas kernels: 0 us -> 271 us
  other arithmetic: 95.3 us -> 8.31 us
  matrix products: 61.8 us -> 0 us
  local copies, waits for them, and re-layouts: 56.5 us -> 19.6 us
  between operations: 13.8 us -> 0.75 us
    pallas_call x0 -> x8, Pallas kernels: none -> 271 us  [the longest x1 94.5 us: recon_error(): pl.pallas_call(recon_kernel, out_shape=jax.ShapeDtypeStruct(part.shape, p...]
    psum x2 -> x0, waiting for transfers between devices: 129 us -> none  [the longest x1 70.5 us: on_device(): pre_act = lax.psum(pre_part, 'tok') + enc_bias[:, None, None, :]]
    all_gather x2 -> x0, waiting for transfers between devices: 128 us -> none  [the longest x1 73.9 us: on_device(): gathered = lax.all_gather(activations, 'lat', axis=0, tiled=True)]
    reduce_scatter x1 -> x0, waiting for transfers between devices: 85.5 us -> none  [on_device(): lax.psum_scatter(rounded.astype(jnp.bfloat16), 'lat', scatter_dimension=0...]
    scatter-add x1 -> x0, other arithmetic: 65.6 us -> none  [on_device(): partial_value = jnp.zeros((tile_count, tile_rows, models, feat_width), jn...]
    dot_general x5 -> x0, matrix products: 61.8 us -> none  [the longest x1 13.5 us: on_device(): jnp.einsum('smrad,sadj->smrj', chosen, enc_weight, preferred_element_type...]
    gather x2 -> x0, local copies, waits for them, and re-layouts: 21 us -> none  [the longest x1 10.5 us: on_device(): err_chosen = tile_err[slot_tile]]
    convert_element_type x3 -> x2, other arithmetic: 14.2 us -> 0.01 us  [the longest x1 0.01 us: slot_lists(): live_slot = jnp.any(picked, axis=0).astype(jnp.int32)]
  transfers between devices with their start and end apart: 5 -> 0, of which waited for: 5 -> 0; matrix products, arithmetic and copies ran while one was open for 2% -> 0% of each run, Pallas kernels for 0% -> 0%
where the time goes in v1:
time: 315 us; the launch traced here: 313 us
  Pallas kernels  271 us (86%)
  local copies, waits for them, and re-layouts  19.6 us (6%)
  blocking collectives  14.1 us (4%)
  other arithmetic  8.31 us (3%)
    pallas_call x1, Pallas kernels, recon_error(): pl.pallas_call(recon_kernel, out_shape=jax.ShapeDtypeStruct(part.shape, p...  94.5 us
    pallas_call x2, Pallas kernels, tok_sum(): pl.pallas_call(functools.partial(tok_sum_kernel, epilogue, len(extra)), o...  72.9 us
    pallas_call x1, Pallas kernels, gather_acts(): pl.pallas_call(gather_kernel, out_shape=jax.ShapeDtypeStruct((SIDE * SIDE...  49.5 us
    pallas_call x3, Pallas kernels, slab_call(): pl.pallas_call(kernel, out_shape=[jax.ShapeDtypeStruct(s, t) for s, t in...  39.3 us
    unnamed x10, local copies, waits for them, and re-layouts  15.1 us
    pallas_call x1, Pallas kernels, decode(): pl.pallas_call(decode_kernel, out_shape=jax.ShapeDtypeStruct(shape, jnp.b...  14.3 us
    psum x1, blocking collectives, on_device(): lax.psum(jnp.sum(jnp.square(dec.astype(jnp.float32)), axis=3), 'tok')  14.1 us

profile of v1, /device:TPU:1, one launch (start us, length us, event | category | flops | bytes accessed | tf_op | source)
XLA Modules:
  0.0 313.4 jit_solution(10082930091243982571)
XLA Ops:
  0.6 0.9 compare_reduce_fusion
  1.6 0.1 multiply_reduce_fusion.1
  1.7 0.2 fusion
  2.0 0.7 reshape.69.live
  2.6 0.2 select_reduce_fusion
  2.8 0.6 reshape.65.tile_of
  3.4 2.0 copy.29
  5.4 49.5 %gather_acts.1.acts = bf16[16,2,128,1024]{3,2,1,0:T(8,128)(2,1)} custom-call(bf16[2,128,1024]{2,1,0:T(8,128)(2,1)} %bitcast.16), custom_call_target="tpu_custom_call" | custom-call | tf_op jit(solution)/shard_map/gather_acts/pallas_call | solution.py:156
  54.9 0.0 copy-start.2
  54.9 10.9 %encode.1.part = f32[4,8,128,256]{3,2,1,0:T(8,128)} custom-call(s32[32]{0:T(128)} %reshape.65.tile_of, s32[32]{0:T(128)} %reshape.69.live, bf16[16,2,128,1024]{3,2,1,0:T(8,128)(2,1)} %gather_acts.1.acts, bf16[4,2,1024,256]{3,2,1,0:T(8,128)(2,1)} %enc.1), custom_call_target="tpu_custom_call" | custom-call | tf_op jit(solution)/shard_map/encode/pallas_call | solution.py:546
  65.8 0.0 copy-done.2
  65.8 0.6 reshape.66.refs_0_
  66.4 41.4 %features.1.feat.refs_0_ = bf16[4,8,128,256]{3,2,1,0:T(8,128)(2,1)} custom-call(f32[4,8,128,256]{3,2,1,0:T(8,128)} %encode.1.part, f32[4,1,256]{2,1,0:T(1,128)} %reshape.66.refs_0_), custom_call_target="tpu_custom_call" | custom-call | tf_op jit(solution)/shard_map/features/pallas_call | solution.py:495
  107.8 0.1 copy.18
  107.8 0.6 select_n.14.rank
  108.4 5.5 %copy.28 = bf16[4,256,2,1024]{3,1,2,0:T(8,128)(2,1)} copy(bf16[4,256,2,1024]{3,2,1,0:T(2,128)(2,1)} %param.9) | data formatting | bytes 8388608 | tf_op args[3]
  114.0 14.3 %decode.1.part = bf16[16,2,128,1024]{3,2,1,0:T(8,128)(2,1)} custom-call(s32[64]{0:T(128)} %select_n.14.rank, bf16[4,8,128,256]{3,2,1,0:T(8,128)(2,1)} %features.1.feat.refs_0_, bf16[4,2,256,1024]{3,2,1,0:T(8,128)(2,1)} %bitcast.14), custom_call_target="tpu_custom_call" | custom-call | tf_op jit(solution)/shard_map/decode/pallas_call | solution.py:580
  128.3 0.0 copy-start
  128.3 94.5 %recon_error.1.err = bf16[16,2,128,1024]{3,2,1,0:T(8,128)(2,1)} custom-call(bf16[16,2,128,1024]{3,2,1,0:T(8,128)(2,1)} %decode.1.part, bf16[2,128,1024]{2,1,0:T(8,128)(2,1)} %bitcast.17, f32[2,1024]{1,0:T(2,128)} %bias.1), custom_call_target="tpu_custom_call" | custom-call | tf_op jit(solution)/shard_map/recon_error/pallas_call | solution.py:342
  222.8 0.0 copy-done
  222.8 1.2 multiply_reduce_fusion
  224.0 14.1 %psum.7 = f32[4,2,256]{2,1,0:T(2,128)S(1)} all-reduce(f32[4,2,256]{2,1,0:T(2,128)S(1)} %multiply_reduce_fusion), channel_id=1, replica_groups=mesh['tok'=8,'lat'=16] {'tok'}, use_global_device_ids=true, to_apply=%region_5.6 | all-reduce | flops 2048 | bytes 16384 | tf_op jit(solution)/shard_map/psum | solution.py:679
  238.2 1.4 copy.20.inv_norm
  239.5 15.9 %dec_grad.1 = (bf16[4,8,128,256]{3,2,1,0:T(8,128)(2,1)}, bf16[4,2,256,1024]{3,2,1,0:T(8,128)(2,1)}) custom-call(s32[32]{0:T(128)} %reshape.65.tile_of, s32[32]{0:T(128)} %reshape.69.live, bf16[16,2,128,1024]{3,2,1,0:T(8,128)(2,1)} %recon_error.1.err, bf16[4,2,256,1024]{3,2,1,0:T(8,128)(2,1)} %bitcast.15, bf16[4,8,128,256]{3,2,1,0:T(8,128)(2,1)} %features.1.feat.refs_0_, ...), custom_call_target="tpu_custom_call" | custom-call | tf_op jit(solution)/shard_map/dec_grad/pallas_call | solution.py:546
  255.4 0.6 reshape.67.refs_1_
  256.0 31.6 %pre_grad.1 = bf16[4,8,128,256]{3,2,1,0:T(8,128)(2,1)} custom-call(bf16[4,8,128,256]{3,2,1,0:T(8,128)(2,1)} %get-tuple-element.8.part, bf16[4,8,128,256]{3,2,1,0:T(8,128)(2,1)} %features.1.feat.refs_0_, f32[4,1,256]{2,1,0:T(1,128)} %reshape.67.refs_1_), custom_call_target="tpu_custom_call" | custom-call | tf_op jit(solution)/shard_map/pre_grad/pallas_call | solution.py:495
  287.6 0.0 copy-start.1
  287.6 12.6 %enc_grad.1 = (bf16[4,2,1024,256]{3,2,1,0:T(8,128)(2,1)}, f32[4,1,256]{2,1,0:T(1,128)}) custom-call(s32[32]{0:T(128)} %reshape.65.tile_of, s32[32]{0:T(128)} %reshape.69.live, bf16[16,2,128,1024]{3,2,1,0:T(8,128)(2,1)} %gather_acts.1.acts, bf16[4,8,128,256]{3,2,1,0:T(8,128)(2,1)} %pre_grad.1), custom_call_target="tpu_custom_call" | custom-call | tf_op jit(solution)/shard_map/enc_grad/pallas_call | solution.py:546
  300.2 1.3 copy.30
  301.5 0.0 copy-done.1
  301.5 6.3 %copy.21 = bf16[4,256,2,1024]{3,2,1,0:T(2,128)(2,1)} copy(bf16[4,256,2,1024]{3,1,2,0:T(8,128)(2,1)S(1)} %bitcast.18) | data formatting | bytes 8388608
  307.8 5.0 %convert_reduce_fusion = f32[2,1024]{1,0:T(2,128)S(1)} fusion(bf16[16,2,128,1024]{3,2,1,0:T(8,128)(2,1)} %recon_error.1.err), kind=kLoop, calls=%fused_computation | loop fusion | flops 8386560 | bytes 8396800 | tf_op jit(solution)/shard_map/reduce_sum | solution.py:717
  312.8 0.6 broadcast_multiply_fusion
  (7 shorter events, 0.1 us)
Async XLA Ops:
  54.9 10.9 %copy-start.2 = (f32[4,256]{1,0:T(4,128)S(1)}, f32[4,256]{1,0:T(4,128)}, u32[]{:S(2)}) copy-start(f32[4,256]{1,0:T(4,128)} %param.8) | copy-start | bytes 12292
  128.3 94.5 %copy-start = (bf16[4,256,2,1024]{3,2,1,0:T(2,128)(2,1)S(1)}, bf16[4,256,2,1024]{3,2,1,0:T(2,128)(2,1)}, u32[]{:S(2)}) copy-start(bf16[4,256,2,1024]{3,2,1,0:T(2,128)(2,1)} %param.9) | copy-start | bytes 12582916
  287.6 13.9 %copy-start.1 = (bf16[4,2,256,1024]{3,2,1,0:T(8,128)(2,1)S(1)}, bf16[4,2,256,1024]{3,2,1,0:T(8,128)(2,1)}, u32[]{:S(2)}) copy-start(bf16[4,2,256,1024]{3,2,1,0:T(8,128)(2,1)} %get-tuple-element.11) | copy-start | bytes 12582916

commit v2 on v0

v2 whole, which is shorter than its diff:
```python
import functools
import math

import jax
import jax.numpy as jnp
from jax import lax
from jax.experimental import pallas as pl
from jax.experimental.pallas import tpu as pltpu
from jax.sharding import PartitionSpec as P

MOST = 8
TILE = 128
SPARSITY = 0.25
NORM_EPSILON = 1e-06
MESH = pl.DeviceIdType.MESH
SIDE = 4
UNIT = TILE // 2
HALF = UNIT // 2
CHUNK = 32
DIRS = (1, -1)
ORDER = (0, 1, 3, 2)
BF16, F32 = jnp.bfloat16, jnp.float32
NT = (((1,), (1,)), ((), ()))
TN = (((0,), (0,)), ((), ()))


def ring(i, step):
    return lax.rem(i + step + SIDE, SIDE)


def lat_peer(y, x):
    return {"lat": y * SIDE + x}


def tok_peer(z, core):
    return {"tok": z * 2 + core}


def plane():
    lat = lax.axis_index("lat")
    return lax.rem(lat, SIDE), lax.div(lat, SIDE)


def column():
    tok = lax.axis_index("tok")
    return lax.div(tok, 2), lax.rem(tok, 2)


def greet():
    x, y = plane()
    z, core = column()
    peers = [lat_peer(y, ring(x, d)) for d in DIRS] + [lat_peer(ring(y, d), x) for d in DIRS]
    peers += [tok_peer(ring(z, d), core) for d in DIRS] + [tok_peer(z, 1 - core)]
    barrier = pltpu.get_barrier_semaphore()
    for peer in peers:
        pl.semaphore_signal(barrier, inc=1, device_id=peer, device_id_type=MESH)
    pl.semaphore_wait(barrier, len(peers))


def s(d):
    return 0 if d == 1 else 1


def rows_of(d):
    return pl.ds(0 if d == 1 else HALF, HALF)


def f32(v):
    return v.astype(F32)


class Wires:
    def __init__(self, send, recv):
        self.send, self.recv = send, recv
        self.numbers, self.started = {}, []

    def copy(self, key, src, dst, peer):
        n = self.numbers.setdefault(key, len(self.numbers))
        return pltpu.make_async_remote_copy(
            src_ref=src,
            dst_ref=dst,
            send_sem=self.send.at[n],
            recv_sem=self.recv.at[n],
            device_id=peer,
            device_id_type=MESH,
        )

    def go(self, copy):
        copy.start()
        self.started.append(copy)

    def drain(self):
        for copy in self.started:
            copy.wait_send()


class Flow:
    def __init__(self, h):
        x, y = plane()
        self.h = h
        self.p, self.q = (x, y) if h == 0 else (y, x)

    def near(self, dp, dq):
        p, q = ring(self.p, dp), ring(self.q, dq)
        return lat_peer(q, p) if self.h == 0 else lat_peer(p, q)

    def unit(self, dq):
        return self.h * SIDE + ring(self.q, dq)


FLOWS = (0, 1)


def sweep(wires, tag, own, held, arrived, flow):
    flows = [Flow(h) for h in FLOWS]

    def p1(f, d):
        dst = held.at[1 if d == 1 else 3, f.unit(0)]
        return wires.copy((tag, 0, f.h, d), own(f.h), dst, f.near(d, 0))

    def p1half(f, d):
        src = held.at[1 if d == 1 else 3, f.unit(0), rows_of(d)]
        return wires.copy((tag, 1, f.h, d), src, held.at[2, f.unit(0), rows_of(d)], f.near(d, 0))

    def p2(f, k, d):
        at = held.at[k, f.unit(0)]
        return wires.copy((tag, 2, f.h, k, d), own(f.h) if k == 0 else at, at, f.near(0, d))

    def p2half(f, k, d):
        at = held.at[k, f.unit(-d), rows_of(d)]
        return wires.copy((tag, 3, f.h, k, d), at, at, f.near(0, d))

    def each(make, *k):
        for f in flows:
            for d in DIRS:
                wires.go(make(f, *k, d))

    def relay(k):
        for f in flows:
            for d in DIRS:
                p2(f, k, d).wait_recv()
                wires.go(p2half(f, k, d))

    def complete(k):
        for f in flows:
            for d in DIRS:
                p2half(f, k, d).wait_recv()
        arrived(k)

    each(p1)
    each(p2, 0)
    for f in flows:
        p1(f, 1).wait_recv()
        wires.go(p1half(f, 1))
        for d in DIRS:
            wires.go(p2(f, 1, d))
    for f in flows:
        p1(f, -1).wait_recv()
        wires.go(p1half(f, -1))
    relay(0)
    each(p2, 3)
    complete(0)
    t0 = flow(0)
    next(t0)
    relay(1)
    for f in flows:
        for d in DIRS:
            p1half(f, d).wait_recv()
    each(p2, 2)
    next(t0)
    complete(1)
    t1 = flow(1)
    next(t1)
    next(t0)
    relay(3)
    next(t0)
    next(t1)
    complete(3)
    t3 = flow(3)
    next(t3)
    next(t1)
    next(t0)
    relay(2)
    next(t1)
    next(t3)
    next(t0)
    complete(2)
    t2 = flow(2)
    next(t2)
    next(t3)
    next(t1)
    next(t2)
    next(t3)
    next(t1)
    next(t2)
    next(t3)
    next(t2)
    next(t3)
    next(t2)
    next(t2)
    for t in (t0, t1, t3, t2):
        for _ in t:
            pass


def by_rows(rows, body):
    def step(i, carry):
        body(pl.ds(pl.multiple_of(i * CHUNK, CHUNK), CHUNK))
        return carry

    lax.fori_loop(0, rows // CHUNK, step, 0)


def tok_flow(wires, tag, k, part, out, r1, s1, r2, r3, s3, epilogue):
    z, core = column()
    other = tok_peer(z, 1 - core)
    me = core * SIDE + z

    def peer(d):
        return tok_peer(ring(z, d), core)

    def swap(j):
        at = ring(z, j)
        return wires.copy((tag, k, 0, j), part.at[k, (1 - core) * SIDE + at], r1.at[k, j], other)

    def far(d):
        return wires.copy((tag, k, 1, d), s1.at[k, 2, rows_of(d)], r2.at[k, s(d)], peer(d))

    def plain(d):
        src = s1.at[k, 1 if d == 1 else 3, rows_of(-d)]
        return wires.copy((tag, k, 2, d), src, r3.at[k, s(d), rows_of(-d)], peer(d))

    def summed(d):
        return wires.copy((tag, k, 3, d), s3.at[k, s(d)], r3.at[k, s(d), rows_of(d)], peer(d))

    def spread(d):
        return wires.copy((tag, k, 4, d), out.at[k, me], out.at[k, me], peer(d))

    def forward(d):
        at = out.at[k, core * SIDE + ring(z, -d), rows_of(d)]
        return wires.copy((tag, k, 5, d), at, at, peer(d))

    def hand(j):
        at = out.at[k, core * SIDE + ring(z, j)]
        return wires.copy((tag, k, 6, j), at, at, other)

    def first(j):
        swap(j).wait_recv()
        at = core * SIDE + ring(z, j)

        def add(i):
            s1[k, j, i] = (f32(part[k, at, i]) + f32(r1[k, j, i])).astype(s1.dtype)

        by_rows(UNIT, add)

    for j in (2, 1, 3, 0):
        wires.go(swap(j))
    yield
    first(2)
    for d in DIRS:
        wires.go(far(d))
    for d in DIRS:
        first(1 if d == 1 else 3)
        wires.go(plain(d))
    first(0)
    yield
    for d in DIRS:
        far(d).wait_recv()
        s3[k, s(d)] = (f32(s1[k, 1 if d == 1 else 3, rows_of(d)]) + f32(r2[k, s(d)])).astype(s3.dtype)
        wires.go(summed(d))
    yield
    for d in DIRS:
        plain(d).wait_recv()
        summed(d).wait_recv()

    def last(i):
        total = f32(s1[k, 0, i]) + f32(r3[k, 0, i]) + f32(r3[k, 1, i])
        out[k, me, i] = epilogue(k, me, i, total).astype(out.dtype)

    by_rows(UNIT, last)
    for d in DIRS:
        wires.go(spread(d))
    wires.go(hand(0))
    yield
    for d in DIRS:
        spread(d).wait_recv()
        wires.go(forward(d))
        wires.go(hand(3 if d == 1 else 1))
    yield
    for d in DIRS:
        forward(d).wait_recv()
    wires.go(hand(2))
    yield
    for j in range(SIDE):
        hand(j).wait_recv()
    yield


def tok_buffers(dtype, width):
    return [
        pltpu.VMEM((SIDE, SIDE, UNIT, width), dtype),
        pltpu.VMEM((SIDE, SIDE, UNIT, width), dtype),
        pltpu.VMEM((SIDE, 2, HALF, width), dtype),
        pltpu.VMEM((SIDE, 2, UNIT, width), dtype),
        pltpu.VMEM((SIDE, 2, HALF, width), dtype),
    ]


def blocks(count, body):
    def step(i, carry):
        body(i)
        return carry

    lax.fori_loop(0, count, step, 0)


def own_tile(k):
    x, y = plane()
    z, core = column()
    return (1 - core) * (z * SIDE + ring(x, -k)) + core * (ring(y, -k) * SIDE + z)


QUAD = 4


def forward_kernel(x, enc, bias, mask, sq, xs, feat, sq_sum, held, part, feats, *rest):
    bufs, (sq_a, sq_b, local, send, recv) = rest[:5], rest[5:]
    wires = Wires(send, recv)
    z, core = column()
    flows = [Flow(h) for h in FLOWS]
    greet()
    slab_count, depth, width = enc.shape
    keep = [pltpu.make_async_copy(x.at[f.h], held.at[0, f.unit(0)], local.at[f.h]) for f in flows]
    for copy in keep:
        copy.start()
    saves = [pltpu.make_async_copy(held.at[k], xs.at[k], local.at[2 + k]) for k in range(SIDE)]
    saves_f = [pltpu.make_async_copy(feats.at[k], feat.at[k], local.at[6 + k]) for k in range(SIDE)]

    def epilogue(k, me, i, total):
        live = mask[own_tile(k)] > 0.0
        return jnp.where(live, jnp.maximum(total + bias[...], 0.0), 0.0)

    def arrived(k):
        if k == 0:
            for copy in keep:
                copy.wait()
        saves[k].start()

        def encode(i):
            slab, quad = lax.div(i, 2), lax.rem(i, 2)
            rows = held[k, pl.ds(quad * QUAD, QUAD)].reshape(QUAD * UNIT, depth)
            at = pl.ds(pl.multiple_of(slab * width, width), width)
            value = jnp.dot(rows, enc[slab], preferred_element_type=F32)
            part[k, pl.ds(quad * QUAD, QUAD), :, at] = value.reshape(QUAD, UNIT, width)

        blocks(2 * slab_count, encode)

    def flow(k):
        yield from tok_flow(wires, "f", k, part, feats, *bufs, epilogue)

    other = tok_peer(z, 1 - core)
    swap = wires.copy("sq", sq, sq_a.at[0], other)
    wires.go(swap)
    swap.wait_recv()
    sq_b[0] = sq[...] + sq_a[0]
    rounds = []
    for d in DIRS:
        rounds.append(wires.copy(("sq", d), sq_b.at[0], sq_b.at[1 + s(d)], tok_peer(ring(z, d), core)))
        wires.go(rounds[-1])
    sweep(wires, "x", lambda h: x.at[h], held, arrived, flow)
    for copy in rounds:
        copy.wait_recv()
    on = wires.copy(("sq", 2), sq_b.at[1], sq_b.at[3], tok_peer(ring(z, 1), core))
    wires.go(on)
    on.wait_recv()
    sq_sum[...] = (sq_b[0] + sq_b[3]) + (sq_b[1] + sq_b[2])
    for copy in saves_f:
        copy.start()
    for copy in saves + saves_f:
        copy.wait()
    wires.drain()


VMEM = pl.BlockSpec(memory_space=pltpu.VMEM)
ANY = pl.BlockSpec(memory_space=pl.ANY)


def forward(x, enc, bias, mask, sq):
    depth = x.shape[2]
    width = bias.shape[1]
    units = (SIDE, 2 * SIDE, UNIT)
    return pl.pallas_call(
        forward_kernel,
        out_shape=[
            jax.ShapeDtypeStruct(units + (depth,), BF16),
            jax.ShapeDtypeStruct(units + (width,), BF16),
            jax.ShapeDtypeStruct(sq.shape, F32),
        ],
        in_specs=[VMEM] * 5,
        out_specs=[ANY, ANY, VMEM],
        scratch_shapes=[
            pltpu.VMEM(units + (depth,), BF16),
            pltpu.VMEM(units + (width,), F32),
            pltpu.VMEM(units + (width,), BF16),
        ]
        + tok_buffers(F32, width)
        + [
            pltpu.VMEM((1,) + sq.shape, F32),
            pltpu.VMEM((4,) + sq.shape, F32),
            pltpu.SemaphoreType.DMA((10,)),
            pltpu.SemaphoreType.DMA((124,)),
            pltpu.SemaphoreType.DMA((124,)),
        ],
        compiler_params=pltpu.CompilerParams(
            vmem_limit_bytes=60 * 1024 * 1024, collective_id=0, has_side_effects=True
        ),
        name="forward",
    )(x, enc, bias, mask, sq)


def backward_kernel(
    scale, x, dec, bias, feats, norm, es, grads, part, r1, r2, s2, c, r4, r5, s5, err, gpart, out, *rest
):
    bufs, (local, send, recv) = rest[:5], rest[5:]
    wires = Wires(send, recv)
    flows = [Flow(h) for h in FLOWS]
    greet()
    width, depth = dec.shape
    cols = 512

    def decode(k):
        def step(i):
            col, quad = lax.div(i, 2), lax.rem(i, 2)
            at = pl.ds(pl.multiple_of(col * cols, cols), cols)
            f = feats[k, pl.ds(quad * QUAD, QUAD)].reshape(QUAD * UNIT, width)
            value = jnp.dot(f, dec[:, at], preferred_element_type=F32)
            part[k, pl.ds(quad * QUAD, QUAD), :, at] = value.reshape(QUAD, UNIT, cols).astype(BF16)

        blocks(2 * (depth // cols), step)

    def far(f, k, d):
        src = part.at[k, f.unit(2), rows_of(d)]
        return wires.copy((0, f.h, k, d), src, r1.at[f.h, k, s(d)], f.near(0, d))

    def plain(f, k, d):
        src = part.at[k, f.unit(d), rows_of(-d)]
        return wires.copy((1, f.h, k, d), src, r2.at[f.h, k, s(d), rows_of(-d)], f.near(0, d))

    def summed(f, k, d):
        src = s2.at[f.h, k, s(d)]
        return wires.copy((2, f.h, k, d), src, r2.at[f.h, k, s(d), rows_of(d)], f.near(0, d))

    def far2(f, d):
        return wires.copy((3, f.h, d), c.at[f.h, 2, rows_of(d)], r4.at[f.h, s(d)], f.near(d, 0))

    def plain2(f, d):
        src = c.at[f.h, 3 if d == 1 else 1, rows_of(-d)]
        return wires.copy((4, f.h, d), src, r5.at[f.h, s(d), rows_of(-d)], f.near(d, 0))

    def summed2(f, d):
        return wires.copy((5, f.h, d), s5.at[f.h, s(d)], r5.at[f.h, s(d), rows_of(d)], f.near(d, 0))

    def add_far(f, k):
        for d in DIRS:
            far(f, k, d).wait_recv()
            s2[f.h, k, s(d)] = (f32(part[k, f.unit(d), rows_of(d)]) + f32(r1[f.h, k, s(d)])).astype(BF16)
            wires.go(summed(f, k, d))

    def reduce(f, k):
        for d in DIRS:
            plain(f, k, d).wait_recv()
            summed(f, k, d).wait_recv()

        def add(i):
            total = f32(part[k, f.unit(0), i]) + f32(r2[f.h, k, 0, i]) + f32(r2[f.h, k, 1, i])
            c[f.h, k, i] = total.astype(BF16)

        by_rows(UNIT, add)

    def begin(k):
        decode(k)
        for f in flows:
            for d in DIRS:
                wires.go(far(f, k, d))
        for f in flows:
            for d in DIRS:
                wires.go(plain(f, k, d))

    def relay(k):
        for f in flows:
            add_far(f, k)

    begin(2)
    begin(1)
    relay(2)
    begin(3)
    relay(1)
    begin(0)
    for f in flows:
        reduce(f, 2)
        for d in DIRS:
            wires.go(far2(f, d))
    relay(3)
    for f in flows:
        reduce(f, 1)
        wires.go(plain2(f, -1))
    relay(0)
    for f in flows:
        reduce(f, 3)
        wires.go(plain2(f, 1))
    for f in flows:
        for d in DIRS:
            far2(f, d).wait_recv()
            s5[f.h, s(d)] = (f32(c[f.h, 3 if d == 1 else 1, rows_of(d)]) + f32(r4[f.h, s(d)])).astype(BF16)
            wires.go(summed2(f, d))
    for f in flows:
        reduce(f, 0)
    for f in flows:
        for d in DIRS:
            plain2(f, d).wait_recv()
            summed2(f, d).wait_recv()

        def finish(i):
            recon = f32(c[f.h, 0, i]) + f32(r5[f.h, 0, i]) + f32(r5[f.h, 1, i]) + bias[...]
            err[0, f.unit(0), i] = (recon - f32(x[f.h, i])).astype(BF16)

        by_rows(UNIT, finish)

    saves = [pltpu.make_async_copy(err.at[k], es.at[k], local.at[k]) for k in range(SIDE)]
    saves_g = [pltpu.make_async_copy(out.at[k], grads.at[k], local.at[4 + k]) for k in range(SIDE)]

    def arrived(k):
        saves[k].start()

        def step(i):
            slab, quad = lax.div(i, 2), lax.rem(i, 2)
            at = pl.ds(pl.multiple_of(slab * 256, 256), 256)
            e = err[k, pl.ds(quad * QUAD, QUAD)].reshape(QUAD * UNIT, depth)
            value = lax.dot_general(e, dec[at], NT, preferred_element_type=F32)
            gpart[k, pl.ds(quad * QUAD, QUAD), :, at] = value.reshape(QUAD, UNIT, 256).astype(BF16)

        blocks(2 * (width // 256), step)

    def epilogue(k, me, i, total):
        grad = scale * (total + SPARSITY * norm[...])
        return jnp.where(f32(feats[k, me, i]) > 0.0, grad, 0.0)

    def flow(k):
        yield from tok_flow(wires, "g", k, gpart, out, *bufs, epilogue)

    sweep(wires, "e", lambda h: err.at[0, flows[h].unit(0)], err, arrived, flow)
    for copy in saves_g:
        copy.start()
    for copy in saves + saves_g:
        copy.wait()
    wires.drain()


def backward(scale, x, dec, bias, feats, norm):
    width, depth = dec.shape
    units = (SIDE, 2 * SIDE, UNIT)
    return pl.pallas_call(
        functools.partial(backward_kernel, scale),
        out_shape=[
            jax.ShapeDtypeStruct(units + (depth,), BF16),
            jax.ShapeDtypeStruct(units + (width,), BF16),
        ],
        in_specs=[VMEM] * 5,
        out_specs=[ANY, ANY],
        scratch_shapes=[
            pltpu.VMEM(units + (depth,), BF16),
            pltpu.VMEM((2, SIDE, 2, HALF, depth), BF16),
            pltpu.VMEM((2, SIDE, 2, UNIT, depth), BF16),
            pltpu.VMEM((2, SIDE, 2, HALF, depth), BF16),
            pltpu.VMEM((2, SIDE, UNIT, depth), BF16),
            pltpu.VMEM((2, 2, HALF, depth), BF16),
            pltpu.VMEM((2, 2, UNIT, depth), BF16),
            pltpu.VMEM((2, 2, HALF, depth), BF16),
            pltpu.VMEM(units + (depth,), BF16),
            pltpu.VMEM(units + (width,), BF16),
            pltpu.VMEM(units + (width,), BF16),
        ]
        + tok_buffers(BF16, width)
        + [
            pltpu.SemaphoreType.DMA((8,)),
            pltpu.SemaphoreType.DMA((190,)),
            pltpu.SemaphoreType.DMA((190,)),
        ],
        compiler_params=pltpu.CompilerParams(
            vmem_limit_bytes=60 * 1024 * 1024, collective_id=1, has_side_effects=True
        ),
        name="backward",
    )(x, dec, bias, feats, norm)


def on_device(activations, enc_weight, enc_bias, dec_weight, dec_bias, active):
    slabs, models, depth, block = enc_weight.shape
    rows = activations.shape[0]
    width = slabs * block
    scale = 1.0 / math.sqrt(MOST * TILE)
    first = lax.axis_index("lat") * slabs
    ids = first + jnp.arange(slabs, dtype=jnp.int32)
    live = jnp.any(active[:, :, None] == ids[None, None, :], axis=1).astype(F32)
    mask = jnp.broadcast_to(live[:, None, :, None], (active.shape[0], 1, slabs, block))
    mask = mask.reshape(active.shape[0], 1, width)
    x = activations.reshape(2, rows // 2, models * depth)
    dec = dec_weight.reshape(width, models * depth)
    dec_wide = dec.reshape(width, models, depth).astype(F32)
    sq = jnp.sum(jnp.square(dec_wide), axis=2).T
    enc = enc_weight.reshape(slabs, models * depth, block)
    xs, feats, sq_sum = forward(x, enc, enc_bias.reshape(1, width), mask, sq)
    norms = jnp.sqrt(sq_sum + NORM_EPSILON)
    es, grads = backward(
        scale,
        x,
        dec,
        dec_bias.reshape(1, models * depth),
        feats,
        jnp.sum(norms, axis=0, keepdims=True),
    )
    count = active.shape[0] * rows
    xs, es = xs.reshape(count, models, depth), es.reshape(count, models, depth)
    feats, grads = feats.reshape(count, width), grads.reshape(count, slabs, block)
    grad_enc = jnp.einsum("rmd,rsj->smdj", xs, grads, preferred_element_type=F32).astype(BF16)
    grad_enc_bias = jnp.sum(grads.astype(F32), axis=0)
    feat_total = jnp.sum(feats.astype(F32), axis=0)
    recon_term = jnp.einsum("rj,rmd->jmd", feats, es, preferred_element_type=F32)
    norm_term = (SPARSITY * feat_total[:, None] / norms.T)[:, :, None] * dec_wide
    grad_dec = (scale * (recon_term + norm_term)).astype(BF16)
    grad_dec_bias = scale * jnp.sum(es.astype(F32), axis=0)
    return (grad_enc, grad_enc_bias, grad_dec.reshape(dec_weight.shape), grad_dec_bias)


def solution(mesh):
    placed = (
        P("lat", None, "tok"),
        P("lat", None, "tok", None),
        P("lat", None),
        P("lat", None, None, "tok"),
        P(None, "tok"),
        P(),
    )
    return jax.shard_map(
        on_device,
        mesh=mesh,
        in_specs=placed,
        out_specs=(
            P("lat", None, "tok", None),
            P("lat", None),
            P("lat", None, None, "tok"),
            P(None, "tok"),
        ),
        check_vma=False,
    )
```

time: 586 us -> 373 us (0.64)
  waiting for transfers between devices: 342 us -> 0 us
  Pallas kernels: 0 us -> 252 us
  other arithmetic: 95.3 us -> 16.5 us
  matrix products: 61.8 us -> 28.8 us
  blocking collectives: 14.3 us -> 0 us
  between operations: 13.8 us -> 0.88 us
  local copies, waits for them, and re-layouts: 56.5 us -> 69 us
    pallas_call x0 -> x2, Pallas kernels: none -> 252 us  [the longest x1 140 us: backward(): pl.pallas_call(functools.partial(backward_kernel, scale), out_shape=[jax....]
    psum x2 -> x0, waiting for transfers between devices: 129 us -> none  [the longest x1 70.5 us: on_device(): pre_act = lax.psum(pre_part, 'tok') + enc_bias[:, None, None, :]]
    all_gather x2 -> x0, waiting for transfers between devices: 128 us -> none  [the longest x1 73.9 us: on_device(): gathered = lax.all_gather(activations, 'lat', axis=0, tiled=True)]
    reduce_scatter x1 -> x0, waiting for transfers between devices: 85.5 us -> none  [on_device(): lax.psum_scatter(rounded.astype(jnp.bfloat16), 'lat', scatter_dimension=0...]
    scatter-add x1 -> x0, other arithmetic: 65.6 us -> none  [on_device(): partial_value = jnp.zeros((tile_count, tile_rows, models, feat_width), jn...]
    dot_general x5 -> x2, matrix products: 61.8 us -> 28.8 us  [the longest x1 14.5 us: on_device(): jnp.einsum('rj,rmd->jmd', feats, es, preferred_element_type=F32)]
    reshape x1 -> x4, local copies, waits for them, and re-layouts: 8.19 us -> 39 us  [the longest x1 14.5 us: on_device(): xs.reshape(count, models, depth)]
    gather x2 -> x0, local copies, waits for them, and re-layouts: 21 us -> none  [the longest x1 10.5 us: on_device(): err_chosen = tile_err[slot_tile]]
  transfers between devices with their start and end apart: 5 -> 0, of which waited for: 5 -> 0; matrix products, arithmetic and copies ran while one was open for 2% -> 0% of each run, Pallas kernels for 0% -> 0%
where the time goes in v2:
time: 373 us; the launch traced here: 367 us
  Pallas kernels  252 us (68%)
  local copies, waits for them, and re-layouts  69 us (18%)
  matrix products  28.8 us (8%)
  other arithmetic  16.5 us (4%)
    pallas_call x1, Pallas kernels, backward(): pl.pallas_call(functools.partial(backward_kernel, scale), out_shape=[jax....  140 us
    pallas_call x1, Pallas kernels, forward(): pl.pallas_call(forward_kernel, out_shape=[jax.ShapeDtypeStruct(units + (d...  111 us
    unnamed x11, local copies, waits for them, and re-layouts  20.2 us
    reshape x1, local copies, waits for them, and re-layouts, on_device(): xs.reshape(count, models, depth)  14.5 us
    dot_general x1, matrix products, on_device(): jnp.einsum('rj,rmd->jmd', feats, es, preferred_element_type=F32)  14.5 us
    reshape x1, local copies, waits for them, and re-layouts, on_device(): es.reshape(count, models, depth)  14.4 us
    dot_general x1, matrix products, on_device(): jnp.einsum('rmd,rsj->smdj', xs, grads, preferred_element_type=F32)  14.3 us
    reshape x1, local copies, waits for them, and re-layouts, on_device(): grads.reshape(count, slabs, block)  7.83 us

profile of v2, /device:TPU:1, one launch (start us, length us, event | category | flops | bytes accessed | tf_op | source)
XLA Modules:
  0.0 367.0 jit_solution(13000171606720006775)
XLA Ops:
  0.6 2.2 reshape.64.x
  2.8 1.3 copy.42
  4.1 0.9 compare_reduce_fusion
  5.1 0.1 copy.25
  5.1 0.1 broadcast_in_dim.6
  5.2 0.7 broadcast_in_dim.7.mask
  5.9 6.6 %multiply_reduce_fusion = f32[4,256,2]{2,1,0:T(8,128)S(1)} fusion(bf16[4,256,2,1024]{3,2,1,0:T(2,128)(2,1)} %param.9), kind=kLoop, calls=%fused_computation.12 | loop fusion | flops 6289408 | bytes 4202496 | tf_op jit(solution)/shard_map/reduce_sum | solution.py:609
  12.6 0.8 copy.36
  13.3 111.5 %forward.1 = (bf16[4,8,64,2048]{3,2,1,0:T(8,128)(2,1)}, bf16[4,8,64,1024]{3,2,1,0:T(8,128)(2,1)}, f32[2,1024]{1,0:T(2,128)}) custom-call(bf16[2,64,2048]{2,1,0:T(8,128)(2,1)} %reshape.64.x, bf16[4,2048,256]{2,1,0:T(8,128)(2,1)} %bitcast.45, f32[1,1024]{1,0:T(1,128)} %bitcast.52, f32[16,1,1024]{2,1,0:T(1,128)} %broadcast_in_dim.7.mask, f32[2,1024]{1,0:T(2,128)} %bitcast.49), custom_call_target="tpu_custom_call" | custom-call | tf_op jit(solution)/shard_map/forward/pallas_call | solution.py:392
  124.8 14.5 %reshape.70 = bf16[2048,2,1024]{2,1,0:T(2,128)(2,1)} reshape(bf16[4,8,64,2048]{3,2,1,0:T(8,128)(2,1)} %get-tuple-element.12) | data formatting | bytes 16777216 | tf_op jit(solution)/shard_map/reshape | solution.py:622
  139.3 0.0 copy-start.2
  139.3 0.0 copy-start
  139.3 0.0 copy-start.1
  139.3 5.8 %copy.40 = bf16[128,8,2,1024]{3,1,2,0:T(8,128)(2,1)} copy(bf16[128,8,2,1024]{3,2,1,0:T(2,128)(2,1)} %bitcast.42) | data formatting | bytes 8388608
  145.1 0.0 copy-done.2
  145.1 0.6 copy.41
  145.7 0.0 copy-done
  145.7 0.7 convert_reduce_fusion.1
  146.5 0.0 copy-done.1
  146.5 0.6 divide_bitcast_fusion
  147.1 140.3 %backward.1 = (bf16[4,8,64,2048]{3,2,1,0:T(8,128)(2,1)}, bf16[4,8,64,1024]{3,2,1,0:T(8,128)(2,1)}) custom-call(bf16[2,64,2048]{2,1,0:T(8,128)(2,1)} %reshape.64.x, bf16[1024,2048]{1,0:T(8,128)(2,1)} %bitcast.44, f32[1,2048]{1,0:T(1,128)} %bitcast.50, bf16[4,8,64,1024]{3,2,1,0:T(8,128)(2,1)} %get-tuple-element.9.feats, f32[1,1024]{1,0:T(1,128)} %bitcast.51), custom_call_target="tpu_custom_call" | custom-call | tf_op jit(solution)/shard_map/backward/pallas_call | solution.py:562
  287.4 7.8 %reshape.69 = bf16[2048,4,256]{2,1,0:T(4,128)(2,1)} reshape(bf16[4,8,64,1024]{3,2,1,0:T(8,128)(2,1)} %get-tuple-element.11) | data formatting | bytes 8388608 | tf_op jit(solution)/shard_map/reshape | solution.py:623
  295.2 14.3 %convert_bitcast_fusion = bf16[4,2,1024,256]{2,3,1,0:T(8,128)(2,1)} fusion(bf16[2048,2,1024]{2,1,0:T(2,128)(2,1)} %reshape.70, bf16[2048,4,256,1]{2,1,0,3:T(4,128)(2,1)} %bitcast.47), kind=kOutput, calls=%fused_computation.14 | convolution fusion | flops 8592031744 | bytes 16777216 | tf_op jit(solution)/shard_map/rmd,rsj->smdj/dot_general | solution.py:624
  309.5 6.2 %copy.32 = bf16[4,2,1024,256]{3,2,1,0:T(8,128)(2,1)} copy(bf16[4,2,1024,256]{2,3,1,0:T(8,128)(2,1)} %convert_bitcast_fusion) | data formatting | bytes 8388608
  315.7 2.9 convert_reduce_fusion.2
  318.6 0.6 reduce_sum.53
  319.2 6.9 %copy.31 = f32[4,256,2,1024]{3,1,0,2:T(8,128)} copy(bf16[4,256,2,1024]{3,2,1,0:T(2,128)(2,1)} %param.9) | data formatting | bytes 12582912 | tf_op jit(solution)/shard_map/convert_element_type | solution.py:608
  326.1 14.4 %reshape.72 = bf16[2048,2,1024]{2,1,0:T(2,128)(2,1)} reshape(bf16[4,8,64,2048]{3,2,1,0:T(8,128)(2,1)} %get-tuple-element.13) | data formatting | bytes 16777216 | tf_op jit(solution)/shard_map/reshape | solution.py:622
  340.6 14.5 %fusion.2 = bf16[1024,2,1024]{2,0,1:T(8,128)(2,1)S(1)} fusion(f32[4,256,2,1024]{3,1,0,2:T(8,128)} %copy.31, bf16[2048,1024,1]{1,0,2:T(8,128)(2,1)} %bitcast.43, bf16[2048,2,1024]{2,1,0:T(2,128)(2,1)} %reshape.72, f32[1024,2]{0,1:T(2,128)S(1)} %get-tuple-element.26), kind=kOutput, calls=%fused_computation.4 | convolution fusion | flops 8598323200 | bytes 25174016 | tf_op jit(solution)/shard_map/rj,rmd->jmd/dot_general | solution.py:627
  355.1 6.3 %copy.33 = bf16[4,256,2,1024]{3,2,1,0:T(2,128)(2,1)} copy(bf16[4,256,2,1024]{3,1,0,2:T(8,128)(2,1)S(1)} %bitcast.46) | data formatting | bytes 8388608
  361.4 4.7 %convert_reduce_fusion = f32[2048]{0:T(1024)S(1)} fusion(bf16[4,8,64,2048]{3,2,1,0:T(8,128)(2,1)} %get-tuple-element.13), kind=kLoop, calls=%fused_computation | loop fusion | flops 8386560 | bytes 8396800 | tf_op jit(solution)/shard_map/reduce_sum | solution.py:630
  366.2 0.6 mul.46
  (4 shorter events, 0.0 us)
Async XLA Ops:
  139.3 5.8 %copy-start.2 = (f32[2,1024]{1,0:T(2,128)S(1)}, f32[2,1024]{1,0:T(2,128)}, u32[]{:S(2)}) copy-start(f32[2,1024]{1,0:T(2,128)} %param.10) | copy-start | bytes 24580
  139.3 6.4 %copy-start = (bf16[4,8,64,1024]{3,2,1,0:T(8,128)(2,1)S(1)}, bf16[4,8,64,1024]{3,2,1,0:T(8,128)(2,1)}, u32[]{:S(2)}) copy-start(bf16[4,8,64,1024]{3,2,1,0:T(8,128)(2,1)} %get-tuple-element.9.feats) | copy-start | bytes 12582916
  139.3 7.1 %copy-start.1 = (f32[2,1024]{1,0:T(2,128)S(1)}, f32[2,1024]{1,0:T(2,128)}, u32[]{:S(2)}) copy-start(f32[2,1024]{1,0:T(2,128)} %get-tuple-element.10) | copy-start | bytes 24580

commit v3 on v2

v3 whole, which is shorter than its diff:
```python
import functools
import math

import jax
import jax.numpy as jnp
from jax import lax
from jax.experimental import pallas as pl
from jax.experimental.pallas import tpu as pltpu
from jax.sharding import PartitionSpec as P

MOST = 8
TILE = 128
SPARSITY = 0.25
NORM_EPSILON = 1e-06
MESH = pl.DeviceIdType.MESH
SIDE = 4
UNIT = TILE // 2
HALF = UNIT // 2
CHUNK = 32
DIRS = (1, -1)
ORDER = (0, 1, 3, 2)
BF16, F32 = jnp.bfloat16, jnp.float32
NT = (((1,), (1,)), ((), ()))
TN = (((0,), (0,)), ((), ()))


def ring(i, step):
    return lax.rem(i + step + SIDE, SIDE)


def lat_peer(y, x):
    return {"lat": y * SIDE + x}


def tok_peer(z, core):
    return {"tok": z * 2 + core}


def plane():
    lat = lax.axis_index("lat")
    return lax.rem(lat, SIDE), lax.div(lat, SIDE)


def column():
    tok = lax.axis_index("tok")
    return lax.div(tok, 2), lax.rem(tok, 2)


def greet():
    x, y = plane()
    z, core = column()
    peers = [lat_peer(y, ring(x, d)) for d in DIRS] + [lat_peer(ring(y, d), x) for d in DIRS]
    peers += [tok_peer(ring(z, d), core) for d in DIRS] + [tok_peer(z, 1 - core)]
    barrier = pltpu.get_barrier_semaphore()
    for peer in peers:
        pl.semaphore_signal(barrier, inc=1, device_id=peer, device_id_type=MESH)
    pl.semaphore_wait(barrier, len(peers))


def s(d):
    return 0 if d == 1 else 1


def rows_of(d):
    return pl.ds(0 if d == 1 else HALF, HALF)


def f32(v):
    return v.astype(F32)


class Wires:
    def __init__(self, send, recv):
        self.send, self.recv = send, recv
        self.numbers, self.started = {}, []

    def copy(self, key, src, dst, peer):
        n = self.numbers.setdefault(key, len(self.numbers))
        return pltpu.make_async_remote_copy(
            src_ref=src,
            dst_ref=dst,
            send_sem=self.send.at[n],
            recv_sem=self.recv.at[n],
            device_id=peer,
            device_id_type=MESH,
        )

    def go(self, copy, source=None):
        copy.start()
        self.started.append((source, copy))

    def settle(self, source):
        for name, copy in self.started:
            if name == source:
                copy.wait_send()
        self.started = [item for item in self.started if item[0] != source]

    def drain(self):
        for _, copy in self.started:
            copy.wait_send()


FLOWS = (0, 1)


class Flow:
    def __init__(self, h):
        x, y = plane()
        self.h = h
        self.p, self.q = (x, y) if h == 0 else (y, x)

    def near(self, dp, dq):
        p, q = ring(self.p, dp), ring(self.q, dq)
        return lat_peer(q, p) if self.h == 0 else lat_peer(p, q)

    def unit(self, dq):
        return self.h * SIDE + ring(self.q, dq)


class Gather:
    def __init__(self, wires, flows, tag, own, held, own_source):
        self.wires, self.flows, self.tag = wires, flows, tag
        self.own, self.held, self.own_source = own, held, own_source

    def p1(self, f, d):
        dst = self.held.at[1 if d == 1 else 3, f.unit(0)]
        return self.wires.copy((self.tag, 0, f.h, d), self.own(f.h), dst, f.near(d, 0))

    def p1half(self, f, d):
        src = self.held.at[1 if d == 1 else 3, f.unit(0), rows_of(d)]
        dst = self.held.at[2, f.unit(0), rows_of(d)]
        return self.wires.copy((self.tag, 1, f.h, d), src, dst, f.near(d, 0))

    def p2(self, f, k, d):
        at = self.held.at[k, f.unit(0)]
        return self.wires.copy((self.tag, 2, f.h, k, d), self.own(f.h) if k == 0 else at, at, f.near(0, d))

    def p2half(self, f, k, d):
        at = self.held.at[k, f.unit(-d), rows_of(d)]
        return self.wires.copy((self.tag, 3, f.h, k, d), at, at, f.near(0, d))

    def name(self, k):
        return (self.tag, k)

    def send(self, k):
        for f in self.flows:
            for d in DIRS:
                self.wires.go(self.p2(f, k, d), self.own_source if k == 0 else self.name(k))

    def begin(self):
        for f in self.flows:
            for d in DIRS:
                self.wires.go(self.p1(f, d), self.own_source)
        self.send(0)
        for d, k in ((1, 1), (-1, 3)):
            for f in self.flows:
                self.p1(f, d).wait_recv()
                self.wires.go(self.p1half(f, d), self.name(k))
            self.send(k)

    def far(self):
        for f in self.flows:
            for d in DIRS:
                self.p1half(f, d).wait_recv()
        self.send(2)

    def relay(self, k):
        for f in self.flows:
            for d in DIRS:
                self.p2(f, k, d).wait_recv()
                self.wires.go(self.p2half(f, k, d), self.name(k))

    def complete(self, k):
        for f in self.flows:
            for d in DIRS:
                self.p2half(f, k, d).wait_recv()


def by_rows(rows, body):
    def step(i, carry):
        body(pl.ds(pl.multiple_of(i * CHUNK, CHUNK), CHUNK))
        return carry

    lax.fori_loop(0, rows // CHUNK, step, 0)


def tok_flow(wires, tag, k, part, out, r1, s1, r2, r3, epilogue):
    n = ORDER.index(k) % 2
    z, core = column()
    other = tok_peer(z, 1 - core)
    me = core * SIDE + z
    inputs, sums = (tag, k, "in"), (tag, k, "sum")

    def peer(d):
        return tok_peer(ring(z, d), core)

    def swap(j):
        at = ring(z, j)
        return wires.copy((tag, k, 0, j), part.at[n, (1 - core) * SIDE + at], r1.at[n, j], other)

    def far(d):
        return wires.copy((tag, k, 1, d), s1.at[n, 2, rows_of(d)], r2.at[n, s(d)], peer(d))

    def plain(d):
        src = s1.at[n, 1 if d == 1 else 3, rows_of(-d)]
        return wires.copy((tag, k, 2, d), src, r3.at[n, s(d), rows_of(-d)], peer(d))

    def summed(d):
        src = s1.at[n, 1 if d == 1 else 3, rows_of(d)]
        return wires.copy((tag, k, 3, d), src, r3.at[n, s(d), rows_of(d)], peer(d))

    def spread(d):
        return wires.copy((tag, k, 4, d), out.at[k, me], out.at[k, me], peer(d))

    def forward(d):
        at = out.at[k, core * SIDE + ring(z, -d), rows_of(d)]
        return wires.copy((tag, k, 5, d), at, at, peer(d))

    def hand(j):
        at = out.at[k, core * SIDE + ring(z, j)]
        return wires.copy((tag, k, 6, j), at, at, other)

    def first(j):
        swap(j).wait_recv()
        at = core * SIDE + ring(z, j)

        def add(i):
            s1[n, j, i] = (f32(part[n, at, i]) + f32(r1[n, j, i])).astype(s1.dtype)

        by_rows(UNIT, add)

    for j in (2, 1, 3, 0):
        wires.go(swap(j), inputs)
    yield
    first(2)
    for d in DIRS:
        wires.go(far(d), sums)
    for d in DIRS:
        first(1 if d == 1 else 3)
        wires.go(plain(d), sums)
    first(0)
    yield
    for d in DIRS:
        far(d).wait_recv()
        j = 1 if d == 1 else 3
        s1[n, j, rows_of(d)] = (f32(s1[n, j, rows_of(d)]) + f32(r2[n, s(d)])).astype(s1.dtype)
        wires.go(summed(d), sums)
    yield
    for d in DIRS:
        plain(d).wait_recv()
        summed(d).wait_recv()

    def last(i):
        total = f32(s1[n, 0, i]) + f32(r3[n, 0, i]) + f32(r3[n, 1, i])
        out[k, me, i] = epilogue(k, me, i, total).astype(out.dtype)

    by_rows(UNIT, last)
    for d in DIRS:
        wires.go(spread(d))
    wires.go(hand(0))
    yield
    for d in DIRS:
        spread(d).wait_recv()
        wires.go(forward(d))
        wires.go(hand(3 if d == 1 else 1))
    yield
    for d in DIRS:
        forward(d).wait_recv()
    wires.go(hand(2))
    yield
    for j in range(SIDE):
        hand(j).wait_recv()
    wires.settle(inputs)
    wires.settle(sums)
    yield


def tok_buffers(dtype, width):
    return [
        pltpu.VMEM((2, 2 * SIDE, UNIT, width), dtype),
        pltpu.VMEM((2, SIDE, UNIT, width), dtype),
        pltpu.VMEM((2, SIDE, UNIT, width), dtype),
        pltpu.VMEM((2, 2, HALF, width), dtype),
        pltpu.VMEM((2, 2, UNIT, width), dtype),
    ]


def blocks(count, body):
    def step(i, carry):
        body(i)
        return carry

    lax.fori_loop(0, count, step, 0)


def own_tile(k):
    x, y = plane()
    z, core = column()
    return (1 - core) * (z * SIDE + ring(x, -k)) + core * (ring(y, -k) * SIDE + z)


QUAD = 4


def step_kernel(
    scale,
    x,
    enc,
    dec,
    enc_bias,
    dec_bias,
    mask,
    sq,
    xs,
    es,
    feat_out,
    grad_out,
    sq_sum,
    held,
    err,
    feats,
    grads,
    r1,
    r2,
    r4,
    r5,
    norm,
    sq_a,
    sq_b,
    *rest,
):
    fwd, bwd, (local, send, recv) = rest[:5], rest[5:10], rest[10:]
    wires = Wires(send, recv)
    z, core = column()
    flows = [Flow(h) for h in FLOWS]
    slab_count, depth, block = enc.shape
    width = dec.shape[0]
    cols = 512
    keep = [pltpu.make_async_copy(x.at[f.h], held.at[0, f.unit(0)], local.at[f.h]) for f in flows]
    saves = {}

    def save(name, k, src, dst):
        n = 2 + len(saves)
        saves[name, k] = pltpu.make_async_copy(src.at[k], dst.at[k], local.at[n])
        saves[name, k].start()

    for copy in keep:
        copy.start()
    greet()


    def feature(k, me, i, total):
        live = mask[own_tile(k)] > 0.0
        return jnp.where(live, jnp.maximum(total + enc_bias[...], 0.0), 0.0)

    def encode(k):
        n = ORDER.index(k) % 2

        def step(i):
            slab, quad = lax.div(i, 2), lax.rem(i, 2)
            rows = held[k, pl.ds(quad * QUAD, QUAD)].reshape(QUAD * UNIT, depth)
            at = pl.ds(pl.multiple_of(slab * block, block), block)
            value = jnp.dot(rows, enc[slab], preferred_element_type=F32)
            fwd[0][n, pl.ds(quad * QUAD, QUAD), :, at] = value.reshape(QUAD, UNIT, block)

        blocks(2 * slab_count, step)

    swap = wires.copy("sq", sq, sq_a.at[0], tok_peer(z, 1 - core))
    turns = [wires.copy(("sq", d), sq_b.at[0], sq_b.at[1 + s(d)], tok_peer(ring(z, d), core)) for d in DIRS]
    turn_on = wires.copy(("sq", 2), sq_b.at[1], sq_b.at[3], tok_peer(ring(z, 1), core))

    def gather_steps(g, tag, bufs, out, work, epilogue, save_rows, save_out, between):
        t = {k: tok_flow(wires, tag, k, bufs[0], out, *bufs[1:], epilogue) for k in ORDER}

        def arrive(k):
            g.complete(k)
            save_rows(k)
            work(k)
            next(t[k])

        def go(k, count=1):
            for _ in range(count):
                next(t[k])

        def end(k):
            go(k)
            save_out(k)

        g.begin()
        g.relay(0)
        g.far()
        arrive(0)
        between(0)
        go(0)
        g.relay(1)
        go(0)
        arrive(1)
        between(1)
        go(0, 2)
        go(1)
        g.relay(3)
        go(1)
        go(0)
        end(0)
        arrive(3)
        between(2)
        go(1, 2)
        go(3)
        g.relay(2)
        go(3)
        go(1)
        end(1)
        arrive(2)
        yield
        go(3, 2)
        go(2)
        yield
        go(2)
        go(3)
        end(3)
        yield
        go(2, 2)
        yield
        go(2)
        end(2)
        yield

    def own_x(h):
        return x.at[h]

    def norms(stage):
        if stage == 0:
            swap.wait_recv()
            sq_b[0] = sq[...] + sq_a[0]
            for copy in turns:
                wires.go(copy)
        elif stage == 1:
            for copy in turns:
                copy.wait_recv()
            wires.go(turn_on)
        else:
            turn_on.wait_recv()
            total = (sq_b[0] + sq_b[3]) + (sq_b[1] + sq_b[2])
            sq_sum[...] = total
            norm[...] = jnp.sum(jnp.sqrt(total + NORM_EPSILON), axis=0, keepdims=True)

    wires.go(swap)
    front = Gather(wires, flows, "x", own_x, held, "own x")

    def save_x(k):
        if k == 0:
            for copy in keep:
                copy.wait()
        save("x", k, held, xs)

    steps = gather_steps(
        front, "f", fwd, feats, encode, feature, save_x, lambda k: save("f", k, feats, feat_out), norms
    )
    next(steps)


    def decode(k):
        wires.settle(front.name(k))
        saves["x", k].wait()

        def step(i):
            col, quad = lax.div(i, 2), lax.rem(i, 2)
            at = pl.ds(pl.multiple_of(col * cols, cols), cols)
            f = feats[k, pl.ds(quad * QUAD, QUAD)].reshape(QUAD * UNIT, width)
            value = jnp.dot(f, dec[:, at], preferred_element_type=F32)
            held[k, pl.ds(quad * QUAD, QUAD), :, at] = value.reshape(QUAD, UNIT, cols).astype(BF16)

        blocks(2 * (depth // cols), step)

    def far(f, k, d):
        src = held.at[k, f.unit(2), rows_of(d)]
        return wires.copy((0, f.h, k, d), src, r1.at[f.h, k, s(d)], f.near(0, d))

    def plain(f, k, d):
        src = held.at[k, f.unit(d), rows_of(-d)]
        return wires.copy((1, f.h, k, d), src, r2.at[f.h, k, s(d), rows_of(-d)], f.near(0, d))

    def summed(f, k, d):
        src = held.at[k, f.unit(d), rows_of(d)]
        return wires.copy((2, f.h, k, d), src, r2.at[f.h, k, s(d), rows_of(d)], f.near(0, d))

    def far2(f, d):
        src = held.at[2, f.unit(0), rows_of(d)]
        return wires.copy((3, f.h, d), src, r4.at[f.h, s(d)], f.near(d, 0))

    def plain2(f, d):
        src = held.at[3 if d == 1 else 1, f.unit(0), rows_of(-d)]
        return wires.copy((4, f.h, d), src, r5.at[f.h, s(d), rows_of(-d)], f.near(d, 0))

    def summed2(f, d):
        src = held.at[3 if d == 1 else 1, f.unit(0), rows_of(d)]
        return wires.copy((5, f.h, d), src, r5.at[f.h, s(d), rows_of(d)], f.near(d, 0))

    def begin(k):
        decode(k)
        for f in flows:
            for d in DIRS:
                wires.go(far(f, k, d))
        for f in flows:
            for d in DIRS:
                wires.go(plain(f, k, d))

    def relay(k):
        for f in flows:
            for d in DIRS:
                far(f, k, d).wait_recv()
                at = (k, f.unit(d), rows_of(d))
                held[at] = (f32(held[at]) + f32(r1[f.h, k, s(d)])).astype(BF16)
                wires.go(summed(f, k, d))

    def reduce(k):
        for f in flows:
            for d in DIRS:
                plain(f, k, d).wait_recv()
                summed(f, k, d).wait_recv()

            def add(i, f=f):
                total = f32(held[k, f.unit(0), i]) + f32(r2[f.h, k, 0, i]) + f32(r2[f.h, k, 1, i])
                held[k, f.unit(0), i] = total.astype(BF16)

            by_rows(UNIT, add)

    begin(0)
    next(steps)
    begin(1)
    relay(0)
    next(steps)
    begin(3)
    next(steps)
    relay(1)
    reduce(0)
    next(steps)
    begin(2)
    relay(3)
    reduce(1)
    for f in flows:
        wires.go(plain2(f, -1))
    relay(2)
    reduce(3)
    for f in flows:
        wires.go(plain2(f, 1))
    reduce(2)
    for f in flows:
        for d in DIRS:
            wires.go(far2(f, d))
    for f in flows:
        for d in DIRS:
            far2(f, d).wait_recv()
            at = (3 if d == 1 else 1, f.unit(0), rows_of(d))
            held[at] = (f32(held[at]) + f32(r4[f.h, s(d)])).astype(BF16)
            wires.go(summed2(f, d))
    for f in flows:
        for d in DIRS:
            plain2(f, d).wait_recv()
            summed2(f, d).wait_recv()

        def finish(i, f=f):
            recon = f32(held[0, f.unit(0), i]) + f32(r5[f.h, 0, i]) + f32(r5[f.h, 1, i]) + dec_bias[...]
            err[0, f.unit(0), i] = (recon - f32(x[f.h, i])).astype(BF16)

        by_rows(UNIT, finish)


    def project(k):
        n = ORDER.index(k) % 2

        def step(i):
            slab, quad = lax.div(i, 2), lax.rem(i, 2)
            at = pl.ds(pl.multiple_of(slab * block, block), block)
            e = err[k, pl.ds(quad * QUAD, QUAD)].reshape(QUAD * UNIT, depth)
            value = lax.dot_general(e, dec[at], NT, preferred_element_type=F32)
            bwd[0][n, pl.ds(quad * QUAD, QUAD), :, at] = value.reshape(QUAD, UNIT, block).astype(BF16)

        blocks(2 * slab_count, step)

    def pre_grad(k, me, i, total):
        grad = scale * (total + SPARSITY * norm[...])
        return jnp.where(f32(feats[k, me, i]) > 0.0, grad, 0.0)

    back = Gather(wires, flows, "e", lambda h: err.at[0, flows[h].unit(0)], err, "own e")
    for _ in gather_steps(
        back,
        "g",
        bwd,
        grads,
        project,
        pre_grad,
        lambda k: save("e", k, err, es),
        lambda k: save("g", k, grads, grad_out),
        lambda stage: None,
    ):
        pass
    for (name, _), copy in saves.items():
        if name != "x":
            copy.wait()
    wires.drain()


VMEM = pl.BlockSpec(memory_space=pltpu.VMEM)
ANY = pl.BlockSpec(memory_space=pl.ANY)


def step(scale, x, enc, dec, enc_bias, dec_bias, mask, sq):
    width, depth = dec.shape
    units = (SIDE, 2 * SIDE, UNIT)
    rows = jax.ShapeDtypeStruct(units + (depth,), BF16)
    latents = jax.ShapeDtypeStruct(units + (width,), BF16)
    return pl.pallas_call(
        functools.partial(step_kernel, scale),
        out_shape=[rows, rows, latents, latents, jax.ShapeDtypeStruct(sq.shape, F32)],
        in_specs=[VMEM] * 7,
        out_specs=[ANY, ANY, ANY, ANY, VMEM],
        scratch_shapes=[
            pltpu.VMEM(units + (depth,), BF16),
            pltpu.VMEM(units + (depth,), BF16),
            pltpu.VMEM(units + (width,), BF16),
            pltpu.VMEM(units + (width,), BF16),
            pltpu.VMEM((2, SIDE, 2, HALF, depth), BF16),
            pltpu.VMEM((2, SIDE, 2, UNIT, depth), BF16),
            pltpu.VMEM((2, 2, HALF, depth), BF16),
            pltpu.VMEM((2, 2, UNIT, depth), BF16),
            pltpu.VMEM((1, width), F32),
            pltpu.VMEM((1,) + sq.shape, F32),
            pltpu.VMEM((4,) + sq.shape, F32),
        ]
        + tok_buffers(F32, width)
        + tok_buffers(BF16, width)
        + [
            pltpu.SemaphoreType.DMA((18,)),
            pltpu.SemaphoreType.DMA((288,)),
            pltpu.SemaphoreType.DMA((288,)),
        ],
        compiler_params=pltpu.CompilerParams(
            vmem_limit_bytes=60 * 1024 * 1024, collective_id=0, has_side_effects=True
        ),
        name="step",
    )(x, enc, dec, enc_bias, dec_bias, mask, sq)


def weights_kernel(scale, units, count, xs, es, feats, grads, dec, inv_norm, grad_enc, grad_dec, acc_e, acc_d, tot):
    slabs, block = grad_enc.shape[0], grad_enc.shape[2]
    for slab in range(slabs):
        at = pl.ds(slab * block, block)
        acc_e[...] = jnp.zeros_like(acc_e)
        acc_d[...] = jnp.zeros_like(acc_d)
        tot[...] = jnp.zeros_like(tot)

        def pair(i, carry, slab=slab, at=at):
            ids = [units[slab * 2 * MOST + i * QUAD + n] for n in range(QUAD)]
            f = jnp.concatenate([feats[n, :, at] for n in ids], axis=0)
            g = jnp.concatenate([grads[n, :, at] for n in ids], axis=0)
            a = jnp.concatenate([xs[n] for n in ids], axis=0)
            e = jnp.concatenate([es[n] for n in ids], axis=0)
            acc_e[...] += lax.dot_general(a, g, TN, preferred_element_type=F32)
            acc_d[...] += lax.dot_general(f, e, TN, preferred_element_type=F32)
            ones = jnp.ones((QUAD * UNIT, 128), BF16)
            tot[...] += lax.dot_general(f, ones, TN, preferred_element_type=F32)
            return carry

        lax.fori_loop(0, lax.div(count[slab] + 1, 2), pair, 0)
        grad_enc[slab] = acc_e[...].astype(grad_enc.dtype)
        col = SPARSITY * tot[:, :1] * inv_norm[at, :]
        grad_dec[at] = (scale * (acc_d[...] + col * f32(dec[at]))).astype(grad_dec.dtype)


def weights(scale, units, count, xs, es, feats, grads, dec, inv_norm, models, slabs):
    width, depth = dec.shape
    cols = 512
    block = width // slabs
    per = depth // models // cols

    def whole(a):
        return pl.BlockSpec(a.shape, lambda c, *_: (0,) * a.ndim)

    def wide(rank):
        return lambda c, *_: (0,) * (rank - 1) + (c,)

    return pl.pallas_call(
        functools.partial(weights_kernel, scale),
        out_shape=[
            jax.ShapeDtypeStruct((slabs, depth, block), BF16),
            jax.ShapeDtypeStruct((width, depth), BF16),
        ],
        grid_spec=pltpu.PrefetchScalarGridSpec(
            num_scalar_prefetch=2,
            grid=(depth // cols,),
            in_specs=[
                pl.BlockSpec(xs.shape[:2] + (cols,), wide(3)),
                pl.BlockSpec(es.shape[:2] + (cols,), wide(3)),
                whole(feats),
                whole(grads),
                pl.BlockSpec((width, cols), wide(2)),
                pl.BlockSpec((None, width, 1), lambda c, *_: (lax.div(c, per), 0, 0)),
            ],
            out_specs=[
                pl.BlockSpec((slabs, cols, block), lambda c, *_: (0, c, 0)),
                pl.BlockSpec((width, cols), wide(2)),
            ],
            scratch_shapes=[
                pltpu.VMEM((cols, block), F32),
                pltpu.VMEM((block, cols), F32),
                pltpu.VMEM((block, 128), F32),
            ],
        ),
        compiler_params=pltpu.CompilerParams(vmem_limit_bytes=56 * 1024 * 1024),
        name="weights",
    )(units, count, xs, es, feats, grads, dec, inv_norm)


def unit_lists(is_active):
    tiles = is_active.shape[0]
    ids = jnp.arange(tiles, dtype=jnp.int32)
    before = (ids[:, None] > ids[None, :]).astype(jnp.int32)
    rank = jnp.sum(before[:, :, None] * is_active[None], axis=1)
    places = jnp.arange(MOST, dtype=jnp.int32)
    picked = (is_active[:, :, None] == 1) & (rank[:, :, None] == places)
    idle = jnp.min(jnp.where(is_active == 0, ids[:, None], tiles - 1), axis=0)
    count = jnp.sum(is_active, axis=0)
    tile = jnp.sum(jnp.where(picked, ids[:, None, None], 0), axis=0)
    tile = jnp.where(places[None, :] < count[:, None], tile, idle[:, None])
    x, y = plane()
    tx, ty = tile % SIDE, tile // SIDE
    one = ((x - tx) % SIDE) * 2 * SIDE + ty
    two = ((y - ty) % SIDE) * 2 * SIDE + SIDE + tx
    return jnp.stack([one, two], axis=2).reshape(-1), count


def on_device(activations, enc_weight, enc_bias, dec_weight, dec_bias, active):
    slabs, models, depth, block = enc_weight.shape
    rows, tiles = activations.shape[0], active.shape[0]
    width = slabs * block
    scale = 1.0 / math.sqrt(MOST * TILE)
    ids = lax.axis_index("lat") * slabs + jnp.arange(slabs, dtype=jnp.int32)
    is_active = jnp.any(active[:, :, None] == ids[None, None, :], axis=1).astype(jnp.int32)
    mask = jnp.broadcast_to(is_active.astype(F32)[:, None, :, None], (tiles, 1, slabs, block))
    mask = mask.reshape(tiles, 1, width)
    units, count = unit_lists(is_active)
    x = activations.reshape(2, rows // 2, models * depth)
    dec = dec_weight.reshape(width, models * depth)
    sq = jnp.stack(
        [jnp.sum(jnp.square(dec[:, m * depth : (m + 1) * depth].astype(F32)), axis=1) for m in range(models)]
    )
    enc = enc_weight.reshape(slabs, models * depth, block)
    xs, es, feats, grads, sq_sum = step(
        scale, x, enc, dec, enc_bias.reshape(1, width), dec_bias.reshape(1, models * depth), mask, sq
    )
    inv_norm = (1.0 / jnp.sqrt(sq_sum + NORM_EPSILON))[:, :, None]
    flat = (2 * tiles, UNIT)
    grad_enc, grad_dec = weights(
        scale,
        units,
        count,
        xs.reshape(flat + (models * depth,)),
        es.reshape(flat + (models * depth,)),
        feats.reshape(flat + (width,)),
        grads.reshape(flat + (width,)),
        dec,
        inv_norm,
        models,
        slabs,
    )
    grad_enc_bias = jnp.sum(grads.astype(F32), axis=(0, 1, 2))
    grad_dec_bias = scale * jnp.sum(es.astype(F32), axis=(0, 1, 2))
    return (
        grad_enc.reshape(enc_weight.shape),
        grad_enc_bias.reshape(slabs, block),
        grad_dec.reshape(dec_weight.shape),
        grad_dec_bias.reshape(models, depth),
    )


def solution(mesh):
    placed = (
        P("lat", None, "tok"),
        P("lat", None, "tok", None),
        P("lat", None),
        P("lat", None, None, "tok"),
        P(None, "tok"),
        P(),
    )
    return jax.shard_map(
        on_device,
        mesh=mesh,
        in_specs=placed,
        out_specs=(
            P("lat", None, "tok", None),
            P("lat", None),
            P("lat", None, None, "tok"),
            P(None, "tok"),
        ),
        check_vma=False,
    )
```

time: 373 us -> 323 us (0.87)
  local copies, waits for them, and re-layouts: 69 us -> 20.3 us
  Pallas kernels: 252 us -> 287 us
  matrix products: 28.8 us -> 0 us
  other arithmetic: 16.5 us -> 11.3 us
    pallas_call x2, Pallas kernels: 252 us -> 287 us  [the longest x1 263 us: step(): pl.pallas_call(functools.partial(step_kernel, scale), out_shape=[rows, ro...]
    dot_general x2 -> x0, matrix products: 28.8 us -> none  [the longest x1 14.5 us: on_device(): jnp.einsum('rj,rmd->jmd', feats, es, preferred_element_type=F32)]
    reshape x3, local copies, waits for them, and re-layouts: 36.8 us -> 9.25 us  [the longest x1 8 us: on_device(): grad_dec.reshape(dec_weight.shape)]
    unnamed x11 -> x13, local copies, waits for them, and re-layouts: 20.2 us -> 6.82 us
    convert_element_type x2 -> x1, local copies, waits for them, and re-layouts: 7.02 us -> 0.08 us  [on_device(): is_active.astype(F32)[:, None, :, None]]
    reduce_sum x4 -> x6, other arithmetic: 14.9 us -> 8.94 us  [the longest x1 4.73 us: on_device(): grad_dec_bias = scale * jnp.sum(es.astype(F32), axis=(0, 1, 2))]
where the time goes in v3:
time: 323 us; the launch traced here: 319 us
  Pallas kernels  287 us (89%)
  local copies, waits for them, and re-layouts  20.3 us (6%)
  other arithmetic  11.3 us (3%)
    pallas_call x1, Pallas kernels, step(): pl.pallas_call(functools.partial(step_kernel, scale), out_shape=[rows, ro...  263 us
    pallas_call x1, Pallas kernels, weights(): pl.pallas_call(functools.partial(weights_kernel, scale), out_shape=[jax.S...  23.9 us
    reshape x1, local copies, waits for them, and re-layouts, on_device(): grad_dec.reshape(dec_weight.shape)  8 us
    unnamed x13, local copies, waits for them, and re-layouts  6.82 us

profile of v3, /device:TPU:1, one launch (start us, length us, event | category | flops | bytes accessed | tf_op | source)
XLA Modules:
  0.0 319.0 jit_solution(5630438700202779949)
XLA Ops:
  0.6 0.9 compare_reduce_fusion
  1.6 0.1 multiply_reduce_fusion.2
  1.7 0.2 select_reduce_fusion
  1.9 0.2 convert_reduce_fusion.2
  2.0 0.0 copy-start.4
  2.0 0.1 fusion.4
  2.2 0.1 copy.13
  2.3 0.6 reshape.346.units
  2.9 3.6 %copy.16 = bf16[128,8,2,1024]{3,1,2,0:T(8,128)(2,1)S(1)} copy(bf16[128,8,2,1024]{3,2,1,0:T(2,128)(2,1)} %bitcast.43) | data formatting | bytes 8388608
  6.5 0.0 copy-done.4
  6.5 0.0 copy-start
  6.5 0.0 copy-start.1
  6.6 0.0 copy-start.2
  6.6 0.0 copy-start.3
  6.6 2.0 copy-done
  8.6 0.9 multiply_reduce_fusion.1
  9.4 0.6 pad_maximum_fusion.sq
  10.0 0.1 copy.14
  10.1 0.1 broadcast_in_dim.62
  10.2 0.7 broadcast_in_dim.63.mask
  10.9 0.0 copy-done.1
  10.9 1.2 reshape.347.x
  12.1 0.0 copy-done.2
  12.1 0.6 copy.18
  12.7 0.0 copy-done.3
  12.7 0.6 copy.17
  13.3 262.7 %step.1 = (bf16[4,8,64,2048]{3,2,1,0:T(8,128)(2,1)}, bf16[4,8,64,2048]{3,2,1,0:T(8,128)(2,1)}, bf16[4,8,64,1024]{3,2,1,0:T(8,128)(2,1)}, bf16[4,8,64,1024]{3,2,1,0:T(8,128)(2,1)}, f32[2,1024]{1,0:T(2,128)}) custom-call(bf16[2,64,2048]{2,1,0:T(8,128)(2,1)} %reshape.347.x, bf16[4,2048,256]{2,1,0:T(8,128)(2,1)} %bitcast.44, bf16[1024,2048]{1,0:T(8,128)(2,1)} %bitcast.38, ...), custom_call_target="tpu_custom_call" | custom-call | tf_op jit(solution)/shard_map/step/pallas_call | solution.py:613
  276.1 0.7 rsqrt_bitcast_fusion
  276.8 1.4 copy.15.inv_norm
  278.2 23.9 %weights.1 = (bf16[4,2048,256]{2,1,0:T(8,128)(2,1)}, bf16[1024,2048]{1,0:T(8,128)(2,1)}) custom-call(s32[64]{0:T(128)} %reshape.346.units, s32[4]{0:T(128)} %copy-done.4, bf16[32,64,2048]{2,1,0:T(8,128)(2,1)} %bitcast.42, bf16[32,64,2048]{2,1,0:T(8,128)(2,1)} %bitcast.40, bf16[32,64,1024]{2,1,0:T(8,128)(2,1)} %bitcast.45, bf16[32,64,1024]{2,1,0:T(8,128)(2,1)} %bitcast.41, ...), custom_call_target="tpu_custom_call" | custom-call | tf_op jit(solution)/shard_map/weights/pallas_call | solution.py:683
  302.1 8.0 %reshape.358 = bf16[4,256,2,1024]{3,2,1,0:T(2,128)(2,1)} reshape(bf16[1024,2048]{1,0:T(8,128)(2,1)} %get-tuple-element.17) | data formatting | bytes 8388608 | tf_op jit(solution)/shard_map/reshape | solution.py:772
  310.1 4.7 %convert_reduce_fusion = f32[2048]{0:T(1024)S(1)} fusion(bf16[4,8,64,2048]{3,2,1,0:T(8,128)(2,1)} %get-tuple-element.12), kind=kLoop, calls=%fused_computation | loop fusion | flops 8386560 | bytes 8396800 | tf_op jit(solution)/shard_map/reduce_sum | solution.py:768
  314.9 0.6 mul.59
  315.5 2.9 convert_reduce_fusion.1
  318.4 0.6 reshape.357
  (5 shorter events, 0.0 us)
Async XLA Ops:
  2.0 4.5 %copy-start.4 = (s32[4]{0:T(128)}, s32[4]{0:T(128)S(1)}, u32[]{:S(2)}) copy-start(s32[4]{0:T(128)S(1)} %get-tuple-element.20.count) | copy-start | bytes 52
  6.5 2.0 copy-start
  6.5 4.4 %copy-start.1 = (bf16[128,2,1024]{2,1,0:T(2,128)(2,1)S(1)}, bf16[128,2,1024]{2,1,0:T(2,128)(2,1)}, u32[]{:S(2)}) copy-start(bf16[128,2,1024]{2,1,0:T(2,128)(2,1)} %param.6) | copy-start | bytes 1572868
  6.6 5.6 %copy-start.2 = (f32[2,1024]{1,0:T(2,128)S(1)}, f32[2,1024]{1,0:T(2,128)}, u32[]{:S(2)}) copy-start(f32[2,1024]{1,0:T(2,128)} %param.10) | copy-start | bytes 24580
  6.6 6.2 %copy-start.3 = (f32[4,256]{1,0:T(4,128)S(1)}, f32[4,256]{1,0:T(4,128)}, u32[]{:S(2)}) copy-start(f32[4,256]{1,0:T(4,128)} %param.8) | copy-start | bytes 12292

commit v4 on v3

v4 whole, which is shorter than its diff:
```python
import functools
import math

import jax
import jax.numpy as jnp
from jax import lax
from jax.experimental import pallas as pl
from jax.experimental.pallas import tpu as pltpu
from jax.sharding import PartitionSpec as P

MOST = 8
TILE = 128
SPARSITY = 0.25
NORM_EPSILON = 1e-06
MESH = pl.DeviceIdType.MESH
SIDE = 4
UNIT = TILE // 2
PIECE = UNIT // 2
HALF = PIECE // 2
PIECES = (0, 1)
SLOTS = 4
DIRS = (1, -1)
ORDER = tuple((k, e) for k in (0, 1, 3, 2) for e in PIECES)
BF16, F32 = jnp.bfloat16, jnp.float32
NT = (((1,), (1,)), ((), ()))
TN = (((0,), (0,)), ((), ()))


def ring(i, step):
    return lax.rem(i + step + SIDE, SIDE)


def lat_peer(y, x):
    return {"lat": y * SIDE + x}


def tok_peer(z, core):
    return {"tok": z * 2 + core}


def plane():
    lat = lax.axis_index("lat")
    return lax.rem(lat, SIDE), lax.div(lat, SIDE)


def column():
    tok = lax.axis_index("tok")
    return lax.div(tok, 2), lax.rem(tok, 2)


def greet():
    x, y = plane()
    z, core = column()
    peers = [lat_peer(y, ring(x, d)) for d in DIRS] + [lat_peer(ring(y, d), x) for d in DIRS]
    peers += [tok_peer(ring(z, d), core) for d in DIRS] + [tok_peer(z, 1 - core)]
    barrier = pltpu.get_barrier_semaphore()
    for peer in peers:
        pl.semaphore_signal(barrier, inc=1, device_id=peer, device_id_type=MESH)
    pl.semaphore_wait(barrier, len(peers))


def s(d):
    return 0 if d == 1 else 1


def rows_of(d, e=0):
    return pl.ds(e * PIECE + (0 if d == 1 else HALF), HALF)


def piece(e):
    return pl.ds(e * PIECE, PIECE)


def f32(v):
    return v.astype(F32)


class Wires:
    def __init__(self, send, recv):
        self.send, self.recv = send, recv
        self.numbers, self.started = {}, []

    def copy(self, key, src, dst, peer):
        n = self.numbers.setdefault(key, len(self.numbers))
        return pltpu.make_async_remote_copy(
            src_ref=src,
            dst_ref=dst,
            send_sem=self.send.at[n],
            recv_sem=self.recv.at[n],
            device_id=peer,
            device_id_type=MESH,
        )

    def go(self, copy, source=None):
        copy.start()
        self.started.append((source, copy))

    def settle(self, source):
        for name, copy in self.started:
            if name == source:
                copy.wait_send()
        self.started = [item for item in self.started if item[0] != source]

    def drain(self):
        for _, copy in self.started:
            copy.wait_send()
        self.started = []


FLOWS = (0, 1)
FWD, MID, BWD = range(3)
SEND, CROSS, NEAR, FAR, RELAY, WORK, TOK, NORM, BEGIN, REDUCE, JOIN, FINISH = range(12)
SCRIPT = (
    (FWD, SEND, 0, 0), (FWD, CROSS, 0), (FWD, SEND, 0, 1), (FWD, RELAY, 0, 0), (FWD, NEAR, 0),
    (FWD, CROSS, 1), (FWD, RELAY, 0, 1), (FWD, WORK, 0, 0), (FWD, TOK, 0, 0, 1), (FWD, NORM, 0),
    (FWD, FAR, 0), (FWD, SEND, 1, 0), (FWD, NEAR, 1), (FWD, TOK, 0, 0, 2), (FWD, WORK, 0, 1),
    (FWD, TOK, 0, 1, 1), (FWD, SEND, 1, 1), (FWD, TOK, 0, 0, 3), (FWD, RELAY, 1, 0), (FWD, FAR, 1),
    (FWD, TOK, 0, 1, 2), (FWD, TOK, 0, 0, 4), (FWD, SEND, 3, 0), (FWD, RELAY, 1, 1),
    (FWD, TOK, 0, 1, 3), (FWD, WORK, 1, 0), (FWD, NORM, 1), (FWD, TOK, 1, 0, 1), (FWD, SEND, 3, 1),
    (FWD, TOK, 0, 0, 5), (FWD, RELAY, 3, 0), (FWD, TOK, 0, 1, 4), (FWD, WORK, 1, 1),
    (FWD, TOK, 0, 0, 6), (FWD, TOK, 1, 0, 2), (FWD, TOK, 1, 1, 1), (FWD, SEND, 2, 0),
    (FWD, RELAY, 3, 1), (FWD, TOK, 0, 0, 7), (FWD, TOK, 0, 1, 5), (FWD, WORK, 3, 0), (FWD, NORM, 2),
    (FWD, TOK, 1, 0, 3), (FWD, TOK, 3, 0, 1), (FWD, TOK, 1, 1, 2), (FWD, SEND, 2, 1),
    (FWD, RELAY, 2, 0), (FWD, TOK, 0, 1, 6), (FWD, WORK, 3, 1), (FWD, TOK, 0, 1, 7),
    (FWD, TOK, 1, 0, 4), (FWD, TOK, 1, 1, 3), (FWD, TOK, 3, 0, 2), (FWD, TOK, 3, 1, 1),
    (FWD, RELAY, 2, 1), (FWD, TOK, 1, 0, 5), (FWD, WORK, 2, 0), (FWD, TOK, 2, 0, 1),
    (FWD, TOK, 1, 1, 4), (FWD, TOK, 3, 1, 2), (FWD, TOK, 3, 0, 3), (FWD, TOK, 2, 0, 2),
    (FWD, TOK, 1, 0, 6), (FWD, TOK, 1, 1, 5), (FWD, WORK, 2, 1), (FWD, TOK, 1, 0, 7),
    (FWD, TOK, 3, 1, 3), (FWD, TOK, 2, 1, 1), (MID, BEGIN, 0, 0), (MID, BEGIN, 0, 1),
    (FWD, TOK, 3, 0, 4), (FWD, TOK, 2, 1, 2), (FWD, TOK, 2, 0, 3), (MID, RELAY, 0, 0),
    (MID, BEGIN, 1, 0), (FWD, TOK, 1, 1, 6), (FWD, TOK, 3, 1, 4), (MID, RELAY, 0, 1),
    (FWD, TOK, 3, 0, 5), (FWD, TOK, 1, 1, 7), (MID, BEGIN, 1, 1), (FWD, TOK, 2, 1, 3),
    (MID, REDUCE, 0, 0), (MID, RELAY, 1, 0), (FWD, TOK, 2, 0, 4), (FWD, TOK, 3, 1, 5),
    (MID, REDUCE, 0, 1), (FWD, TOK, 3, 0, 6), (MID, RELAY, 1, 1), (FWD, TOK, 2, 1, 4),
    (FWD, TOK, 3, 0, 7), (MID, BEGIN, 3, 0), (FWD, TOK, 3, 1, 6), (FWD, TOK, 2, 0, 5),
    (MID, REDUCE, 1, 0), (FWD, TOK, 2, 1, 5), (MID, REDUCE, 1, 1), (FWD, TOK, 3, 1, 7),
    (MID, BEGIN, 3, 1), (FWD, TOK, 2, 0, 6), (FWD, TOK, 2, 1, 6), (MID, RELAY, 3, 0),
    (FWD, TOK, 2, 0, 7), (MID, BEGIN, 2, 0), (FWD, TOK, 2, 1, 7), (MID, BEGIN, 2, 1),
    (MID, RELAY, 3, 1), (MID, REDUCE, 3, 0), (MID, RELAY, 2, 0), (MID, RELAY, 2, 1),
    (MID, REDUCE, 3, 1), (MID, REDUCE, 2, 0), (MID, REDUCE, 2, 1), (MID, JOIN, 0), (MID, JOIN, 1),
    (MID, FINISH, 0), (MID, FINISH, 1), (BWD, SEND, 0, 0), (BWD, CROSS, 0), (BWD, SEND, 0, 1),
    (BWD, RELAY, 0, 0), (BWD, NEAR, 0), (BWD, CROSS, 1), (BWD, RELAY, 0, 1), (BWD, WORK, 0, 0),
    (BWD, TOK, 0, 0, 1), (BWD, FAR, 0), (BWD, SEND, 1, 0), (BWD, TOK, 0, 0, 2), (BWD, NEAR, 1),
    (BWD, WORK, 0, 1), (BWD, TOK, 0, 0, 3), (BWD, TOK, 0, 1, 1), (BWD, SEND, 1, 1),
    (BWD, RELAY, 1, 0), (BWD, TOK, 0, 0, 4), (BWD, TOK, 0, 1, 2), (BWD, FAR, 1), (BWD, SEND, 3, 0),
    (BWD, TOK, 0, 0, 5), (BWD, RELAY, 1, 1), (BWD, TOK, 0, 1, 3), (BWD, WORK, 1, 0),
    (BWD, TOK, 0, 0, 6), (BWD, TOK, 1, 0, 1), (BWD, TOK, 0, 1, 4), (BWD, SEND, 3, 1),
    (BWD, RELAY, 3, 0), (BWD, TOK, 0, 0, 7), (BWD, TOK, 1, 0, 2), (BWD, WORK, 1, 1),
    (BWD, TOK, 0, 1, 5), (BWD, TOK, 1, 1, 1), (BWD, SEND, 2, 0), (BWD, TOK, 1, 0, 3),
    (BWD, RELAY, 3, 1), (BWD, TOK, 0, 1, 6), (BWD, WORK, 3, 0), (BWD, TOK, 1, 0, 4),
    (BWD, TOK, 1, 1, 2), (BWD, TOK, 0, 1, 7), (BWD, TOK, 3, 0, 1), (BWD, SEND, 2, 1),
    (BWD, RELAY, 2, 0), (BWD, WORK, 3, 1), (BWD, TOK, 1, 0, 5), (BWD, TOK, 1, 1, 3),
    (BWD, TOK, 3, 0, 2), (BWD, TOK, 3, 1, 1), (BWD, RELAY, 2, 1), (BWD, TOK, 1, 0, 6),
    (BWD, TOK, 1, 1, 4), (BWD, WORK, 2, 0), (BWD, TOK, 1, 0, 7), (BWD, TOK, 3, 0, 3),
    (BWD, TOK, 3, 1, 2), (BWD, TOK, 2, 0, 1), (BWD, TOK, 1, 1, 5), (BWD, WORK, 2, 1),
    (BWD, TOK, 3, 0, 4), (BWD, TOK, 3, 1, 3), (BWD, TOK, 2, 0, 2), (BWD, TOK, 2, 1, 1),
    (BWD, TOK, 1, 1, 6), (BWD, TOK, 3, 0, 5), (BWD, TOK, 3, 1, 4), (BWD, TOK, 2, 1, 2),
    (BWD, TOK, 1, 1, 7), (BWD, TOK, 2, 0, 3), (BWD, TOK, 3, 0, 6), (BWD, TOK, 3, 1, 5),
    (BWD, TOK, 3, 0, 7), (BWD, TOK, 2, 1, 3), (BWD, TOK, 2, 0, 4), (BWD, TOK, 3, 1, 6),
    (BWD, TOK, 2, 1, 4), (BWD, TOK, 3, 1, 7), (BWD, TOK, 2, 0, 5), (BWD, TOK, 2, 1, 5),
    (BWD, TOK, 2, 0, 6), (BWD, TOK, 2, 1, 6), (BWD, TOK, 2, 0, 7), (BWD, TOK, 2, 1, 7),
)


class Flow:
    def __init__(self, h):
        x, y = plane()
        self.h = h
        self.p, self.q = (x, y) if h == 0 else (y, x)

    def near(self, dp, dq):
        p, q = ring(self.p, dp), ring(self.q, dq)
        return lat_peer(q, p) if self.h == 0 else lat_peer(p, q)

    def unit(self, dq):
        return self.h * SIDE + ring(self.q, dq)


class Gather:
    def __init__(self, wires, flows, tag, own, held):
        self.wires, self.flows, self.tag, self.own, self.held = wires, flows, tag, own, held

    def p1(self, f, e, d):
        dst = self.held.at[1 if d == 1 else 3, f.unit(0), piece(e)]
        return self.wires.copy(("p1", f.h, e, d), self.own(f.h, e), dst, f.near(d, 0))

    def p1half(self, f, e, d):
        src = self.held.at[1 if d == 1 else 3, f.unit(0), rows_of(d, e)]
        dst = self.held.at[2, f.unit(0), rows_of(d, e)]
        return self.wires.copy(("p1half", f.h, e, d), src, dst, f.near(d, 0))

    def p2(self, f, k, e, d):
        at = self.held.at[k, f.unit(0), piece(e)]
        return self.wires.copy(("p2", f.h, k, e, d), self.own(f.h, e) if k == 0 else at, at, f.near(0, d))

    def p2half(self, f, k, e, d):
        at = self.held.at[k, f.unit(-d), rows_of(d, e)]
        return self.wires.copy(("p2half", f.h, k, e, d), at, at, f.near(0, d))

    def name(self, k):
        return (self.tag, k)

    def each(self, make, *where):
        for f in self.flows:
            for d in DIRS:
                yield make(f, *where, d)

    def send(self, k, e):
        for copy in self.each(self.p2, k, e):
            self.wires.go(copy, self.name(k))

    def cross(self, e):
        for copy in self.each(self.p1, e):
            self.wires.go(copy, self.name(0))

    def near(self, e):
        for copy in self.each(self.p1, e):
            copy.wait_recv()
        for f in self.flows:
            for d, k in ((1, 1), (-1, 3)):
                self.wires.go(self.p1half(f, e, d), self.name(k))

    def far(self, e):
        for copy in self.each(self.p1half, e):
            copy.wait_recv()

    def relay(self, k, e):
        for f in self.flows:
            for d in DIRS:
                self.p2(f, k, e, d).wait_recv()
                self.wires.go(self.p2half(f, k, e, d), self.name(k))

    def complete(self, k, e):
        for copy in self.each(self.p2half, k, e):
            copy.wait_recv()


def tok_flow(wires, tag, k, e, part, out, r1, s1, r2, r3, epilogue):
    n = ORDER.index((k, e)) % SLOTS
    z, core = column()
    other = tok_peer(z, 1 - core)
    me = core * SIDE + z
    source = (tag, k, e)

    def peer(d):
        return tok_peer(ring(z, d), core)

    def swap(j):
        at = ring(z, j)
        return wires.copy(("tok", k, e, 0, j), part.at[n, (1 - core) * SIDE + at], r1.at[n, j], other)

    def far(d):
        return wires.copy(("tok", k, e, 1, d), s1.at[n, 2, rows_of(d)], r2.at[n, s(d)], peer(d))

    def plain(d):
        src = s1.at[n, 1 if d == 1 else 3, rows_of(-d)]
        return wires.copy(("tok", k, e, 2, d), src, r3.at[n, s(d), rows_of(-d)], peer(d))

    def summed(d):
        src = s1.at[n, 1 if d == 1 else 3, rows_of(d)]
        return wires.copy(("tok", k, e, 3, d), src, r3.at[n, s(d), rows_of(d)], peer(d))

    def spread(d):
        at = out.at[k, me, piece(e)]
        return wires.copy(("tok", k, e, 4, d), at, at, peer(d))

    def forward(d):
        at = out.at[k, core * SIDE + ring(z, -d), rows_of(d, e)]
        return wires.copy(("tok", k, e, 5, d), at, at, peer(d))

    def hand(j):
        at = out.at[k, core * SIDE + ring(z, j), piece(e)]
        return wires.copy(("tok", k, e, 6, j), at, at, other)

    def first(j):
        swap(j).wait_recv()
        at = core * SIDE + ring(z, j)
        s1[n, j] = (f32(part[n, at]) + f32(r1[n, j])).astype(s1.dtype)

    for j in (2, 1, 3, 0):
        wires.go(swap(j), source)
    yield
    first(2)
    for d in DIRS:
        wires.go(far(d), source)
    for d in DIRS:
        first(1 if d == 1 else 3)
        wires.go(plain(d), source)
    first(0)
    yield
    for d in DIRS:
        far(d).wait_recv()
        j = 1 if d == 1 else 3
        s1[n, j, rows_of(d)] = (f32(s1[n, j, rows_of(d)]) + f32(r2[n, s(d)])).astype(s1.dtype)
        wires.go(summed(d), source)
    yield
    for d in DIRS:
        plain(d).wait_recv()
        summed(d).wait_recv()
    total = f32(s1[n, 0]) + f32(r3[n, 0]) + f32(r3[n, 1])
    out[k, me, piece(e)] = epilogue(k, e, me, total).astype(out.dtype)
    for d in DIRS:
        wires.go(spread(d))
    wires.go(hand(0))
    yield
    for d in DIRS:
        spread(d).wait_recv()
        wires.go(forward(d))
        wires.go(hand(3 if d == 1 else 1))
    hand(0).wait_recv()
    wires.settle(source)
    yield
    for d in DIRS:
        forward(d).wait_recv()
    wires.go(hand(2))
    yield
    for j in range(1, SIDE):
        hand(j).wait_recv()
    yield


def tok_buffers(dtype, width):
    return [
        pltpu.VMEM((SLOTS, 2 * SIDE, PIECE, width), dtype),
        pltpu.VMEM((SLOTS, SIDE, PIECE, width), dtype),
        pltpu.VMEM((SLOTS, SIDE, PIECE, width), dtype),
        pltpu.VMEM((SLOTS, 2, HALF, width), dtype),
        pltpu.VMEM((SLOTS, 2, PIECE, width), dtype),
    ]


def blocks(count, body):
    def step(i, carry):
        body(i)
        return carry

    lax.fori_loop(0, count, step, 0)


def own_tile(k):
    x, y = plane()
    z, core = column()
    return (1 - core) * (z * SIDE + ring(x, -k)) + core * (ring(y, -k) * SIDE + z)


ALL = 2 * SIDE * PIECE


def step_kernel(
    scale,
    x,
    enc_in,
    dec_in,
    enc_bias,
    dec_bias,
    mask,
    sq,
    xs,
    es,
    feat_out,
    grad_out,
    sq_sum,
    enc,
    dec,
    held,
    err,
    feats,
    grads,
    r1,
    r2,
    r4,
    r5,
    norm,
    sq_a,
    sq_b,
    *rest,
):
    fwd, bwd, (local, send, recv) = rest[:5], rest[5:10], rest[10:]
    wires = Wires(send, recv)
    z, core = column()
    flows = [Flow(h) for h in FLOWS]
    slab_count, depth, block = enc.shape
    width = dec.shape[0]
    cols = 512
    loads = [
        pltpu.make_async_copy(enc_in, enc, local.at[18]),
        pltpu.make_async_copy(dec_in, dec, local.at[19]),
    ]
    keep = [pltpu.make_async_copy(x.at[f.h], held.at[0, f.unit(0)], local.at[f.h]) for f in flows]
    saves = {}

    def save(name, k, src, dst):
        n = 2 + len(saves)
        saves[name, k] = pltpu.make_async_copy(src.at[k], dst.at[k], local.at[n])
        saves[name, k].start()

    for copy in keep:
        copy.start()
    for copy in loads:
        copy.start()
    greet()


    def feature(k, e, me, total):
        live = mask[own_tile(k)] > 0.0
        return jnp.where(live, jnp.maximum(total + enc_bias[...], 0.0), 0.0)

    def encode(k, e):
        n = ORDER.index((k, e)) % SLOTS
        if (k, e) == ORDER[0]:
            for copy in keep + loads:
                copy.wait()

        def step(slab):
            rows = held[k, :, piece(e)].reshape(ALL, depth)
            at = pl.ds(pl.multiple_of(slab * block, block), block)
            value = jnp.dot(rows, enc[slab], preferred_element_type=F32)
            fwd[0][n, :, :, at] = value.reshape(2 * SIDE, PIECE, block)

        blocks(slab_count, step)
        if e == PIECES[-1]:
            save("x", k, held, xs)

    swap = wires.copy("sq", sq, sq_a.at[0], tok_peer(z, 1 - core))
    turns = [wires.copy(("sq", d), sq_b.at[0], sq_b.at[1 + s(d)], tok_peer(ring(z, d), core)) for d in DIRS]
    turn_on = wires.copy(("sq", 2), sq_b.at[1], sq_b.at[3], tok_peer(ring(z, 1), core))

    def norms(stage):
        if stage == 0:
            swap.wait_recv()
            sq_b[0] = sq[...] + sq_a[0]
            for copy in turns:
                wires.go(copy)
        elif stage == 1:
            for copy in turns:
                copy.wait_recv()
            wires.go(turn_on)
        else:
            turn_on.wait_recv()
            total = (sq_b[0] + sq_b[3]) + (sq_b[1] + sq_b[2])
            sq_sum[...] = total
            norm[...] = jnp.sum(jnp.sqrt(total + NORM_EPSILON), axis=0, keepdims=True)

    wires.go(swap)


    def decode(k, e):
        if e == PIECES[0]:
            wires.settle(front.name(k))
            saves["x", k].wait()

        def step(col):
            at = pl.ds(pl.multiple_of(col * cols, cols), cols)
            f = feats[k, :, piece(e)].reshape(ALL, width)
            value = jnp.dot(f, dec[:, at], preferred_element_type=F32)
            held[k, :, piece(e), at] = value.reshape(2 * SIDE, PIECE, cols).astype(BF16)

        blocks(depth // cols, step)

    def half(d, e):
        return pl.ds(e * HALF, HALF)

    def far(f, k, e, d):
        src = held.at[k, f.unit(2), rows_of(d, e)]
        return wires.copy((0, f.h, k, e, d), src, r1.at[f.h, k, s(d), half(d, e)], f.near(0, d))

    def plain(f, k, e, d):
        src = held.at[k, f.unit(d), rows_of(-d, e)]
        return wires.copy((1, f.h, k, e, d), src, r2.at[f.h, k, s(d), rows_of(-d, e)], f.near(0, d))

    def summed(f, k, e, d):
        src = held.at[k, f.unit(d), rows_of(d, e)]
        return wires.copy((2, f.h, k, e, d), src, r2.at[f.h, k, s(d), rows_of(d, e)], f.near(0, d))

    def far2(f, e, d):
        src = held.at[2, f.unit(0), rows_of(d, e)]
        return wires.copy((3, f.h, e, d), src, r4.at[f.h, s(d), half(d, e)], f.near(d, 0))

    def plain2(f, e, d):
        src = held.at[3 if d == 1 else 1, f.unit(0), rows_of(-d, e)]
        return wires.copy((4, f.h, e, d), src, r5.at[f.h, s(d), rows_of(-d, e)], f.near(d, 0))

    def summed2(f, e, d):
        src = held.at[3 if d == 1 else 1, f.unit(0), rows_of(d, e)]
        return wires.copy((5, f.h, e, d), src, r5.at[f.h, s(d), rows_of(d, e)], f.near(d, 0))

    def reduce_begin(k, e):
        decode(k, e)
        for make in (far, plain):
            for f in flows:
                for d in DIRS:
                    wires.go(make(f, k, e, d))

    def reduce_relay(k, e):
        for f in flows:
            for d in DIRS:
                far(f, k, e, d).wait_recv()
                at = (k, f.unit(d), rows_of(d, e))
                held[at] = (f32(held[at]) + f32(r1[f.h, k, s(d), half(d, e)])).astype(BF16)
                wires.go(summed(f, k, e, d))

    def reduce(k, e):
        for f in flows:
            for d in DIRS:
                plain(f, k, e, d).wait_recv()
                summed(f, k, e, d).wait_recv()
            at = (k, f.unit(0), piece(e))
            total = f32(held[at]) + f32(r2[f.h, k, 0, piece(e)]) + f32(r2[f.h, k, 1, piece(e)])
            held[at] = total.astype(BF16)
            if k == 2:
                for d in DIRS:
                    wires.go(far2(f, e, d))
            elif k != 0:
                wires.go(plain2(f, e, 1 if k == 3 else -1))

    def reduce_far(e):
        for f in flows:
            for d in DIRS:
                far2(f, e, d).wait_recv()
                at = (3 if d == 1 else 1, f.unit(0), rows_of(d, e))
                held[at] = (f32(held[at]) + f32(r4[f.h, s(d), half(d, e)])).astype(BF16)
                wires.go(summed2(f, e, d))

    def finish(e):
        for f in flows:
            for d in DIRS:
                plain2(f, e, d).wait_recv()
                summed2(f, e, d).wait_recv()
            at = f.unit(0), piece(e)
            recon = f32(held[(0,) + at]) + f32(r5[f.h, 0, piece(e)]) + f32(r5[f.h, 1, piece(e)]) + dec_bias[...]
            err[(0,) + at] = (recon - f32(x[f.h, piece(e)])).astype(BF16)
        if e == PIECES[-1]:
            wires.drain()


    def project(k, e):
        n = ORDER.index((k, e)) % SLOTS

        def step(slab):
            at = pl.ds(pl.multiple_of(slab * block, block), block)
            rows = err[k, :, piece(e)].reshape(ALL, depth)
            value = lax.dot_general(rows, dec[at], NT, preferred_element_type=F32)
            bwd[0][n, :, :, at] = value.reshape(2 * SIDE, PIECE, block).astype(BF16)

        blocks(slab_count, step)
        if e == PIECES[-1]:
            save("e", k, err, es)

    def pre_grad(k, e, me, total):
        grad = scale * (total + SPARSITY * norm[...])
        return jnp.where(f32(feats[k, me, piece(e)]) > 0.0, grad, 0.0)

    front = Gather(wires, flows, "x", lambda h, e: x.at[h, piece(e)], held)
    back = Gather(wires, flows, "e", lambda h, e: err.at[0, flows[h].unit(0), piece(e)], err)
    toks = {
        FWD: {g: tok_flow(wires, FWD, *g, fwd[0], feats, *fwd[1:], feature) for g in ORDER},
        BWD: {g: tok_flow(wires, BWD, *g, bwd[0], grads, *bwd[1:], pre_grad) for g in ORDER},
    }

    def tok(phase, k, e, number):
        next(toks[phase][k, e])
        if number == 7 and e == PIECES[-1]:
            save(phase, k, *((feats, feat_out) if phase == FWD else (grads, grad_out)))

    steps = {MID: {BEGIN: reduce_begin, RELAY: reduce_relay, REDUCE: reduce, JOIN: reduce_far, FINISH: finish}}
    for phase, g, work in ((FWD, front, encode), (BWD, back, project)):
        steps[phase] = {SEND: g.send, CROSS: g.cross, NEAR: g.near, FAR: g.far, RELAY: g.relay, NORM: norms}
        steps[phase][TOK] = functools.partial(tok, phase)

        def arrive(k, e, g=g, work=work):
            g.complete(k, e)
            work(k, e)

        steps[phase][WORK] = arrive
    for phase, what, *where in SCRIPT:
        steps[phase][what](*where)
    for (name, _), copy in saves.items():
        if name != "x":
            copy.wait()
    wires.drain()


VMEM = pl.BlockSpec(memory_space=pltpu.VMEM)
ANY = pl.BlockSpec(memory_space=pl.ANY)


def step(scale, x, enc, dec, enc_bias, dec_bias, mask, sq):
    width, depth = dec.shape
    units = (SIDE, 2 * SIDE, UNIT)
    rows = jax.ShapeDtypeStruct(units + (depth,), BF16)
    latents = jax.ShapeDtypeStruct(units + (width,), BF16)
    return pl.pallas_call(
        functools.partial(step_kernel, scale),
        out_shape=[rows, rows, latents, latents, jax.ShapeDtypeStruct(sq.shape, F32)],
        in_specs=[VMEM, ANY, ANY] + [VMEM] * 4,
        out_specs=[ANY, ANY, ANY, ANY, VMEM],
        scratch_shapes=[
            pltpu.VMEM(enc.shape, BF16),
            pltpu.VMEM(dec.shape, BF16),
            pltpu.VMEM(units + (depth,), BF16),
            pltpu.VMEM(units + (depth,), BF16),
            pltpu.VMEM(units + (width,), BF16),
            pltpu.VMEM(units + (width,), BF16),
            pltpu.VMEM((2, SIDE, 2, UNIT // 2, depth), BF16),
            pltpu.VMEM((2, SIDE, 2, UNIT, depth), BF16),
            pltpu.VMEM((2, 2, UNIT // 2, depth), BF16),
            pltpu.VMEM((2, 2, UNIT, depth), BF16),
            pltpu.VMEM((1, width), F32),
            pltpu.VMEM((1,) + sq.shape, F32),
            pltpu.VMEM((4,) + sq.shape, F32),
        ]
        + tok_buffers(F32, width)
        + tok_buffers(BF16, width)
        + [
            pltpu.SemaphoreType.DMA((20,)),
            pltpu.SemaphoreType.DMA((348,)),
            pltpu.SemaphoreType.DMA((348,)),
        ],
        compiler_params=pltpu.CompilerParams(
            vmem_limit_bytes=60 * 1024 * 1024, collective_id=0, has_side_effects=True
        ),
        name="step",
    )(x, enc, dec, enc_bias, dec_bias, mask, sq)


QUAD = 4


def weights_kernel(
    scale, units, count, x0, x1, e0, e1, feats, grads, d0, d1, inv_norm, grad_enc, grad_dec, enc_sum, err_sum, acc_e, acc_d, tot, gsum, mixed
):
    slabs, block = grad_enc.shape[0], grad_enc.shape[3]
    for m, err in enumerate((e0, e1)):
        rows = err[...].reshape(-1, err.shape[2])
        ones = jnp.ones((16, rows.shape[0]), BF16)
        total = jnp.dot(ones, rows, preferred_element_type=F32)
        err_sum[pl.ds(m, 1)] = scale * total[:1]
    for slab in range(slabs):
        at = pl.ds(slab * block, block)
        acc_e[...] = jnp.zeros_like(acc_e)
        acc_d[...] = jnp.zeros_like(acc_d)
        tot[...] = jnp.zeros_like(tot)
        gsum[...] = jnp.zeros_like(gsum)

        def pair(i, carry, slab=slab, at=at):
            ids = [units[slab * 2 * MOST + i * QUAD + n] for n in range(QUAD)]
            f = jnp.concatenate([feats[n, :, at] for n in ids], axis=0)
            g = jnp.concatenate([grads[n, :, at] for n in ids], axis=0)
            for m, (acts, err) in enumerate(((x0, e0), (x1, e1))):
                a = jnp.concatenate([acts[n] for n in ids], axis=0)
                e = jnp.concatenate([err[n] for n in ids], axis=0)
                acc_e[m] += lax.dot_general(a, g, TN, preferred_element_type=F32)
                acc_d[m] += lax.dot_general(f, e, TN, preferred_element_type=F32)
            tot[...] += lax.dot_general(f, jnp.ones((QUAD * UNIT, 128), BF16), TN, preferred_element_type=F32)
            gsum[...] += jnp.dot(jnp.ones((16, QUAD * UNIT), BF16), g, preferred_element_type=F32)
            return carry

        lax.fori_loop(0, lax.div(count[slab] + 1, 2), pair, 0)
        enc_sum[:, at] = gsum[:8]
        both = []
        for m, dec in enumerate((d0, d1)):
            grad_enc[slab, m] = acc_e[m].astype(grad_enc.dtype)
            col = SPARSITY * tot[:, :1] * inv_norm[m, at, :]
            both.append(scale * (acc_d[m] + col * f32(dec[at])))
        for m in range(len(both)):
            mixed[:, m, :] = both[m]
        grad_dec[at] = mixed[...].astype(grad_dec.dtype)


def weights(scale, units, count, xs, es, feats, grads, dec, inv_norm, models, slabs):
    width, depth = dec.shape
    cols = 256
    block = width // slabs
    part = depth // models
    steps = part // cols

    def whole(a):
        return pl.BlockSpec(a.shape, lambda c, *_: (0,) * a.ndim)

    def wide(a, m):
        return pl.BlockSpec(a.shape[:-1] + (cols,), lambda c, *_: (0,) * (a.ndim - 1) + (c + m * steps,))

    return pl.pallas_call(
        functools.partial(weights_kernel, scale),
        out_shape=[
            jax.ShapeDtypeStruct((slabs, models, part, block), BF16),
            jax.ShapeDtypeStruct((width, models, part), BF16),
            jax.ShapeDtypeStruct((8, width), F32),
            jax.ShapeDtypeStruct((models, part), F32),
        ],
        grid_spec=pltpu.PrefetchScalarGridSpec(
            num_scalar_prefetch=2,
            grid=(steps,),
            in_specs=[
                wide(xs, 0),
                wide(xs, 1),
                wide(es, 0),
                wide(es, 1),
                whole(feats),
                whole(grads),
                wide(dec, 0),
                wide(dec, 1),
                whole(inv_norm),
            ],
            out_specs=[
                pl.BlockSpec((slabs, models, cols, block), lambda c, *_: (0, 0, c, 0)),
                pl.BlockSpec((width, models, cols), lambda c, *_: (0, 0, c)),
                pl.BlockSpec((8, width), lambda c, *_: (0, 0)),
                pl.BlockSpec((models, cols), lambda c, *_: (0, c)),
            ],
            scratch_shapes=[
                pltpu.VMEM((models, cols, block), F32),
                pltpu.VMEM((models, block, cols), F32),
                pltpu.VMEM((block, 128), F32),
                pltpu.VMEM((16, block), F32),
                pltpu.VMEM((block, models, cols), F32),
            ],
        ),
        compiler_params=pltpu.CompilerParams(vmem_limit_bytes=56 * 1024 * 1024),
        name="weights",
    )(units, count, xs, xs, es, es, feats, grads, dec, dec, inv_norm)


def unit_lists(is_active):
    tiles = is_active.shape[0]
    ids = jnp.arange(tiles, dtype=jnp.int32)
    before = (ids[:, None] > ids[None, :]).astype(jnp.int32)
    rank = jnp.sum(before[:, :, None] * is_active[None], axis=1)
    places = jnp.arange(MOST, dtype=jnp.int32)
    picked = (is_active[:, :, None] == 1) & (rank[:, :, None] == places)
    idle = jnp.min(jnp.where(is_active == 0, ids[:, None], tiles - 1), axis=0)
    count = jnp.sum(is_active, axis=0)
    tile = jnp.sum(jnp.where(picked, ids[:, None, None], 0), axis=0)
    tile = jnp.where(places[None, :] < count[:, None], tile, idle[:, None])
    x, y = plane()
    tx, ty = tile % SIDE, tile // SIDE
    one = ((x - tx) % SIDE) * 2 * SIDE + ty
    two = ((y - ty) % SIDE) * 2 * SIDE + SIDE + tx
    return jnp.stack([one, two], axis=2).reshape(-1), count


def on_device(activations, enc_weight, enc_bias, dec_weight, dec_bias, active):
    slabs, models, depth, block = enc_weight.shape
    rows, tiles = activations.shape[0], active.shape[0]
    width = slabs * block
    scale = 1.0 / math.sqrt(MOST * TILE)
    ids = lax.axis_index("lat") * slabs + jnp.arange(slabs, dtype=jnp.int32)
    is_active = jnp.any(active[:, :, None] == ids[None, None, :], axis=1).astype(jnp.int32)
    mask = jnp.broadcast_to(is_active.astype(F32)[:, None, :, None], (tiles, 1, slabs, block))
    mask = mask.reshape(tiles, 1, width)
    units, count = unit_lists(is_active)
    x = activations.reshape(2, rows // 2, models * depth)
    dec = dec_weight.reshape(width, models * depth)
    sq = jnp.stack(
        [jnp.sum(jnp.square(dec[:, m * depth : (m + 1) * depth].astype(F32)), axis=1) for m in range(models)]
    )
    enc = enc_weight.reshape(slabs, models * depth, block)
    xs, es, feats, grads, sq_sum = step(
        scale, x, enc, dec, enc_bias.reshape(1, width), dec_bias.reshape(1, models * depth), mask, sq
    )
    inv_norm = (1.0 / jnp.sqrt(sq_sum + NORM_EPSILON))[:, :, None]
    flat = (2 * tiles, UNIT)
    grad_enc, grad_dec, enc_sum, err_sum = weights(
        scale,
        units,
        count,
        xs.reshape(flat + (models * depth,)),
        es.reshape(flat + (models * depth,)),
        feats.reshape(flat + (width,)),
        grads.reshape(flat + (width,)),
        dec,
        inv_norm,
        models,
        slabs,
    )
    return (
        grad_enc,
        enc_sum[0].reshape(slabs, block),
        grad_dec.reshape(dec_weight.shape),
        err_sum,
    )


def solution(mesh):
    placed = (
        P("lat", None, "tok"),
        P("lat", None, "tok", None),
        P("lat", None),
        P("lat", None, None, "tok"),
        P(None, "tok"),
        P(),
    )
    return jax.shard_map(
        on_device,
        mesh=mesh,
        in_specs=placed,
        out_specs=(
            P("lat", None, "tok", None),
            P("lat", None),
            P("lat", None, None, "tok"),
            P(None, "tok"),
        ),
        check_vma=False,
    )
```

time: 323 us -> 254 us (0.79); the launches traced: 319 us -> 253 us
  Pallas kernels: 287 us -> 234 us
  other arithmetic: 11.3 us -> 3.68 us
  local copies, waits for them, and re-layouts: 20.3 us -> 14.7 us
    pallas_call x1, Pallas kernels: 263 us -> 199 us  [step(): pl.pallas_call(functools.partial(step_kernel, scale), out_shape=[rows, ro...]
    pallas_call x1, Pallas kernels: 23.9 us -> 34.9 us  [weights(): pl.pallas_call(functools.partial(weights_kernel, scale), out_shape=[jax.S...]
    reshape x2 -> x0, local copies, waits for them, and re-layouts: 8.61 us -> none  [the longest x1 8 us: on_device(): grad_dec.reshape(dec_weight.shape)]
    reduce_sum x2 -> x0, other arithmetic: 7.6 us -> none  [the longest x1 4.73 us: on_device(): grad_dec_bias = scale * jnp.sum(es.astype(F32), axis=(0, 1, 2))]
    unnamed x13 -> x7, local copies, waits for them, and re-layouts: 6.82 us -> 8.13 us
where the time goes in v4:
time: 254 us; the launch traced here: 253 us
  Pallas kernels  234 us (92%)
  local copies, waits for them, and re-layouts  14.7 us (6%)
  other arithmetic  3.68 us (1%)
    pallas_call x1, Pallas kernels, step(): pl.pallas_call(functools.partial(step_kernel, scale), out_shape=[rows, ro...  199 us
    pallas_call x1, Pallas kernels, weights(): pl.pallas_call(functools.partial(weights_kernel, scale), out_shape=[jax.S...  34.9 us
    unnamed x7, local copies, waits for them, and re-layouts  8.13 us

profile of v4, /device:TPU:1, one launch (start us, length us, event | category | flops | bytes accessed | tf_op | source)
XLA Modules:
  0.0 253.2 jit_solution(11303576030085137026)
XLA Ops:
  0.6 0.9 compare_reduce_fusion
  1.6 0.2 convert_reduce_fusion
  1.7 0.0 copy-start.1
  1.7 1.3 copy.17
  3.0 0.1 copy.14
  3.1 1.3 copy.18
  4.4 0.1 multiply_reduce_fusion.2
  4.6 0.2 select_reduce_fusion
  4.7 0.1 fusion.4
  4.8 0.1 copy.13
  4.9 0.6 reshape.336.units
  5.6 0.1 broadcast_in_dim.62
  5.7 0.7 broadcast_in_dim.63.mask
  6.4 2.2 reshape.337.x
  8.6 3.6 %copy.16 = bf16[128,8,2,1024]{3,1,2,0:T(8,128)(2,1)S(1)} copy(bf16[128,8,2,1024]{3,2,1,0:T(2,128)(2,1)} %bitcast.45) | data formatting | bytes 8388608
  12.2 0.0 copy-done.1
  12.2 0.0 copy-start
  12.2 1.9 copy-done
  14.1 0.9 multiply_reduce_fusion.1
  15.0 0.6 pad_maximum_fusion.sq
  15.6 199.1 %step.1 = (bf16[4,8,64,2048]{3,2,1,0:T(8,128)(2,1)}, bf16[4,8,64,2048]{3,2,1,0:T(8,128)(2,1)}, bf16[4,8,64,1024]{3,2,1,0:T(8,128)(2,1)}, bf16[4,8,64,1024]{3,2,1,0:T(8,128)(2,1)}, f32[2,1024]{1,0:T(2,128)}) custom-call(bf16[2,64,2048]{2,1,0:T(8,128)(2,1)} %reshape.337.x, bf16[4,2048,256]{2,1,0:T(8,128)(2,1)} %bitcast.46, bf16[1024,2048]{1,0:T(8,128)(2,1)} %bitcast.38, ...), custom_call_target="tpu_custom_call" | custom-call | tf_op jit(solution)/shard_map/step/pallas_call | solution.py:592
  214.7 0.7 rsqrt_bitcast_fusion
  215.5 1.4 copy.15.inv_norm
  216.9 34.9 %weights.1 = (bf16[4,2,1024,256]{3,2,1,0:T(8,128)(2,1)}, bf16[1024,2,1024]{2,1,0:T(2,128)(2,1)}, f32[8,1024]{1,0:T(8,128)}, f32[2,1024]{1,0:T(2,128)}) custom-call(s32[64]{0:T(128)} %reshape.336.units, s32[4]{0:T(128)} %copy-done.1, bf16[32,64,2048]{2,1,0:T(8,128)(2,1)} %bitcast.41, bf16[32,64,2048]{2,1,0:T(8,128)(2,1)} %bitcast.42, ...), custom_call_target="tpu_custom_call" | custom-call | tf_op jit(solution)/shard_map/weights/pallas_call | solution.py:683
  251.8 0.8 slice_reduce_fusion
  252.6 0.6 reshape_squeeze.3
  (4 shorter events, 0.0 us)
Async XLA Ops:
  1.7 10.5 %copy-start.1 = (s32[4]{0:T(128)}, s32[4]{0:T(128)S(1)}, u32[]{:S(2)}) copy-start(s32[4]{0:T(128)S(1)} %get-tuple-element.24.count) | copy-start | bytes 52
  12.2 1.9 copy-start

commit v5 on v4

--- a/solution.py
+++ b/solution.py
@@ -115,50 +115,50 @@
     (FWD, CROSS, 1), (FWD, RELAY, 0, 1), (FWD, WORK, 0, 0), (FWD, TOK, 0, 0, 1), (FWD, NORM, 0),
     (FWD, FAR, 0), (FWD, SEND, 1, 0), (FWD, NEAR, 1), (FWD, TOK, 0, 0, 2), (FWD, WORK, 0, 1),
     (FWD, TOK, 0, 1, 1), (FWD, SEND, 1, 1), (FWD, TOK, 0, 0, 3), (FWD, RELAY, 1, 0), (FWD, FAR, 1),
-    (FWD, TOK, 0, 1, 2), (FWD, TOK, 0, 0, 4), (FWD, SEND, 3, 0), (FWD, RELAY, 1, 1),
-    (FWD, TOK, 0, 1, 3), (FWD, WORK, 1, 0), (FWD, NORM, 1), (FWD, TOK, 1, 0, 1), (FWD, SEND, 3, 1),
-    (FWD, TOK, 0, 0, 5), (FWD, RELAY, 3, 0), (FWD, TOK, 0, 1, 4), (FWD, WORK, 1, 1),
-    (FWD, TOK, 0, 0, 6), (FWD, TOK, 1, 0, 2), (FWD, TOK, 1, 1, 1), (FWD, SEND, 2, 0),
-    (FWD, RELAY, 3, 1), (FWD, TOK, 0, 0, 7), (FWD, TOK, 0, 1, 5), (FWD, WORK, 3, 0), (FWD, NORM, 2),
-    (FWD, TOK, 1, 0, 3), (FWD, TOK, 3, 0, 1), (FWD, TOK, 1, 1, 2), (FWD, SEND, 2, 1),
-    (FWD, RELAY, 2, 0), (FWD, TOK, 0, 1, 6), (FWD, WORK, 3, 1), (FWD, TOK, 0, 1, 7),
-    (FWD, TOK, 1, 0, 4), (FWD, TOK, 1, 1, 3), (FWD, TOK, 3, 0, 2), (FWD, TOK, 3, 1, 1),
-    (FWD, RELAY, 2, 1), (FWD, TOK, 1, 0, 5), (FWD, WORK, 2, 0), (FWD, TOK, 2, 0, 1),
-    (FWD, TOK, 1, 1, 4), (FWD, TOK, 3, 1, 2), (FWD, TOK, 3, 0, 3), (FWD, TOK, 2, 0, 2),
-    (FWD, TOK, 1, 0, 6), (FWD, TOK, 1, 1, 5), (FWD, WORK, 2, 1), (FWD, TOK, 1, 0, 7),
-    (FWD, TOK, 3, 1, 3), (FWD, TOK, 2, 1, 1), (MID, BEGIN, 0, 0), (MID, BEGIN, 0, 1),
-    (FWD, TOK, 3, 0, 4), (FWD, TOK, 2, 1, 2), (FWD, TOK, 2, 0, 3), (MID, RELAY, 0, 0),
-    (MID, BEGIN, 1, 0), (FWD, TOK, 1, 1, 6), (FWD, TOK, 3, 1, 4), (MID, RELAY, 0, 1),
-    (FWD, TOK, 3, 0, 5), (FWD, TOK, 1, 1, 7), (MID, BEGIN, 1, 1), (FWD, TOK, 2, 1, 3),
-    (MID, REDUCE, 0, 0), (MID, RELAY, 1, 0), (FWD, TOK, 2, 0, 4), (FWD, TOK, 3, 1, 5),
-    (MID, REDUCE, 0, 1), (FWD, TOK, 3, 0, 6), (MID, RELAY, 1, 1), (FWD, TOK, 2, 1, 4),
-    (FWD, TOK, 3, 0, 7), (MID, BEGIN, 3, 0), (FWD, TOK, 3, 1, 6), (FWD, TOK, 2, 0, 5),
-    (MID, REDUCE, 1, 0), (FWD, TOK, 2, 1, 5), (MID, REDUCE, 1, 1), (FWD, TOK, 3, 1, 7),
-    (MID, BEGIN, 3, 1), (FWD, TOK, 2, 0, 6), (FWD, TOK, 2, 1, 6), (MID, RELAY, 3, 0),
-    (FWD, TOK, 2, 0, 7), (MID, BEGIN, 2, 0), (FWD, TOK, 2, 1, 7), (MID, BEGIN, 2, 1),
-    (MID, RELAY, 3, 1), (MID, REDUCE, 3, 0), (MID, RELAY, 2, 0), (MID, RELAY, 2, 1),
-    (MID, REDUCE, 3, 1), (MID, REDUCE, 2, 0), (MID, REDUCE, 2, 1), (MID, JOIN, 0), (MID, JOIN, 1),
-    (MID, FINISH, 0), (MID, FINISH, 1), (BWD, SEND, 0, 0), (BWD, CROSS, 0), (BWD, SEND, 0, 1),
-    (BWD, RELAY, 0, 0), (BWD, NEAR, 0), (BWD, CROSS, 1), (BWD, RELAY, 0, 1), (BWD, WORK, 0, 0),
-    (BWD, TOK, 0, 0, 1), (BWD, FAR, 0), (BWD, SEND, 1, 0), (BWD, TOK, 0, 0, 2), (BWD, NEAR, 1),
-    (BWD, WORK, 0, 1), (BWD, TOK, 0, 0, 3), (BWD, TOK, 0, 1, 1), (BWD, SEND, 1, 1),
-    (BWD, RELAY, 1, 0), (BWD, TOK, 0, 0, 4), (BWD, TOK, 0, 1, 2), (BWD, FAR, 1), (BWD, SEND, 3, 0),
-    (BWD, TOK, 0, 0, 5), (BWD, RELAY, 1, 1), (BWD, TOK, 0, 1, 3), (BWD, WORK, 1, 0),
-    (BWD, TOK, 0, 0, 6), (BWD, TOK, 1, 0, 1), (BWD, TOK, 0, 1, 4), (BWD, SEND, 3, 1),
-    (BWD, RELAY, 3, 0), (BWD, TOK, 0, 0, 7), (BWD, TOK, 1, 0, 2), (BWD, WORK, 1, 1),
-    (BWD, TOK, 0, 1, 5), (BWD, TOK, 1, 1, 1), (BWD, SEND, 2, 0), (BWD, TOK, 1, 0, 3),
-    (BWD, RELAY, 3, 1), (BWD, TOK, 0, 1, 6), (BWD, WORK, 3, 0), (BWD, TOK, 1, 0, 4),
-    (BWD, TOK, 1, 1, 2), (BWD, TOK, 0, 1, 7), (BWD, TOK, 3, 0, 1), (BWD, SEND, 2, 1),
-    (BWD, RELAY, 2, 0), (BWD, WORK, 3, 1), (BWD, TOK, 1, 0, 5), (BWD, TOK, 1, 1, 3),
-    (BWD, TOK, 3, 0, 2), (BWD, TOK, 3, 1, 1), (BWD, RELAY, 2, 1), (BWD, TOK, 1, 0, 6),
-    (BWD, TOK, 1, 1, 4), (BWD, WORK, 2, 0), (BWD, TOK, 1, 0, 7), (BWD, TOK, 3, 0, 3),
-    (BWD, TOK, 3, 1, 2), (BWD, TOK, 2, 0, 1), (BWD, TOK, 1, 1, 5), (BWD, WORK, 2, 1),
-    (BWD, TOK, 3, 0, 4), (BWD, TOK, 3, 1, 3), (BWD, TOK, 2, 0, 2), (BWD, TOK, 2, 1, 1),
-    (BWD, TOK, 1, 1, 6), (BWD, TOK, 3, 0, 5), (BWD, TOK, 3, 1, 4), (BWD, TOK, 2, 1, 2),
-    (BWD, TOK, 1, 1, 7), (BWD, TOK, 2, 0, 3), (BWD, TOK, 3, 0, 6), (BWD, TOK, 3, 1, 5),
-    (BWD, TOK, 3, 0, 7), (BWD, TOK, 2, 1, 3), (BWD, TOK, 2, 0, 4), (BWD, TOK, 3, 1, 6),
-    (BWD, TOK, 2, 1, 4), (BWD, TOK, 3, 1, 7), (BWD, TOK, 2, 0, 5), (BWD, TOK, 2, 1, 5),
-    (BWD, TOK, 2, 0, 6), (BWD, TOK, 2, 1, 6), (BWD, TOK, 2, 0, 7), (BWD, TOK, 2, 1, 7),
+    (FWD, TOK, 0, 1, 2), (FWD, TOK, 0, 0, 4), (FWD, RELAY, 1, 1), (FWD, TOK, 0, 1, 3),
+    (FWD, WORK, 1, 0), (FWD, NORM, 1), (FWD, SEND, 3, 0), (FWD, TOK, 1, 0, 1), (FWD, SEND, 3, 1),
+    (FWD, WORK, 1, 1), (FWD, TOK, 1, 1, 1), (FWD, SEND, 2, 0), (FWD, TOK, 0, 0, 5),
+    (FWD, TOK, 0, 1, 4), (FWD, TOK, 1, 0, 2), (FWD, RELAY, 3, 0), (FWD, TOK, 0, 0, 6),
+    (FWD, TOK, 1, 1, 2), (FWD, TOK, 0, 1, 5), (FWD, TOK, 0, 0, 7), (FWD, RELAY, 3, 1),
+    (FWD, TOK, 1, 0, 3), (FWD, SEND, 2, 1), (FWD, RELAY, 2, 0), (FWD, TOK, 1, 1, 3),
+    (FWD, WORK, 3, 0), (FWD, NORM, 2), (FWD, TOK, 3, 0, 1), (FWD, TOK, 0, 1, 6), (FWD, WORK, 3, 1),
+    (FWD, TOK, 1, 0, 4), (FWD, TOK, 3, 1, 1), (FWD, TOK, 1, 1, 4), (FWD, RELAY, 2, 1),
+    (FWD, TOK, 3, 0, 2), (FWD, TOK, 0, 1, 7), (FWD, TOK, 1, 0, 5), (FWD, WORK, 2, 0),
+    (FWD, TOK, 3, 1, 2), (FWD, TOK, 2, 0, 1), (FWD, TOK, 1, 1, 5), (FWD, WORK, 2, 1),
+    (MID, BEGIN, 0, 1), (FWD, TOK, 1, 0, 6), (MID, BEGIN, 0, 0), (FWD, TOK, 3, 1, 3),
+    (FWD, TOK, 1, 0, 7), (FWD, TOK, 2, 0, 2), (MID, BEGIN, 1, 0), (FWD, TOK, 1, 1, 6),
+    (MID, RELAY, 0, 1), (FWD, TOK, 3, 1, 4), (MID, RELAY, 0, 0), (FWD, TOK, 2, 0, 3),
+    (FWD, TOK, 1, 1, 7), (MID, BEGIN, 1, 1), (FWD, TOK, 3, 0, 3), (FWD, TOK, 2, 1, 1),
+    (MID, RELAY, 1, 0), (FWD, TOK, 3, 1, 5), (FWD, TOK, 2, 0, 4), (MID, REDUCE, 0, 1),
+    (FWD, TOK, 3, 0, 4), (FWD, TOK, 2, 1, 2), (FWD, TOK, 3, 1, 6), (MID, REDUCE, 0, 0),
+    (FWD, TOK, 2, 0, 5), (MID, RELAY, 1, 1), (FWD, TOK, 3, 1, 7), (MID, BEGIN, 3, 1),
+    (FWD, TOK, 3, 0, 5), (FWD, TOK, 2, 1, 3), (MID, REDUCE, 1, 0), (MID, REDUCE, 1, 1),
+    (FWD, TOK, 2, 0, 6), (FWD, TOK, 3, 0, 6), (MID, RELAY, 3, 1), (FWD, TOK, 2, 0, 7),
+    (MID, BEGIN, 2, 0), (FWD, TOK, 2, 1, 4), (FWD, TOK, 3, 0, 7), (MID, BEGIN, 3, 0),
+    (MID, REDUCE, 3, 1), (FWD, TOK, 2, 1, 5), (MID, RELAY, 2, 0), (FWD, TOK, 2, 1, 6),
+    (MID, RELAY, 3, 0), (FWD, TOK, 2, 1, 7), (MID, BEGIN, 2, 1), (MID, REDUCE, 2, 0),
+    (MID, REDUCE, 3, 0), (MID, RELAY, 2, 1), (MID, JOIN, 0), (MID, REDUCE, 2, 1), (MID, FINISH, 0),
+    (BWD, SEND, 0, 0), (BWD, CROSS, 0), (MID, JOIN, 1), (BWD, RELAY, 0, 0), (BWD, NEAR, 0),
+    (MID, FINISH, 1), (BWD, SEND, 0, 1), (BWD, WORK, 0, 0), (BWD, TOK, 0, 0, 1), (BWD, CROSS, 1),
+    (BWD, FAR, 0), (BWD, TOK, 0, 0, 2), (BWD, RELAY, 0, 1), (BWD, SEND, 1, 0), (BWD, TOK, 0, 0, 3),
+    (BWD, NEAR, 1), (BWD, WORK, 0, 1), (BWD, TOK, 0, 1, 1), (BWD, TOK, 0, 0, 4), (BWD, SEND, 1, 1),
+    (BWD, SEND, 3, 0), (BWD, RELAY, 1, 0), (BWD, TOK, 0, 1, 2), (BWD, FAR, 1), (BWD, TOK, 0, 0, 5),
+    (BWD, TOK, 0, 1, 3), (BWD, RELAY, 1, 1), (BWD, TOK, 0, 0, 6), (BWD, TOK, 0, 1, 4),
+    (BWD, TOK, 0, 0, 7), (BWD, RELAY, 3, 0), (BWD, WORK, 1, 0), (BWD, SEND, 3, 1),
+    (BWD, TOK, 1, 0, 1), (BWD, TOK, 0, 1, 5), (BWD, WORK, 1, 1), (BWD, TOK, 1, 1, 1),
+    (BWD, SEND, 2, 0), (BWD, WORK, 3, 0), (BWD, TOK, 1, 0, 2), (BWD, TOK, 3, 0, 1),
+    (BWD, RELAY, 3, 1), (BWD, TOK, 1, 1, 2), (BWD, TOK, 0, 1, 6), (BWD, SEND, 2, 1),
+    (BWD, TOK, 1, 0, 3), (BWD, TOK, 3, 0, 2), (BWD, TOK, 0, 1, 7), (BWD, RELAY, 2, 0),
+    (BWD, TOK, 1, 1, 3), (BWD, WORK, 3, 1), (BWD, TOK, 1, 0, 4), (BWD, TOK, 3, 1, 1),
+    (BWD, TOK, 3, 0, 3), (BWD, TOK, 1, 1, 4), (BWD, RELAY, 2, 1), (BWD, TOK, 3, 1, 2),
+    (BWD, TOK, 1, 0, 5), (BWD, WORK, 2, 0), (BWD, TOK, 2, 0, 1), (BWD, TOK, 1, 1, 5),
+    (BWD, TOK, 3, 0, 4), (BWD, TOK, 3, 1, 3), (BWD, WORK, 2, 1), (BWD, TOK, 2, 1, 1),
+    (BWD, TOK, 2, 0, 2), (BWD, TOK, 1, 1, 6), (BWD, TOK, 1, 0, 6), (BWD, TOK, 3, 0, 5),
+    (BWD, TOK, 2, 1, 2), (BWD, TOK, 1, 0, 7), (BWD, TOK, 2, 0, 3), (BWD, TOK, 1, 1, 7),
+    (BWD, TOK, 3, 1, 4), (BWD, TOK, 3, 0, 6), (BWD, TOK, 2, 1, 3), (BWD, TOK, 3, 0, 7),
+    (BWD, TOK, 2, 0, 4), (BWD, TOK, 3, 1, 5), (BWD, TOK, 2, 1, 4), (BWD, TOK, 2, 0, 5),
+    (BWD, TOK, 3, 1, 6), (BWD, TOK, 2, 1, 5), (BWD, TOK, 3, 1, 7), (BWD, TOK, 2, 0, 6),
+    (BWD, TOK, 2, 1, 6), (BWD, TOK, 2, 0, 7), (BWD, TOK, 2, 1, 7),
 )
 
 
@@ -444,8 +444,11 @@
     wires.go(swap)
 
 
+    ready = set()
+
     def decode(k, e):
-        if e == PIECES[0]:
+        if k not in ready:
+            ready.add(k)
             wires.settle(front.name(k))
             saves["x", k].wait()
 
@@ -557,9 +560,12 @@
         BWD: {g: tok_flow(wires, BWD, *g, bwd[0], grads, *bwd[1:], pre_grad) for g in ORDER},
     }
 
+    done = []
+
     def tok(phase, k, e, number):
         next(toks[phase][k, e])
-        if number == 7 and e == PIECES[-1]:
+        done.append((phase, k, number))
+        if number == 7 and done.count((phase, k, 7)) == len(PIECES):
             save(phase, k, *((feats, feat_out) if phase == FWD else (grads, grad_out)))
 
     steps = {MID: {BEGIN: reduce_begin, RELAY: reduce_relay, REDUCE: reduce, JOIN: reduce_far, FINISH: finish}}
@@ -623,62 +629,53 @@
     )(x, enc, dec, enc_bias, dec_bias, mask, sq)
 
 
-QUAD = 4
+QUAD = 8
 
 
 def weights_kernel(
-    scale, units, count, x0, x1, e0, e1, feats, grads, d0, d1, inv_norm, grad_enc, grad_dec, enc_sum, err_sum, acc_e, acc_d, tot, gsum, mixed
+    scale, units, count, xs, es, feats, grads, dec, inv_norm, grad_enc, grad_dec, enc_sum, err_sum, acc_e, acc_d, tot, gsum, mixed
 ):
-    slabs, block = grad_enc.shape[0], grad_enc.shape[3]
-    for m, err in enumerate((e0, e1)):
-        rows = err[...].reshape(-1, err.shape[2])
-        ones = jnp.ones((16, rows.shape[0]), BF16)
-        total = jnp.dot(ones, rows, preferred_element_type=F32)
-        err_sum[pl.ds(m, 1)] = scale * total[:1]
-    for slab in range(slabs):
-        at = pl.ds(slab * block, block)
-        acc_e[...] = jnp.zeros_like(acc_e)
-        acc_d[...] = jnp.zeros_like(acc_d)
-        tot[...] = jnp.zeros_like(tot)
-        gsum[...] = jnp.zeros_like(gsum)
-
-        def pair(i, carry, slab=slab, at=at):
-            ids = [units[slab * 2 * MOST + i * QUAD + n] for n in range(QUAD)]
-            f = jnp.concatenate([feats[n, :, at] for n in ids], axis=0)
-            g = jnp.concatenate([grads[n, :, at] for n in ids], axis=0)
-            for m, (acts, err) in enumerate(((x0, e0), (x1, e1))):
-                a = jnp.concatenate([acts[n] for n in ids], axis=0)
-                e = jnp.concatenate([err[n] for n in ids], axis=0)
-                acc_e[m] += lax.dot_general(a, g, TN, preferred_element_type=F32)
-                acc_d[m] += lax.dot_general(f, e, TN, preferred_element_type=F32)
-            tot[...] += lax.dot_general(f, jnp.ones((QUAD * UNIT, 128), BF16), TN, preferred_element_type=F32)
-            gsum[...] += jnp.dot(jnp.ones((16, QUAD * UNIT), BF16), g, preferred_element_type=F32)
-            return carry
-
-        lax.fori_loop(0, lax.div(count[slab] + 1, 2), pair, 0)
-        enc_sum[:, at] = gsum[:8]
-        both = []
-        for m, dec in enumerate((d0, d1)):
-            grad_enc[slab, m] = acc_e[m].astype(grad_enc.dtype)
-            col = SPARSITY * tot[:, :1] * inv_norm[m, at, :]
-            both.append(scale * (acc_d[m] + col * f32(dec[at])))
-        for m in range(len(both)):
-            mixed[:, m, :] = both[m]
-        grad_dec[at] = mixed[...].astype(grad_dec.dtype)
+    slab = pl.program_id(0)
+    models, part = grad_enc.shape[1], grad_enc.shape[2]
+    cols = err_sum.shape[2]
+    rows = es[:, :, pl.ds(pl.multiple_of(slab * cols, cols), cols)].reshape(-1, cols)
+    err_sum[0] = scale * jnp.dot(jnp.ones((16, rows.shape[0]), BF16), rows, preferred_element_type=F32)[:8]
+    acc_e[...] = jnp.zeros_like(acc_e)
+    acc_d[...] = jnp.zeros_like(acc_d)
+    tot[...] = jnp.zeros_like(tot)
+    gsum[...] = jnp.zeros_like(gsum)
+
+    def pair(i, carry):
+        ids = [units[slab * 2 * MOST + i * QUAD + n] for n in range(QUAD)]
+        f = jnp.concatenate([feats[n] for n in ids], axis=0)
+        g = jnp.concatenate([grads[n] for n in ids], axis=0)
+        a = jnp.concatenate([xs[n] for n in ids], axis=0)
+        e = jnp.concatenate([es[n] for n in ids], axis=0)
+        acc_e[...] += lax.dot_general(g, a, TN, preferred_element_type=F32)
+        acc_d[...] += lax.dot_general(f, e, TN, preferred_element_type=F32)
+        tot[...] += lax.dot_general(f, jnp.ones((QUAD * UNIT, 128), BF16), TN, preferred_element_type=F32)
+        gsum[...] += jnp.dot(jnp.ones((16, QUAD * UNIT), BF16), g, preferred_element_type=F32)
+        return carry
+
+    lax.fori_loop(0, lax.div(count[slab] + 3, 4), pair, 0)
+    enc_sum[...] = gsum[:8]
+    for m in range(models):
+        at = pl.ds(m * part, part)
+        grad_enc[0, m] = acc_e[:, at].astype(BF16).T
+        col = SPARSITY * tot[:, :1] * inv_norm[m]
+        mixed[:, m, :] = scale * (acc_d[:, at] + col * f32(dec[:, at]))
+    grad_dec[...] = mixed[...].astype(grad_dec.dtype)
 
 
 def weights(scale, units, count, xs, es, feats, grads, dec, inv_norm, models, slabs):
     width, depth = dec.shape
-    cols = 256
     block = width // slabs
     part = depth // models
-    steps = part // cols
+    cols = depth // slabs
+    once = pl.Buffered(1)
 
     def whole(a):
-        return pl.BlockSpec(a.shape, lambda c, *_: (0,) * a.ndim)
-
-    def wide(a, m):
-        return pl.BlockSpec(a.shape[:-1] + (cols,), lambda c, *_: (0,) * (a.ndim - 1) + (c + m * steps,))
+        return pl.BlockSpec(a.shape, lambda c, *_: (0,) * a.ndim, pipeline_mode=once)
 
     return pl.pallas_call(
         functools.partial(weights_kernel, scale),
@@ -686,39 +683,36 @@
             jax.ShapeDtypeStruct((slabs, models, part, block), BF16),
             jax.ShapeDtypeStruct((width, models, part), BF16),
             jax.ShapeDtypeStruct((8, width), F32),
-            jax.ShapeDtypeStruct((models, part), F32),
+            jax.ShapeDtypeStruct((slabs, 8, cols), F32),
         ],
         grid_spec=pltpu.PrefetchScalarGridSpec(
             num_scalar_prefetch=2,
-            grid=(steps,),
+            grid=(slabs,),
             in_specs=[
-                wide(xs, 0),
-                wide(xs, 1),
-                wide(es, 0),
-                wide(es, 1),
-                whole(feats),
-                whole(grads),
-                wide(dec, 0),
-                wide(dec, 1),
-                whole(inv_norm),
+                whole(xs),
+                whole(es),
+                pl.BlockSpec(feats.shape[:2] + (block,), lambda c, *_: (0, 0, c)),
+                pl.BlockSpec(grads.shape[:2] + (block,), lambda c, *_: (0, 0, c)),
+                pl.BlockSpec((block, depth), lambda c, *_: (c, 0)),
+                pl.BlockSpec((models, block, 1), lambda c, *_: (0, c, 0)),
             ],
             out_specs=[
-                pl.BlockSpec((slabs, models, cols, block), lambda c, *_: (0, 0, c, 0)),
-                pl.BlockSpec((width, models, cols), lambda c, *_: (0, 0, c)),
-                pl.BlockSpec((8, width), lambda c, *_: (0, 0)),
-                pl.BlockSpec((models, cols), lambda c, *_: (0, c)),
+                pl.BlockSpec((1, models, part, block), lambda c, *_: (c, 0, 0, 0)),
+                pl.BlockSpec((block, models, part), lambda c, *_: (c, 0, 0)),
+                pl.BlockSpec((8, block), lambda c, *_: (0, c)),
+                pl.BlockSpec((1, 8, cols), lambda c, *_: (c, 0, 0)),
             ],
             scratch_shapes=[
-                pltpu.VMEM((models, cols, block), F32),
-                pltpu.VMEM((models, block, cols), F32),
+                pltpu.VMEM((block, depth), F32),
+                pltpu.VMEM((block, depth), F32),
                 pltpu.VMEM((block, 128), F32),
                 pltpu.VMEM((16, block), F32),
-                pltpu.VMEM((block, models, cols), F32),
+                pltpu.VMEM((block, models, part), F32),
             ],
         ),
         compiler_params=pltpu.CompilerParams(vmem_limit_bytes=56 * 1024 * 1024),
         name="weights",
-    )(units, count, xs, xs, es, es, feats, grads, dec, dec, inv_norm)
+    )(units, count, xs, es, feats, grads, dec, inv_norm)
 
 
 def unit_lists(is_active):
@@ -777,7 +771,7 @@
         grad_enc,
         enc_sum[0].reshape(slabs, block),
         grad_dec.reshape(dec_weight.shape),
-        err_sum,
+        err_sum[:, 0].reshape(models, depth),
     )
 
 

time: 254 us -> 236 us (0.929)
  Pallas kernels: 234 us -> 214 us
    pallas_call x1, Pallas kernels: 34.9 us -> 24.1 us  [weights(): pl.pallas_call(functools.partial(weights_kernel, scale), out_shape=[jax.S...]
    pallas_call x1, Pallas kernels: 199 us -> 190 us  [step(): pl.pallas_call(functools.partial(step_kernel, scale), out_shape=[rows, ro...]
where the time goes in v5:
time: 236 us; the launch traced here: 235 us
  Pallas kernels  214 us (91%)
  local copies, waits for them, and re-layouts  16.2 us (7%)
  other arithmetic  3.68 us (2%)
    pallas_call x1, Pallas kernels, step(): pl.pallas_call(functools.partial(step_kernel, scale), out_shape=[rows, ro...  190 us
    pallas_call x1, Pallas kernels, weights(): pl.pallas_call(functools.partial(weights_kernel, scale), out_shape=[jax.S...  24.1 us
    unnamed x7, local copies, waits for them, and re-layouts  8.13 us

profile of v5, /device:TPU:1, one launch (start us, length us, event | category | flops | bytes accessed | tf_op | source)
XLA Modules:
  0.0 234.7 jit_solution(184509304810089357)
XLA Ops:
  0.6 0.9 compare_reduce_fusion
  1.6 0.2 convert_reduce_fusion
  1.7 0.0 copy-start.1
  1.7 1.3 copy.17
  3.0 0.1 copy.14
  3.1 1.3 copy.18
  4.4 0.1 multiply_reduce_fusion.2
  4.6 0.2 select_reduce_fusion
  4.7 0.1 fusion.4
  4.8 0.1 copy.13
  4.9 0.6 reshape.336.units
  5.6 0.1 broadcast_in_dim.62
  5.7 0.7 broadcast_in_dim.63.mask
  6.4 2.2 reshape.337.x
  8.6 3.6 %copy.16 = bf16[128,8,2,1024]{3,1,2,0:T(8,128)(2,1)S(1)} copy(bf16[128,8,2,1024]{3,2,1,0:T(2,128)(2,1)} %bitcast.42) | data formatting | bytes 8388608
  12.2 0.0 copy-done.1
  12.2 0.0 copy-start
  12.2 1.9 copy-done
  14.1 0.9 multiply_reduce_fusion.1
  15.0 0.6 pad_maximum_fusion.sq
  15.6 190.0 %step.1 = (bf16[4,8,64,2048]{3,2,1,0:T(8,128)(2,1)}, bf16[4,8,64,2048]{3,2,1,0:T(8,128)(2,1)}, bf16[4,8,64,1024]{3,2,1,0:T(8,128)(2,1)}, bf16[4,8,64,1024]{3,2,1,0:T(8,128)(2,1)}, f32[2,1024]{1,0:T(2,128)}) custom-call(bf16[2,64,2048]{2,1,0:T(8,128)(2,1)} %reshape.337.x, bf16[4,2048,256]{2,1,0:T(8,128)(2,1)} %bitcast.43, bf16[1024,2048]{1,0:T(8,128)(2,1)} %bitcast.38, ...), custom_call_target="tpu_custom_call" | custom-call | tf_op jit(solution)/shard_map/step/pallas_call | solution.py:598
  205.6 0.7 rsqrt_bitcast_fusion
  206.3 1.4 copy.15.inv_norm
  207.7 24.1 %weights.1 = (bf16[4,2,1024,256]{3,2,1,0:T(8,128)(2,1)}, bf16[1024,2,1024]{2,1,0:T(2,128)(2,1)}, f32[8,1024]{1,0:T(8,128)}, f32[4,8,512]{2,1,0:T(8,128)}) custom-call(s32[64]{0:T(128)} %reshape.336.units, s32[4]{0:T(128)} %copy-done.1, bf16[32,64,2048]{2,1,0:T(8,128)(2,1)} %bitcast.40, bf16[32,64,2048]{2,1,0:T(8,128)(2,1)} %bitcast.41, ...), custom_call_target="tpu_custom_call" | custom-call | tf_op jit(solution)/shard_map/weights/pallas_call | solution.py:680
  231.8 0.8 slice_reduce_fusion.1
  232.6 0.6 reshape_squeeze.6
  233.2 0.9 slice_reduce_fusion
  234.1 0.6 reshape_squeeze.7
  (4 shorter events, 0.0 us)
Async XLA Ops:
  1.7 10.5 %copy-start.1 = (s32[4]{0:T(128)}, s32[4]{0:T(128)S(1)}, u32[]{:S(2)}) copy-start(s32[4]{0:T(128)S(1)} %get-tuple-element.24.count) | copy-start | bytes 52
  12.2 1.9 copy-start

commit v6 on v5

--- a/solution.py
+++ b/solution.py
@@ -111,53 +111,53 @@
 FWD, MID, BWD = range(3)
 SEND, CROSS, NEAR, FAR, RELAY, WORK, TOK, NORM, BEGIN, REDUCE, JOIN, FINISH = range(12)
 SCRIPT = (
-    (FWD, SEND, 0, 0), (FWD, CROSS, 0), (FWD, SEND, 0, 1), (FWD, RELAY, 0, 0), (FWD, NEAR, 0),
-    (FWD, CROSS, 1), (FWD, RELAY, 0, 1), (FWD, WORK, 0, 0), (FWD, TOK, 0, 0, 1), (FWD, NORM, 0),
-    (FWD, FAR, 0), (FWD, SEND, 1, 0), (FWD, NEAR, 1), (FWD, TOK, 0, 0, 2), (FWD, WORK, 0, 1),
-    (FWD, TOK, 0, 1, 1), (FWD, SEND, 1, 1), (FWD, TOK, 0, 0, 3), (FWD, RELAY, 1, 0), (FWD, FAR, 1),
-    (FWD, TOK, 0, 1, 2), (FWD, TOK, 0, 0, 4), (FWD, RELAY, 1, 1), (FWD, TOK, 0, 1, 3),
-    (FWD, WORK, 1, 0), (FWD, NORM, 1), (FWD, SEND, 3, 0), (FWD, TOK, 1, 0, 1), (FWD, SEND, 3, 1),
-    (FWD, WORK, 1, 1), (FWD, TOK, 1, 1, 1), (FWD, SEND, 2, 0), (FWD, TOK, 0, 0, 5),
-    (FWD, TOK, 0, 1, 4), (FWD, TOK, 1, 0, 2), (FWD, RELAY, 3, 0), (FWD, TOK, 0, 0, 6),
-    (FWD, TOK, 1, 1, 2), (FWD, TOK, 0, 1, 5), (FWD, TOK, 0, 0, 7), (FWD, RELAY, 3, 1),
-    (FWD, TOK, 1, 0, 3), (FWD, SEND, 2, 1), (FWD, RELAY, 2, 0), (FWD, TOK, 1, 1, 3),
-    (FWD, WORK, 3, 0), (FWD, NORM, 2), (FWD, TOK, 3, 0, 1), (FWD, TOK, 0, 1, 6), (FWD, WORK, 3, 1),
-    (FWD, TOK, 1, 0, 4), (FWD, TOK, 3, 1, 1), (FWD, TOK, 1, 1, 4), (FWD, RELAY, 2, 1),
-    (FWD, TOK, 3, 0, 2), (FWD, TOK, 0, 1, 7), (FWD, TOK, 1, 0, 5), (FWD, WORK, 2, 0),
-    (FWD, TOK, 3, 1, 2), (FWD, TOK, 2, 0, 1), (FWD, TOK, 1, 1, 5), (FWD, WORK, 2, 1),
-    (MID, BEGIN, 0, 1), (FWD, TOK, 1, 0, 6), (MID, BEGIN, 0, 0), (FWD, TOK, 3, 1, 3),
-    (FWD, TOK, 1, 0, 7), (FWD, TOK, 2, 0, 2), (MID, BEGIN, 1, 0), (FWD, TOK, 1, 1, 6),
-    (MID, RELAY, 0, 1), (FWD, TOK, 3, 1, 4), (MID, RELAY, 0, 0), (FWD, TOK, 2, 0, 3),
-    (FWD, TOK, 1, 1, 7), (MID, BEGIN, 1, 1), (FWD, TOK, 3, 0, 3), (FWD, TOK, 2, 1, 1),
-    (MID, RELAY, 1, 0), (FWD, TOK, 3, 1, 5), (FWD, TOK, 2, 0, 4), (MID, REDUCE, 0, 1),
-    (FWD, TOK, 3, 0, 4), (FWD, TOK, 2, 1, 2), (FWD, TOK, 3, 1, 6), (MID, REDUCE, 0, 0),
-    (FWD, TOK, 2, 0, 5), (MID, RELAY, 1, 1), (FWD, TOK, 3, 1, 7), (MID, BEGIN, 3, 1),
-    (FWD, TOK, 3, 0, 5), (FWD, TOK, 2, 1, 3), (MID, REDUCE, 1, 0), (MID, REDUCE, 1, 1),
-    (FWD, TOK, 2, 0, 6), (FWD, TOK, 3, 0, 6), (MID, RELAY, 3, 1), (FWD, TOK, 2, 0, 7),
-    (MID, BEGIN, 2, 0), (FWD, TOK, 2, 1, 4), (FWD, TOK, 3, 0, 7), (MID, BEGIN, 3, 0),
-    (MID, REDUCE, 3, 1), (FWD, TOK, 2, 1, 5), (MID, RELAY, 2, 0), (FWD, TOK, 2, 1, 6),
-    (MID, RELAY, 3, 0), (FWD, TOK, 2, 1, 7), (MID, BEGIN, 2, 1), (MID, REDUCE, 2, 0),
-    (MID, REDUCE, 3, 0), (MID, RELAY, 2, 1), (MID, JOIN, 0), (MID, REDUCE, 2, 1), (MID, FINISH, 0),
-    (BWD, SEND, 0, 0), (BWD, CROSS, 0), (MID, JOIN, 1), (BWD, RELAY, 0, 0), (BWD, NEAR, 0),
-    (MID, FINISH, 1), (BWD, SEND, 0, 1), (BWD, WORK, 0, 0), (BWD, TOK, 0, 0, 1), (BWD, CROSS, 1),
-    (BWD, FAR, 0), (BWD, TOK, 0, 0, 2), (BWD, RELAY, 0, 1), (BWD, SEND, 1, 0), (BWD, TOK, 0, 0, 3),
-    (BWD, NEAR, 1), (BWD, WORK, 0, 1), (BWD, TOK, 0, 1, 1), (BWD, TOK, 0, 0, 4), (BWD, SEND, 1, 1),
-    (BWD, SEND, 3, 0), (BWD, RELAY, 1, 0), (BWD, TOK, 0, 1, 2), (BWD, FAR, 1), (BWD, TOK, 0, 0, 5),
-    (BWD, TOK, 0, 1, 3), (BWD, RELAY, 1, 1), (BWD, TOK, 0, 0, 6), (BWD, TOK, 0, 1, 4),
-    (BWD, TOK, 0, 0, 7), (BWD, RELAY, 3, 0), (BWD, WORK, 1, 0), (BWD, SEND, 3, 1),
-    (BWD, TOK, 1, 0, 1), (BWD, TOK, 0, 1, 5), (BWD, WORK, 1, 1), (BWD, TOK, 1, 1, 1),
-    (BWD, SEND, 2, 0), (BWD, WORK, 3, 0), (BWD, TOK, 1, 0, 2), (BWD, TOK, 3, 0, 1),
-    (BWD, RELAY, 3, 1), (BWD, TOK, 1, 1, 2), (BWD, TOK, 0, 1, 6), (BWD, SEND, 2, 1),
-    (BWD, TOK, 1, 0, 3), (BWD, TOK, 3, 0, 2), (BWD, TOK, 0, 1, 7), (BWD, RELAY, 2, 0),
-    (BWD, TOK, 1, 1, 3), (BWD, WORK, 3, 1), (BWD, TOK, 1, 0, 4), (BWD, TOK, 3, 1, 1),
-    (BWD, TOK, 3, 0, 3), (BWD, TOK, 1, 1, 4), (BWD, RELAY, 2, 1), (BWD, TOK, 3, 1, 2),
-    (BWD, TOK, 1, 0, 5), (BWD, WORK, 2, 0), (BWD, TOK, 2, 0, 1), (BWD, TOK, 1, 1, 5),
-    (BWD, TOK, 3, 0, 4), (BWD, TOK, 3, 1, 3), (BWD, WORK, 2, 1), (BWD, TOK, 2, 1, 1),
-    (BWD, TOK, 2, 0, 2), (BWD, TOK, 1, 1, 6), (BWD, TOK, 1, 0, 6), (BWD, TOK, 3, 0, 5),
-    (BWD, TOK, 2, 1, 2), (BWD, TOK, 1, 0, 7), (BWD, TOK, 2, 0, 3), (BWD, TOK, 1, 1, 7),
-    (BWD, TOK, 3, 1, 4), (BWD, TOK, 3, 0, 6), (BWD, TOK, 2, 1, 3), (BWD, TOK, 3, 0, 7),
-    (BWD, TOK, 2, 0, 4), (BWD, TOK, 3, 1, 5), (BWD, TOK, 2, 1, 4), (BWD, TOK, 2, 0, 5),
-    (BWD, TOK, 3, 1, 6), (BWD, TOK, 2, 1, 5), (BWD, TOK, 3, 1, 7), (BWD, TOK, 2, 0, 6),
+    (FWD, SEND, 0, 0), (FWD, CROSS, 0), (FWD, SEND, 0, 1), (FWD, RELAY, 0, 0), (FWD, CROSS, 1),
+    (FWD, NEAR, 0), (FWD, RELAY, 0, 1), (FWD, WORK, 0, 0), (FWD, TOK, 0, 0, 1), (FWD, NORM, 0),
+    (FWD, SEND, 1, 0), (FWD, NEAR, 1), (FWD, FAR, 0), (FWD, TOK, 0, 0, 2), (FWD, WORK, 0, 1),
+    (FWD, TOK, 0, 1, 1), (FWD, SEND, 1, 1), (FWD, RELAY, 1, 0), (FWD, TOK, 0, 0, 3), (FWD, FAR, 1),
+    (FWD, SEND, 3, 0), (FWD, TOK, 0, 1, 2), (FWD, TOK, 0, 0, 4), (FWD, RELAY, 1, 1),
+    (FWD, WORK, 1, 0), (FWD, NORM, 1), (FWD, TOK, 0, 1, 3), (FWD, TOK, 1, 0, 1), (FWD, RELAY, 3, 0),
+    (FWD, TOK, 0, 0, 5), (FWD, WORK, 1, 1), (FWD, TOK, 0, 1, 4), (FWD, TOK, 1, 1, 1),
+    (FWD, TOK, 1, 0, 2), (FWD, TOK, 0, 0, 6), (FWD, SEND, 3, 1), (FWD, SEND, 2, 0), (FWD, WORK, 3, 0),
+    (FWD, NORM, 2), (FWD, TOK, 3, 0, 1), (FWD, TOK, 0, 1, 5), (FWD, TOK, 1, 1, 2),
+    (FWD, TOK, 1, 0, 3), (FWD, TOK, 0, 0, 7), (FWD, RELAY, 3, 1), (FWD, TOK, 0, 1, 6),
+    (FWD, TOK, 3, 0, 2), (FWD, SEND, 2, 1), (FWD, TOK, 1, 1, 3), (FWD, TOK, 0, 1, 7),
+    (FWD, RELAY, 2, 0), (FWD, WORK, 3, 1), (FWD, TOK, 3, 1, 1), (FWD, TOK, 1, 0, 4),
+    (FWD, TOK, 3, 0, 3), (FWD, RELAY, 2, 1), (FWD, TOK, 1, 1, 4), (FWD, TOK, 3, 1, 2),
+    (FWD, TOK, 1, 0, 5), (FWD, WORK, 2, 0), (FWD, TOK, 2, 0, 1), (FWD, TOK, 3, 0, 4),
+    (FWD, TOK, 1, 1, 5), (FWD, WORK, 2, 1), (MID, BEGIN, 0, 1), (FWD, TOK, 3, 1, 3),
+    (FWD, TOK, 2, 0, 2), (FWD, TOK, 1, 0, 6), (MID, BEGIN, 0, 0), (FWD, TOK, 3, 0, 5),
+    (FWD, TOK, 1, 1, 6), (MID, RELAY, 0, 1), (FWD, TOK, 2, 1, 1), (FWD, TOK, 1, 0, 7),
+    (MID, BEGIN, 1, 0), (FWD, TOK, 2, 0, 3), (FWD, TOK, 1, 1, 7), (MID, BEGIN, 1, 1),
+    (FWD, TOK, 3, 0, 6), (FWD, TOK, 2, 1, 2), (MID, RELAY, 0, 0), (MID, REDUCE, 0, 1),
+    (FWD, TOK, 3, 0, 7), (FWD, TOK, 2, 0, 4), (MID, RELAY, 1, 0), (MID, BEGIN, 3, 0),
+    (FWD, TOK, 2, 1, 3), (MID, RELAY, 1, 1), (FWD, TOK, 3, 1, 4), (FWD, TOK, 2, 0, 5),
+    (MID, REDUCE, 0, 0), (FWD, TOK, 2, 1, 4), (MID, REDUCE, 1, 0), (FWD, TOK, 3, 1, 5),
+    (FWD, TOK, 2, 0, 6), (MID, RELAY, 3, 0), (FWD, TOK, 2, 1, 5), (FWD, TOK, 2, 0, 7),
+    (MID, BEGIN, 2, 0), (MID, REDUCE, 1, 1), (FWD, TOK, 2, 1, 6), (FWD, TOK, 3, 1, 6),
+    (MID, REDUCE, 3, 0), (FWD, TOK, 2, 1, 7), (MID, BEGIN, 2, 1), (FWD, TOK, 3, 1, 7),
+    (MID, RELAY, 2, 0), (MID, BEGIN, 3, 1), (MID, RELAY, 2, 1), (MID, REDUCE, 2, 0),
+    (MID, RELAY, 3, 1), (MID, REDUCE, 2, 1), (MID, JOIN, 0), (MID, REDUCE, 3, 1), (MID, JOIN, 1),
+    (MID, FINISH, 0), (BWD, SEND, 0, 0), (BWD, CROSS, 0), (MID, FINISH, 1), (BWD, SEND, 0, 1),
+    (BWD, RELAY, 0, 0), (BWD, NEAR, 0), (BWD, SEND, 1, 0), (BWD, RELAY, 0, 1), (BWD, WORK, 0, 0),
+    (BWD, TOK, 0, 0, 1), (BWD, FAR, 0), (BWD, CROSS, 1), (BWD, TOK, 0, 0, 2), (BWD, RELAY, 1, 0),
+    (BWD, WORK, 0, 1), (BWD, TOK, 0, 1, 1), (BWD, TOK, 0, 0, 3), (BWD, NEAR, 1), (BWD, SEND, 1, 1),
+    (BWD, TOK, 0, 1, 2), (BWD, TOK, 0, 0, 4), (BWD, WORK, 1, 0), (BWD, TOK, 1, 0, 1), (BWD, FAR, 1),
+    (BWD, SEND, 3, 0), (BWD, TOK, 0, 1, 3), (BWD, RELAY, 1, 1), (BWD, TOK, 1, 0, 2),
+    (BWD, TOK, 0, 1, 4), (BWD, TOK, 0, 0, 5), (BWD, SEND, 3, 1), (BWD, RELAY, 3, 0),
+    (BWD, TOK, 1, 0, 3), (BWD, WORK, 1, 1), (BWD, TOK, 1, 1, 1), (BWD, TOK, 0, 1, 5),
+    (BWD, SEND, 2, 0), (BWD, TOK, 0, 0, 6), (BWD, RELAY, 3, 1), (BWD, TOK, 1, 0, 4),
+    (BWD, TOK, 1, 1, 2), (BWD, TOK, 0, 0, 7), (BWD, TOK, 0, 1, 6), (BWD, WORK, 3, 0),
+    (BWD, SEND, 2, 1), (BWD, TOK, 3, 0, 1), (BWD, TOK, 1, 0, 5), (BWD, RELAY, 2, 0),
+    (BWD, TOK, 0, 1, 7), (BWD, TOK, 1, 1, 3), (BWD, WORK, 3, 1), (BWD, TOK, 3, 0, 2),
+    (BWD, TOK, 1, 0, 6), (BWD, TOK, 1, 1, 4), (BWD, TOK, 3, 1, 1), (BWD, RELAY, 2, 1),
+    (BWD, TOK, 1, 0, 7), (BWD, WORK, 2, 0), (BWD, TOK, 3, 0, 3), (BWD, TOK, 2, 0, 1),
+    (BWD, TOK, 3, 1, 2), (BWD, TOK, 1, 1, 5), (BWD, WORK, 2, 1), (BWD, TOK, 2, 1, 1),
+    (BWD, TOK, 3, 0, 4), (BWD, TOK, 2, 0, 2), (BWD, TOK, 3, 1, 3), (BWD, TOK, 1, 1, 6),
+    (BWD, TOK, 2, 1, 2), (BWD, TOK, 3, 0, 5), (BWD, TOK, 2, 0, 3), (BWD, TOK, 1, 1, 7),
+    (BWD, TOK, 3, 1, 4), (BWD, TOK, 2, 1, 3), (BWD, TOK, 3, 0, 6), (BWD, TOK, 2, 0, 4),
+    (BWD, TOK, 3, 1, 5), (BWD, TOK, 3, 0, 7), (BWD, TOK, 2, 1, 4), (BWD, TOK, 2, 0, 5),
+    (BWD, TOK, 3, 1, 6), (BWD, TOK, 2, 1, 5), (BWD, TOK, 2, 0, 6), (BWD, TOK, 3, 1, 7),
     (BWD, TOK, 2, 1, 6), (BWD, TOK, 2, 0, 7), (BWD, TOK, 2, 1, 7),
 )
 
@@ -351,8 +351,8 @@
     x,
     enc_in,
     dec_in,
-    enc_bias,
-    dec_bias,
+    enc_rows,
+    dec_rows,
     mask,
     sq,
     xs,
@@ -360,6 +360,8 @@
     feat_out,
     grad_out,
     sq_sum,
+    enc_bias,
+    dec_bias,
     enc,
     dec,
     held,
@@ -399,6 +401,9 @@
     for copy in loads:
         copy.start()
     greet()
+    for rows, line in ((enc_rows, enc_bias), (dec_rows, dec_bias)):
+        for i in range(rows.shape[0]):
+            line[:, pl.ds(i * rows.shape[1], rows.shape[1])] = rows[pl.ds(i, 1)]
 
 
     def feature(k, e, me, total):
@@ -601,6 +606,8 @@
         in_specs=[VMEM, ANY, ANY] + [VMEM] * 4,
         out_specs=[ANY, ANY, ANY, ANY, VMEM],
         scratch_shapes=[
+            pltpu.VMEM((1, width), F32),
+            pltpu.VMEM((1, depth), F32),
             pltpu.VMEM(enc.shape, BF16),
             pltpu.VMEM(dec.shape, BF16),
             pltpu.VMEM(units + (depth,), BF16),
@@ -750,7 +757,7 @@
     )
     enc = enc_weight.reshape(slabs, models * depth, block)
     xs, es, feats, grads, sq_sum = step(
-        scale, x, enc, dec, enc_bias.reshape(1, width), dec_bias.reshape(1, models * depth), mask, sq
+        scale, x, enc, dec, enc_bias, dec_bias, mask, sq
     )
     inv_norm = (1.0 / jnp.sqrt(sq_sum + NORM_EPSILON))[:, :, None]
     flat = (2 * tiles, UNIT)

time: 236 us -> 232 us (0.983)
  local copies, waits for them, and re-layouts: 16.2 us -> 13.6 us
    unnamed x7 -> x5, local copies, waits for them, and re-layouts: 8.13 us -> 5.54 us
where the time goes in v6:
time: 232 us
  Pallas kernels  214 us (92%)
  local copies, waits for them, and re-layouts  13.6 us (6%)
  other arithmetic  3.69 us (2%)
    pallas_call x1, Pallas kernels, step(): pl.pallas_call(functools.partial(step_kernel, scale), out_shape=[rows, ro...  188 us
    pallas_call x1, Pallas kernels, weights(): pl.pallas_call(functools.partial(weights_kernel, scale), out_shape=[jax.S...  25.4 us
    unnamed x5, local copies, waits for them, and re-layouts  5.54 us

profile of v6, /device:TPU:1, one launch (start us, length us, event | category | flops | bytes accessed | tf_op | source)
XLA Modules:
  0.0 231.9 jit_solution(12906566610743388145)
XLA Ops:
  0.6 0.9 compare_reduce_fusion
  1.6 0.2 convert_reduce_fusion
  1.7 0.0 copy-start.1
  1.7 0.1 copy.14
  1.8 0.1 multiply_reduce_fusion.2
  2.0 0.2 select_reduce_fusion
  2.1 0.1 fusion.4
  2.2 0.1 copy.13
  2.3 0.6 reshape.330.units
  3.0 0.1 broadcast_in_dim.62
  3.0 0.7 broadcast_in_dim.63.mask
  3.8 2.2 reshape.331.x
  6.0 3.6 %copy.16 = bf16[128,8,2,1024]{3,1,2,0:T(8,128)(2,1)S(1)} copy(bf16[128,8,2,1024]{3,2,1,0:T(2,128)(2,1)} %bitcast.36) | data formatting | bytes 8388608
  9.6 0.0 copy-done.1
  9.6 0.0 copy-start
  9.6 1.9 copy-done
  11.5 0.9 multiply_reduce_fusion.1
  12.4 0.6 pad_maximum_fusion.sq
  13.0 188.5 %step.1 = (bf16[4,8,64,2048]{3,2,1,0:T(8,128)(2,1)}, bf16[4,8,64,2048]{3,2,1,0:T(8,128)(2,1)}, bf16[4,8,64,1024]{3,2,1,0:T(8,128)(2,1)}, bf16[4,8,64,1024]{3,2,1,0:T(8,128)(2,1)}, f32[2,1024]{1,0:T(2,128)}) custom-call(bf16[2,64,2048]{2,1,0:T(8,128)(2,1)} %reshape.331.x, bf16[4,2048,256]{2,1,0:T(8,128)(2,1)} %bitcast.37, bf16[1024,2048]{1,0:T(8,128)(2,1)} %bitcast.32, ...), custom_call_target="tpu_custom_call" | custom-call | tf_op jit(solution)/shard_map/step/pallas_call | solution.py:603
  201.5 0.7 rsqrt_bitcast_fusion
  202.2 1.4 copy.15.inv_norm
  203.7 25.4 %weights.1 = (bf16[4,2,1024,256]{3,2,1,0:T(8,128)(2,1)}, bf16[1024,2,1024]{2,1,0:T(2,128)(2,1)}, f32[8,1024]{1,0:T(8,128)}, f32[4,8,512]{2,1,0:T(8,128)}) custom-call(s32[64]{0:T(128)} %reshape.330.units, s32[4]{0:T(128)} %copy-done.1, bf16[32,64,2048]{2,1,0:T(8,128)(2,1)} %bitcast.34, bf16[32,64,2048]{2,1,0:T(8,128)(2,1)} %bitcast.35, ...), custom_call_target="tpu_custom_call" | custom-call | tf_op jit(solution)/shard_map/weights/pallas_call | solution.py:687
  229.1 0.8 slice_reduce_fusion.1
  229.8 0.6 reshape_squeeze.6
  230.4 0.9 slice_reduce_fusion
  231.3 0.6 reshape_squeeze.7
  (4 shorter events, 0.0 us)
Async XLA Ops:
  1.7 7.9 %copy-start.1 = (s32[4]{0:T(128)}, s32[4]{0:T(128)S(1)}, u32[]{:S(2)}) copy-start(s32[4]{0:T(128)S(1)} %get-tuple-element.24.count) | copy-start | bytes 52
  9.6 1.9 copy-start
